TPU v7x, 128 devices: a whole 4x4x4 slice. The times are simulated.
128 devices in a mesh: head: 4 (over x), ctx: 32 (over y, z, core).
Axes of the slice: x: 4, y: 4, z: 4, core: 2. Of those that a mesh axis runs over, the one named last changes fastest.
Arguments:
- qkv: bfloat16 [12288, 3, 1024], P(('ctx', 'head')), may hold values from -6 to 6
- grad_out: bfloat16 [12288, 1024], P(('ctx', 'head')), may hold values from -6 to 6
- rab: float32 [16, 20], replicated, may hold values from -3 to 3
- doc_ids: int32 [12288], replicated, may hold values from 0 to 7, never falling along the last dimension, each value on 1 to 6144 neighbouring positions
Outputs:
- attn_out: bfloat16 [12288, 1024], P(('ctx', 'head'))
- grad_qkv: bfloat16 [12288, 3, 1024], P(('ctx', 'head'))
- grad_rab: float32 [16, 20], P('head')
Inputs may be any that keep to these rules, and one draw needn't show every extreme that they name: `doc_ids`: 12288 events of 8 user histories laid end to end: history numbers never fall, every history has 1 to 6144 events, one has exactly 6144.
All inputs are finite; a program needn't handle non-finite values.
Results may differ from a plain program's by a relative error of at most 0.014.
Values may be sent and summed in bfloat16 or wider, within the bound.
No kernel may reach another device: no remote copies, remote signals or barrier semaphores. Data moves between devices by JAX's collectives and lax.ppermute only.
A program may use at most 128 MiB of HBM per device.

v0:
```python
import math

import jax
import jax.numpy as jnp
from jax import lax
from jax.sharding import PartitionSpec as P

HD = 64
NB = 20
DOCS = 8


def bucket_of(distance):
    clipped = jnp.maximum(distance, 0)
    bucket = jnp.minimum(clipped, 8)
    for power in range(3, 14):
        bucket = bucket + (clipped >= 2**power).astype(jnp.int32)
    return bucket


def inverse_roots(doc_ids):
    counted = jnp.sum(
        (doc_ids[None, :] == jnp.arange(DOCS, dtype=jnp.int32)[:, None]).astype(jnp.float32), axis=1
    )
    return lax.rsqrt(counted)


def pick_scale(docs, inverse):
    match = docs[:, None] == jnp.arange(DOCS, dtype=jnp.int32)[None, :]
    return jnp.sum(jnp.where(match, inverse[None, :], 0.0), axis=1)


def pair_scores(query_heads, key_heads, relative_bias_table, pos_q, pos_k, doc_q, doc_k):
    attention_scores = jnp.einsum(
        "qhd,khd->hqk", query_heads, key_heads, preferred_element_type=jnp.float32
    ) * HD ** (-0.5)
    buckets = bucket_of(pos_q[:, None] - pos_k[None, :])
    bucket_indicator = (
        buckets[None, :, :] == jnp.arange(NB, dtype=jnp.int32)[:, None, None]
    ).astype(jnp.float32)
    attention_scores = attention_scores + jnp.einsum(
        "jr,reg->jeg", relative_bias_table, bucket_indicator, precision=lax.Precision.HIGHEST
    )
    allowed = (doc_q[:, None] == doc_k[None, :]) & (pos_k[None, :] <= pos_q[:, None])
    return (attention_scores, allowed, bucket_indicator)


def over_blocks(step, carry, piece):
    rows = piece.shape[0]
    size = math.gcd(rows, 512)
    blocks = piece.reshape((rows // size, size) + piece.shape[1:])

    def advance(state, item):
        index, block = item
        return (step(state, block, index * size), None)

    carry, unused = lax.scan(advance, carry, (jnp.arange(rows // size, dtype=jnp.int32), blocks))
    return carry


def per_device(qkv, grad_out, rab, doc_ids):
    local = jnp.concatenate([qkv, grad_out[:, None, :]], axis=1)
    mixed = lax.all_to_all(local, "head", split_axis=2, concat_axis=0, tiled=True)
    count = mixed.shape[0]
    width = mixed.shape[2]
    heads = width // HD
    alpha = HD ** (-0.5)
    relative_bias_table = lax.dynamic_slice_in_dim(rab, lax.axis_index("head") * heads, heads, 0)
    base = lax.axis_index("ctx") * count
    pos_q = base + jnp.arange(count, dtype=jnp.int32)
    doc_q = lax.dynamic_slice_in_dim(doc_ids, base, count, 0)
    inverse = inverse_roots(doc_ids)
    scale_q = pick_scale(doc_q, inverse)
    query_heads = mixed[:, 0].reshape(count, heads, HD)
    grad_heads = mixed[:, 3].reshape(count, heads, HD)

    def key_position_side(state, keyvals, start):
        size = keyvals.shape[0]
        doc_k = lax.dynamic_slice_in_dim(doc_ids, start, size, 0)
        active = (start <= pos_q[count - 1]) & (doc_k[size - 1] >= doc_q[0])

        def key_compute(state):
            out_acc, dq_acc, bias_running_sum = state
            key_heads = keyvals[:, 0].reshape(size, heads, HD)
            value_heads = keyvals[:, 1].reshape(size, heads, HD)
            pos_k = start + jnp.arange(size, dtype=jnp.int32)
            attention_scores, allowed, bucket_indicator = pair_scores(
                query_heads, key_heads, relative_bias_table, pos_q, pos_k, doc_q, doc_k
            )
            signal = jax.nn.sigmoid(attention_scores)
            weights = (
                jnp.where(allowed, attention_scores * signal, 0.0) * scale_q[None, :, None]
            ).astype(jnp.bfloat16)
            out_acc = out_acc + jnp.einsum(
                "hqk,khd->qhd", weights, value_heads, preferred_element_type=jnp.float32
            )
            direct = jnp.einsum(
                "qhd,khd->hqk", grad_heads, value_heads, preferred_element_type=jnp.float32
            )
            slope = signal * (1.0 + attention_scores * (1.0 - signal))
            score_gradient = jnp.where(allowed, direct * slope, 0.0) * scale_q[None, :, None]
            dscore_low = score_gradient.astype(jnp.bfloat16)
            dq_acc = (
                dq_acc
                + jnp.einsum(
                    "hqk,khd->qhd", dscore_low, key_heads, preferred_element_type=jnp.float32
                )
                * alpha
            )
            bias_running_sum = bias_running_sum + jnp.einsum(
                "tic,wic->tw", score_gradient, bucket_indicator, precision=lax.Precision.HIGHEST
            )
            return (out_acc, dq_acc, bias_running_sum)

        return lax.cond(active, key_compute, lambda state: state, state)

    zeros_heads = jnp.zeros((count, heads, HD), jnp.float32)
    zeros_bias = jnp.zeros((heads, NB), jnp.float32)
    kv_whole = lax.all_gather(mixed[:, 1:3], "ctx", axis=0, tiled=True)
    out_acc, dq_acc, bias_running_sum = over_blocks(
        key_position_side, (zeros_heads, zeros_heads, zeros_bias), kv_whole
    )
    size = math.gcd(count * lax.axis_size("ctx"), 512)

    def one_block(index):
        first = index * size
        keyvals = lax.dynamic_slice_in_dim(kv_whole, first, size, 0)
        doc_k = lax.dynamic_slice_in_dim(doc_ids, first, size, 0)
        active = (first <= pos_q[count - 1]) & (doc_k[size - 1] >= doc_q[0])

        def one_compute(unused):
            key_heads = keyvals[:, 0].reshape(size, heads, HD)
            value_heads = keyvals[:, 1].reshape(size, heads, HD)
            pos_k = first + jnp.arange(size, dtype=jnp.int32)
            attention_scores, allowed, bucket_indicator = pair_scores(
                query_heads, key_heads, relative_bias_table, pos_q, pos_k, doc_q, doc_k
            )
            signal = jax.nn.sigmoid(attention_scores)
            weights = (
                jnp.where(allowed, attention_scores * signal, 0.0) * scale_q[None, :, None]
            ).astype(jnp.bfloat16)
            direct = jnp.einsum(
                "qhd,khd->hqk", grad_heads, value_heads, preferred_element_type=jnp.float32
            )
            slope = signal * (1.0 + attention_scores * (1.0 - signal))
            dscore_low = (jnp.where(allowed, direct * slope, 0.0) * scale_q[None, :, None]).astype(
                jnp.bfloat16
            )
            key_part = (
                jnp.einsum(
                    "hqk,qhd->khd", dscore_low, query_heads, preferred_element_type=jnp.float32
                )
                * alpha
            )
            value_part = jnp.einsum(
                "hqk,qhd->khd", weights, grad_heads, preferred_element_type=jnp.float32
            )
            return jnp.stack(
                [key_part.reshape(size, width), value_part.reshape(size, width)], axis=1
            )

        return lax.cond(
            active, one_compute, lambda unused: jnp.zeros((size, 2, width), jnp.float32), 0
        )

    parts = lax.map(one_block, jnp.arange(count * lax.axis_size("ctx") // size, dtype=jnp.int32))
    key_grads = lax.psum_scatter(
        parts.reshape(count * lax.axis_size("ctx"), 2, width).astype(jnp.bfloat16),
        "ctx",
        scatter_dimension=0,
        tiled=True,
    ).astype(jnp.float32)
    results = jnp.stack(
        [
            out_acc.reshape(count, width),
            dq_acc.reshape(count, width),
            key_grads[:, 0],
            key_grads[:, 1],
        ],
        axis=1,
    ).astype(jnp.bfloat16)
    rows_back = lax.all_to_all(results, "head", split_axis=0, concat_axis=2, tiled=True)
    bias_grad = lax.psum(bias_running_sum, "ctx")
    return (rows_back[:, 0], rows_back[:, 1:4], bias_grad)


def solution(mesh):
    return jax.shard_map(
        per_device,
        mesh=mesh,
        in_specs=(P(("ctx", "head"), None, None), P(("ctx", "head"), None), P(), P()),
        out_specs=(P(("ctx", "head"), None), P(("ctx", "head"), None, None), P("head", None)),
        check_vma=False,
    )
```

profile of v0, /device:TPU:1, one launch (start us, length us, event | category | flops | bytes accessed | tf_op | source)
XLA Modules:
  0.0 1173.5 jit_solution(6828095669300578927)
XLA Ops:
  7.2 1.2 pad_maximum_fusion
  9.2 18.8 %all_to_all.36 = bf16[96,4,1024]{0,1,2:T(4,128)(2,1)S(1)} all-to-all(bf16[96,4,1024]{0,1,2:T(4,128)(2,1)S(1)} %copy.128), channel_id=1, replica_groups=mesh['head'=4,'ctx'=32] {'head'}, dimensions={2} | all-to-all | bytes 1572864 | tf_op jit(solution)/shard_map/all_to_all | solution.py:63
  33.7 61.1 %all-gather.2.cloned.1.call-done = bf16[12288,2,256]{2,0,1:T(8,128)(2,1)} async-done(((bf16[384,2,256]{2,0,1:T(8,128)(2,1)}), bf16[12288,2,256]{2,0,1:T(8,128)(2,1)}) %all-gather.2.cloned.1.call-update) | async-done | bytes 12582928 | tf_op jit(solution)/shard_map/all_gather | solution.py:119
  94.8 16.7 %copy.134 = bf16[12288,2,256]{0,2,1:T(8,128)(2,1)} copy(bf16[12288,2,256]{2,0,1:T(8,128)(2,1)} %all-gather.2.cloned.1.call-done) | data formatting | bytes 25165824 | tf_op jit(solution)/shard_map/while | solution.py:166
  112.1 228.4 %while.25 = (s32[]{:T(128)}, bf16[24,512,2,256]{3,1,0,2:T(8,128)(2,1)}, s32[24]{0:T(128)}, s32[384]{0:T(512)S(1)}, s32[12288]{0:T(1024)}, /*index=5*/s32[384]{0:...) while((s32[]{:T(128)}, ...), condition=%wide.region_9.10_spmd, body=%wide.region_6.9_spmd.sunk | while | flops 619250176 | bytes 45443840 | solution.py:166
  112.1 1.3 dynamic_slice.42
  118.4 25.2 %conditional.5 = (bf16[1,512,2,256]{1,3,2,0:T(8,128)(2,1)S(1)}) conditional(s32[]{:T(128)} %convert_element_type.261, () %tuple.76, (s32[384]{0:T(512)S(1)}, s32[512]{0:T(512)S(1)}, s32[]{:T(128)}, s32[384]{0:T(512)S(1)}, bf16[12288,2,256]{0,2,1:T(8,128)(2,1)}, /*index=5*/s32[]{:T(128)}, bf16[384,4,64]{0,2,1:T(8,128)(2,1)}, ...), branch_computations={%region_7.7_spmd, %region_8.8_spmd} | conditional | flops 619250176 | bytes 43341748 | solution.py:162
  118.4 1.0 fusion.81
  119.7 9.0 fusion.52
  128.8 3.2 copy.125
  132.0 2.0 constant_dynamic-slice_fusion
  134.0 2.2 bitcast_add_fusion.1
  136.5 4.9 fusion.59
  141.4 2.1 fusion.57
  144.6 1.3 dynamic_slice.42
  150.9 25.2 %conditional.5 = (bf16[1,512,2,256]{1,3,2,0:T(8,128)(2,1)S(1)}) conditional(s32[]{:T(128)} %convert_element_type.261, () %tuple.76, (s32[384]{0:T(512)S(1)}, s32[512]{0:T(512)S(1)}, s32[]{:T(128)}, s32[384]{0:T(512)S(1)}, bf16[12288,2,256]{0,2,1:T(8,128)(2,1)}, /*index=5*/s32[]{:T(128)}, bf16[384,4,64]{0,2,1:T(8,128)(2,1)}, ...), branch_computations={%region_7.7_spmd, %region_8.8_spmd} | conditional | flops 619250176 | bytes 43341748 | solution.py:162
  151.0 1.0 fusion.81
  152.3 9.0 fusion.52
  161.3 3.2 copy.125
  164.5 2.0 constant_dynamic-slice_fusion
  166.6 2.2 bitcast_add_fusion.1
  169.1 4.9 fusion.59
  173.9 2.1 fusion.57
  177.2 1.3 dynamic_slice.42
  184.6 1.3 dynamic_slice.42
  192.1 1.3 dynamic_slice.42
  199.5 1.3 dynamic_slice.42
  206.9 1.3 dynamic_slice.42
  214.4 1.3 dynamic_slice.42
  221.8 1.3 dynamic_slice.42
  229.2 1.3 dynamic_slice.42
  236.6 1.3 dynamic_slice.42
  244.0 1.3 dynamic_slice.42
  251.4 1.3 dynamic_slice.42
  258.8 1.3 dynamic_slice.42
  266.3 1.3 dynamic_slice.42
  273.7 1.3 dynamic_slice.42
  281.1 1.3 dynamic_slice.42
  288.5 1.3 dynamic_slice.42
  296.0 1.3 dynamic_slice.42
  303.4 1.3 dynamic_slice.42
  310.8 1.3 dynamic_slice.42
  318.2 1.3 dynamic_slice.42
  325.7 1.3 dynamic_slice.42
  333.1 1.3 dynamic_slice.42
  340.6 16.7 %copy.133 = bf16[24,512,2,256]{1,3,2,0:T(8,128)(2,1)} copy(bf16[24,512,2,256]{3,1,0,2:T(8,128)(2,1)} %bitcast.109) | data formatting | bytes 25165824 | tf_op jit(solution)/shard_map/while | solution.py:57
  357.4 190.8 %while.24 = (s32[]{:T(128)}, f32[384,4,64]{0,2,1:T(8,128)S(1)}, f32[384,4,64]{0,2,1:T(8,128)S(1)}, f32[4,20]{1,0:T(4,128)S(1)}, s32[24]{0:T(128)S(1)}, /*index=5...) while((s32[]{:T(128)}, f32[384,4,64]{0,2,1:T(8,128)S(1)}, ...), condition=%wide.region_5.6_spmd, body=%wide.region_2.5_spmd.sunk | while | flops 811696704 | bytes 33248116 | solution.py:57
  363.3 26.3 %conditional.4 = ((f32[384,4,64]{0,2,1:T(8,128)S(1)}, f32[384,4,64]{0,2,1:T(8,128)S(1)}, f32[4,20]{1,0:T(4,128)S(1)})) conditional(s32[]{:T(128)} %convert_element_type.260, (f32[384,4,64]{0,2,1:T(8,128)S(1)}, f32[384,4,64]{0,2,1:T(8,128)S(1)}, f32[4,20]{1,0:T(4,128)S(1)}) %tuple.73, (s32[384]{0:T(512)S(1)}, s32[512]{0:T(512)S(1)}, s32[]{:T(128)}, ...), branch_computations={%region_3.3_spmd, %region_4.4_spmd} | conditional | flops 811696704 | bytes 33243624 | solution.py:115
  364.4 7.9 fusion.1
  372.2 1.1 dynamic-slice_bitcast_fusion
  374.2 1.6 fusion.5
  375.9 12.1 %fusion.35 = f32[4,20]{1,0:T(4,128)S(1)} fusion(f32[4,20]{1,0:T(4,128)S(1)} %get-tuple-element.215, s32[384,512]{0,1:T(8,128)S(1)} %fusion.48, f32[4,384,512]{1,2,0:T(8,128)S(1)} %fusion.5), kind=kOutput, calls=%fused_computation.34 | convolution fusion | flops 192675920 | bytes 3932800 | tf_op jit(solution)/shard_map/while/body/eval_jaxpr/cond/branch_1_fun/tic,wic->tw/dot_general | solution.py:110
  388.4 1.2 fusion.20
  395.4 26.3 %conditional.4 = ((f32[384,4,64]{0,2,1:T(8,128)S(1)}, f32[384,4,64]{0,2,1:T(8,128)S(1)}, f32[4,20]{1,0:T(4,128)S(1)})) conditional(s32[]{:T(128)} %convert_element_type.260, (f32[384,4,64]{0,2,1:T(8,128)S(1)}, f32[384,4,64]{0,2,1:T(8,128)S(1)}, f32[4,20]{1,0:T(4,128)S(1)}) %tuple.73, (s32[384]{0:T(512)S(1)}, s32[512]{0:T(512)S(1)}, s32[]{:T(128)}, ...), branch_computations={%region_3.3_spmd, %region_4.4_spmd} | conditional | flops 811696704 | bytes 33243624 | solution.py:115
  396.4 7.9 fusion.1
  404.3 1.1 dynamic-slice_bitcast_fusion
  406.3 1.6 fusion.5
  407.9 12.1 %fusion.35 = f32[4,20]{1,0:T(4,128)S(1)} fusion(f32[4,20]{1,0:T(4,128)S(1)} %get-tuple-element.215, s32[384,512]{0,1:T(8,128)S(1)} %fusion.48, f32[4,384,512]{1,2,0:T(8,128)S(1)} %fusion.5), kind=kOutput, calls=%fused_computation.34 | convolution fusion | flops 192675920 | bytes 3932800 | tf_op jit(solution)/shard_map/while/body/eval_jaxpr/cond/branch_1_fun/tic,wic->tw/dot_general | solution.py:110
  420.4 1.2 fusion.20
  548.6 170.4 %reduce-scatter.2.cloned.1.call-done = bf16[384,2,256]{2,0,1:T(8,128)(2,1)} async-done(((bf16[12288,2,256]{2,0,1:T(8,128)(2,1)}), bf16[384,2,256]{2,0,1:T(8,128)(2,1)}) %reduce-scatter.2.cloned.1.call-update) | async-done | bytes 393232 | tf_op jit(solution)/shard_map/reduce_scatter | solution.py:167
  719.0 1.1 pad_maximum_fusion.1
  720.1 1.5 copy.138
  721.6 4.0 all-to-all-start.1
  725.6 439.3 %psum.7 = f32[4,20]{1,0:T(4,128)} all-reduce(f32[4,20]{1,0:T(4,128)S(1)} %get-tuple-element.265), channel_id=1, replica_groups=mesh['head'=4,'ctx'=32] {'ctx'}, use_global_device_ids=true, to_apply=%region_11.12 | all-reduce | flops 80 | bytes 640 | tf_op jit(solution)/shard_map/psum | solution.py:183
  (401 shorter events, 177.4 us)
Async XLA Ops:
  7.2 24.2 %copy-start = (f32[16,20]{1,0:T(8,128)S(1)}, f32[16,20]{1,0:T(8,128)}, u32[]{:S(2)}) copy-start(f32[16,20]{1,0:T(8,128)} %param.14) | copy-start | bytes 3844
  7.2 87.6 %all-gather.2.cloned.1.call-start = ((), (), s32[]{:S(2)}) async-start(), calls=%async_computation.3 | async-start | bytes 12976128 | tf_op jit(solution)/shard_map/all_gather | solution.py:119
  29.5 689.5 %reduce-scatter.2.cloned.1.call-start = ((), (), s32[]{:S(2)}) async-start(), calls=%async_computation.4 | async-start | bytes 12976128 | tf_op jit(solution)/shard_map/reduce_scatter | solution.py:167
  136.5 4.9 copy-start.2
  136.5 4.9 copy-start.5
  141.4 2.2 copy-start.3
  169.0 4.9 copy-start.2
  169.0 4.9 copy-start.5
  173.9 2.2 copy-start.3
  340.6 16.8 %copy-start.4 = (bf16[384,4,64]{0,2,1:T(8,128)(2,1)S(1)}, bf16[384,4,64]{0,2,1:T(8,128)(2,1)}, u32[]{:S(2)}) copy-start(bf16[384,4,64]{0,2,1:T(8,128)(2,1)} %get-tuple-element.747) | copy-start | bytes 589828
  340.6 16.8 %copy-start.6 = (f32[384]{0:T(512)S(1)}, f32[384]{0:T(512)}, u32[]{:S(2)}) copy-start(f32[384]{0:T(512)} %get-tuple-element.749) | copy-start | bytes 4612
  720.1 446.5 %copy-start.1 = (f32[16,20]{1,0:T(8,128)S(1)}, f32[16,20]{1,0:T(8,128)}, u32[]{:S(2)}) copy-start(f32[16,20]{1,0:T(8,128)} %param.14) | copy-start | bytes 3844
  721.6 443.2 %all-to-all-start.1 = ((bf16[384,4,256]{2,1,0:T(4,128)(2,1)}), bf16[384,4,256]{2,1,0:T(4,128)(2,1)S(1)}, u32[]{:S(2)}, u32[]{:S(2)}) async-start(bf16[384,4,256]{2,1,0:T(4,128)(2,1)} %copy.138), calls=%async_computation.2 | async-start | bytes 1572864 | tf_op jit(solution)/shard_map/all_to_all | solution.py:182
Sparse Core Ops, SparseCore 0:
  29.6 65.0 all-gather.1
  340.7 378.2 reduce-scatter.1
where the time goes:
time: 1190 us; the launch traced here: 1170 us
  blocking collectives  458 us (38%)
  local copies, waits for them, and re-layouts  247 us (21%)
  waiting for transfers between devices  232 us (19%)
  loops' own time  125 us (11%)
  matrix products  84.2 us (7%)
  between operations  14.2 us (1%)
    psum x1, blocking collectives, per_device(): bias_grad = lax.psum(bias_running_sum, 'ctx')  439 us
    reduce_scatter x1, waiting for transfers between devices, per_device(): lax.psum_scatter(parts.reshape(count * lax.axis_size('ctx'), 2, width).as...  170 us
    another operation x1, loops' own time, over_blocks(): lax.scan(advance, carry, (jnp.arange(rows // size, dtype=jnp.int32), bloc...  62.2 us
    another operation x1, loops' own time, per_device(): lax.map(one_block, jnp.arange(count * lax.axis_size('ctx') // size, dtype...  62.1 us
    all_gather x1, waiting for transfers between devices, per_device(): kv_whole = lax.all_gather(mixed[:, 1:3], 'ctx', axis=0, tiled=True)  61.1 us
    dynamic_slice x48, local copies, waits for them, and re-layouts, over_blocks(): lax.scan(advance, carry, (jnp.arange(rows // size, dtype=jnp.int32), bloc...  44.4 us
    slice x72, local copies, waits for them, and re-layouts, key_position_side(): active = (start <= pos_q[count - 1]) & (doc_k[size - 1] >= doc_q[0])  43.3 us
    slice x72, local copies, waits for them, and re-layouts, one_block(): active = (first <= pos_q[count - 1]) & (doc_k[size - 1] >= doc_q[0])  40.9 us
  transfers between devices with their start and end apart: 3, of which 2 were waited for; matrix products, arithmetic and copies ran while one was open for 13% of the time, Pallas kernels for 0%

commit v1 on v0

v1 whole, which is shorter than its diff:
```python
import jax
import jax.numpy as jnp
from jax import lax
from jax.experimental import pallas as pl
from jax.experimental.pallas import tpu as pltpu
from jax.sharding import Mesh
from jax.sharding import PartitionSpec as P

HD = 64
H = 16
NB = 20
DOCS = 8
ROWS = 96
SUPER = 384
GROUPS = 16
CLASSES = 19
LOW = -1e30
VMEM = pltpu.VMEM
SMEM = pltpu.SMEM
NT = (((1,), (1,)), ((), ()))


def doc_bounds(ids):
    return [jnp.int32(0)] + [
        jnp.sum((ids < d).astype(jnp.float32)).astype(jnp.int32) for d in range(1, DOCS)
    ]


def pack_kernel(where_ref, ids_ref, qkv_ref, g_ref, kv_ref, qg_ref, bounds_ref):
    bounds = doc_bounds(ids_ref[...])
    for d in range(DOCS):
        bounds_ref[d] = bounds[d]
    pos = where_ref[0] + lax.broadcasted_iota(jnp.int32, (ROWS, 128), 0)
    length = jnp.zeros((ROWS, 128), jnp.int32)
    ends = bounds[1:] + [jnp.int32(SUPER * 2 * GROUPS)]
    for d in range(DOCS):
        length = jnp.where(pos >= bounds[d], ends[d] - bounds[d], length)
    scale = lax.rsqrt(length.astype(jnp.float32))[:, :HD]
    for h in range(H):
        cols = slice(h * HD, (h + 1) * HD)
        kv_ref[h] = jnp.concatenate([qkv_ref[:, 1, cols], qkv_ref[:, 2, cols]], axis=1)
        q = (qkv_ref[:, 0, cols].astype(jnp.float32) * 0.0625).astype(jnp.bfloat16)
        g = (g_ref[:, cols].astype(jnp.float32) * scale).astype(jnp.bfloat16)
        qg_ref[h] = jnp.concatenate([q, g], axis=1)


def bucket_scalar(d):
    b = jnp.minimum(d, 8)
    for p in range(3, 14):
        b = b + (d >= 2**p).astype(jnp.int32)
    return b


def next_power(d):
    b = jnp.int32(8)
    for p in range(3, 14):
        b = jnp.where(d >= 2**p, jnp.int32(2 ** (p + 1)), b)
    return b


def main_kernel(
    where_ref, bounds_ref, rab_ref,
    kv0, kv1, kv2, kv3, own_ref, other_ref,
    d0, d1, d2, d3, mine_ref, theirs_ref, bias_ref,
    kvs, qs, table, biasacc, dkv, start_ref, scale_ref, acc, lhs, qgt, buckets,
):
    x = where_ref[0]
    core = where_ref[1]
    for r, ref in enumerate((kv0, kv1, kv2, kv3)):
        at = pl.multiple_of(lax.rem(x + r, 4) * ROWS, ROWS)

        @pl.loop(0, GROUPS)
        def _(n):
            kvs[n, pl.ds(at, ROWS), :] = ref[n]

    mine_at = pl.multiple_of(core * ROWS, ROWS)
    theirs_at = pl.multiple_of((1 - core) * ROWS, ROWS)

    @pl.loop(0, GROUPS)
    def _(n):
        qs[n, pl.ds(mine_at, ROWS), :] = own_ref[n]
        qs[n, pl.ds(theirs_at, ROWS), :] = other_ref[n]
        dkv[n] = jnp.zeros((128, SUPER), jnp.float32)

    rel = lax.broadcasted_iota(jnp.int32, (ROWS, SUPER), 0) - lax.broadcasted_iota(
        jnp.int32, (ROWS, SUPER), 1
    )

    table[pl.ds(0, ROWS), :] = jnp.full((ROWS, SUPER), LOW, jnp.float32)
    for c in range(2):
        d = rel + (SUPER * c + ROWS * x)
        value = jnp.full((ROWS, SUPER), LOW, jnp.float32)
        for k in range(8):
            value = jnp.where(d >= k, rab_ref[k] * 0.5, value)
        for p in range(3, 10):
            value = jnp.where(d >= 2**p, rab_ref[p + 6] * 0.5, value)
        table[pl.ds((c + 1) * ROWS, ROWS), :] = value

    @pl.loop(2, CLASSES - 1)
    def _(c):
        base = SUPER * c + ROWS * x
        lowest = base - (SUPER - 1)
        b = bucket_scalar(lowest)
        d = rel + base
        value = jnp.where(
            d >= next_power(lowest), rab_ref[jnp.minimum(b + 1, NB - 1)] * 0.5, rab_ref[b] * 0.5
        )
        table[pl.ds(pl.multiple_of((c + 1) * ROWS, ROWS), ROWS), :] = value

    @pl.loop(0, CLASSES)
    def _(c):
        biasacc[pl.ds(pl.multiple_of(c * ROWS, ROWS), ROWS), :] = jnp.zeros(
            (ROWS, SUPER), jnp.float32
        )

    lane = lax.broadcasted_iota(jnp.int32, (2 * ROWS, 128), 1)
    left = lane < HD

    def start_of(pos):
        start = jnp.int32(0)
        for d in range(1, DOCS):
            start = jnp.where(pos >= bounds_ref[d], bounds_ref[d], start)
        return start

    @pl.loop(0, GROUPS)
    def _(g):
        row = lax.broadcasted_iota(jnp.int32, (2 * ROWS, 128), 0)
        pos = 2 * SUPER * g + ROWS * x + row + jnp.where(row >= ROWS, SUPER - ROWS, 0)
        start = jnp.zeros((2 * ROWS, 128), jnp.int32)
        length = jnp.zeros((2 * ROWS, 128), jnp.int32)
        for d in range(DOCS):
            first = bounds_ref[d]
            end = bounds_ref[d + 1] if d + 1 < DOCS else jnp.int32(2 * SUPER * GROUPS)
            inside = pos >= first
            start = jnp.where(inside, first, start)
            length = jnp.where(inside, end - first, length)
        start_ref[...] = start
        scale_ref[...] = lax.rsqrt(length.astype(jnp.float32))
        qg = qs[g]
        zero = jnp.zeros_like(qg)
        lhs[pl.ds(0, 2 * ROWS), :] = jnp.where(left, qg, zero)
        lhs[pl.ds(2 * ROWS, 2 * ROWS), :] = jnp.where(left, zero, qg)
        qgt[...] = qg.T
        acc[...] = jnp.zeros((2 * ROWS, 128), jnp.float32)
        first_pos = 2 * SUPER * g + ROWS * x
        start_first = start_of(first_pos)
        start_last = start_of(first_pos + SUPER + ROWS - 1)
        low = lax.div(lax.div(start_first, SUPER) - core + 1, 2)

        def tile(n, masked):
            mk = 2 * n + core
            at = pl.multiple_of((2 * g - mk + 1) * ROWS, ROWS)
            keyvals = kvs[n]
            both = lax.dot_general(lhs[...], keyvals, NT, preferred_element_type=jnp.float32)
            half = both[: 2 * ROWS] + table[pl.ds(at, 2 * ROWS), :]
            if masked:
                key = SUPER * mk + lax.broadcasted_iota(jnp.int32, (2 * ROWS, SUPER), 1)
                starts = jnp.concatenate([start_ref[...]] * 3, axis=1)
                half = jnp.where(key >= starts, half, LOW)
            t = jnp.tanh(half)
            u = 1.0 + t
            w = half * u
            ds = both[2 * ROWS :] * (u + w * (1.0 - t))
            biasacc[pl.ds(at, 2 * ROWS), :] += ds
            wb = w.astype(jnp.bfloat16)
            db = ds.astype(jnp.bfloat16)
            od = jnp.dot(
                jnp.concatenate([wb, db], axis=0), keyvals, preferred_element_type=jnp.float32
            )
            acc[...] += jnp.where(left, od[2 * ROWS :], od[: 2 * ROWS])
            dkv[n, pl.ds(0, HD), :] += jnp.dot(
                qgt[pl.ds(0, HD), :], db, preferred_element_type=jnp.float32
            )
            dkv[n, pl.ds(HD, HD), :] += jnp.dot(
                qgt[pl.ds(HD, HD), :], wb, preferred_element_type=jnp.float32
            )

        @pl.loop(low, g + 1)
        def _(n):
            clear = SUPER * (2 * n + core) >= start_last

            @pl.when(clear)
            def _():
                tile(n, False)

            @pl.when(jnp.logical_not(clear))
            def _():
                tile(n, True)

        result = acc[...] * jnp.where(left, 0.0625, scale_ref[...])
        acc[...] = result
        mine_ref[g] = acc[pl.ds(mine_at, ROWS), :]
        theirs_ref[g] = acc[pl.ds(theirs_at, ROWS), :].astype(jnp.bfloat16)

    @pl.loop(0, GROUPS)
    def _(n):
        kvs[n] = dkv[n].astype(jnp.bfloat16).T

    for r, ref in enumerate((d0, d1, d2, d3)):
        at = pl.multiple_of(lax.rem(x + r, 4) * ROWS, ROWS)

        @pl.loop(0, GROUPS)
        def _(n):
            ref[n] = kvs[n, pl.ds(at, ROWS), :]

    buckets[...] = jnp.zeros((NB, 8, 128), jnp.float32)

    def fold(v):
        v = v[:, :128] + v[:, 128:256] + v[:, 256:]
        out = v[:8]
        for i in range(1, ROWS // 8):
            out = out + v[8 * i : 8 * i + 8]
        return out

    for c in range(2):
        d = rel + (SUPER * c + ROWS * x)
        v = biasacc[pl.ds((c + 1) * ROWS, ROWS), :]
        edges = [(k, k, k + 1) for k in range(8)] + [(p + 6, 2**p, 2 ** (p + 1)) for p in range(3, 10)]
        for b, first, end in edges:
            buckets[b] += fold(jnp.where((d >= first) & (d < end), v, 0.0))

    @pl.loop(2, CLASSES - 1)
    def _(c):
        base = SUPER * c + ROWS * x
        lowest = base - (SUPER - 1)
        b = bucket_scalar(lowest)
        d = rel + base
        v = biasacc[pl.ds(pl.multiple_of((c + 1) * ROWS, ROWS), ROWS), :]
        upper = d >= next_power(lowest)
        buckets[b] += fold(jnp.where(upper, 0.0, v))
        buckets[jnp.minimum(b + 1, NB - 1)] += fold(jnp.where(upper, v, 0.0))

    for b in range(NB):
        bias_ref[pl.ds(b, 1), :] = jnp.sum(buckets[b], axis=0, keepdims=True) * 0.5


def unpack_kernel(qo_ref, dkv_ref, out_ref, grad_ref):
    for h in range(0, H, 2):
        cols = slice(h * HD, (h + 2) * HD)
        a, b = qo_ref[h], qo_ref[h + 1]
        grad_ref[:, 0, cols] = jnp.concatenate([a[:, :HD], b[:, :HD]], axis=1)
        out_ref[:, cols] = jnp.concatenate([a[:, HD:], b[:, HD:]], axis=1)
        a, b = dkv_ref[h, :ROWS], dkv_ref[h + 1, :ROWS]
        grad_ref[:, 1, cols] = jnp.concatenate([a[:, :HD], b[:, :HD]], axis=1)
        grad_ref[:, 2, cols] = jnp.concatenate([a[:, HD:], b[:, HD:]], axis=1)


def shift(v, axis, n, by):
    return lax.ppermute(v, axis, [(i, (i + by) % n) for i in range(n)])


def per_device(qkv, grad_out, rab, doc_ids):
    bf16, f32 = jnp.bfloat16, jnp.float32
    x, y, z, core = (lax.axis_index(a) for a in ("x", "y", "z", "core"))
    whole = pl.BlockSpec(memory_space=VMEM)
    scalars = pl.BlockSpec(memory_space=SMEM)
    block = jax.ShapeDtypeStruct((H, ROWS, 128), bf16)
    params = pltpu.CompilerParams(vmem_limit_bytes=48 * 2**20)
    first_row = (((y * 4 + z) * 2 + core) * 4 + x) * ROWS
    kv, qg, bounds = pl.pallas_call(
        pack_kernel,
        out_shape=(block, block, jax.ShapeDtypeStruct((DOCS,), jnp.int32)),
        in_specs=[scalars, whole, whole, whole],
        out_specs=(whole, whole, scalars),
        compiler_params=params,
        name="pack",
    )(first_row.reshape(1), doc_ids.reshape(96, 128), qkv, grad_out)
    kv = lax.all_to_all(kv, ("y", "z"), 0, 0, tiled=True)
    kvs = [kv] + [shift(kv, "x", 4, -r) for r in (1, 2, 3)]
    qg = lax.all_to_all(qg, ("y", "z"), 0, 0, tiled=True)
    qg_other = shift(qg, "core", 2, 1)
    table_row = lax.dynamic_slice_in_dim(rab, y * 4 + z, 1, 0)[0]
    d0, d1, d2, d3, mine, theirs, bias = pl.pallas_call(
        main_kernel,
        out_shape=(
            [block] * 4
            + [
                jax.ShapeDtypeStruct((H, ROWS, 128), f32),
                block,
                jax.ShapeDtypeStruct((NB, 128), f32),
            ]
        ),
        in_specs=[scalars] * 3 + [whole] * 6,
        out_specs=[whole] * 7,
        scratch_shapes=[
            VMEM((GROUPS, SUPER, 128), bf16),
            VMEM((GROUPS, 2 * ROWS, 128), bf16),
            VMEM((CLASSES * ROWS, SUPER), f32),
            VMEM((CLASSES * ROWS, SUPER), f32),
            VMEM((GROUPS, 128, SUPER), f32),
            VMEM((2 * ROWS, 128), jnp.int32),
            VMEM((2 * ROWS, 128), f32),
            VMEM((2 * ROWS, 128), f32),
            VMEM((4 * ROWS, 128), bf16),
            VMEM((128, 2 * ROWS), bf16),
            VMEM((NB, 8, 128), f32),
        ],
        compiler_params=params,
        name="attend",
    )(jnp.stack([x, core]), bounds, table_row, *kvs, qg, qg_other)
    parts = [shift(d, "x", 4, r) for r, d in ((1, d1), (2, d2), (3, d3))]
    theirs = shift(theirs, "core", 2, 1)
    bias = jnp.sum(bias, axis=1)
    bias = bias + shift(bias, "core", 2, 1)
    bias = bias + shift(bias, "x", 4, 1)
    bias = bias + shift(bias, "x", 4, 2)
    hi = lax.reduce_precision(bias, 8, 7)
    mid = lax.reduce_precision(bias - hi, 8, 7)
    lo = bias - hi - mid
    carried = jnp.pad(jnp.stack([hi, mid, lo]).astype(bf16), ((0, 13), (0, 128 - NB)))
    qo = (mine + theirs.astype(f32)).astype(bf16)
    dkv = d0.astype(f32) + parts[0].astype(f32) + parts[1].astype(f32) + parts[2].astype(f32)
    dkv = jnp.concatenate(
        [dkv.astype(bf16), jnp.broadcast_to(carried[None], (H, 16, 128))], axis=1
    )
    qo = lax.all_to_all(qo, ("y", "z"), 0, 0, tiled=True)
    dkv = lax.all_to_all(dkv, ("y", "z"), 0, 0, tiled=True)
    terms = lax.dynamic_slice(dkv, (x * 4, ROWS, 0), (4, 3, NB)).astype(f32)
    bias_grad = terms[:, 0] + terms[:, 1] + terms[:, 2]
    out, grad_qkv = pl.pallas_call(
        unpack_kernel,
        out_shape=(
            jax.ShapeDtypeStruct((ROWS, H * HD), bf16),
            jax.ShapeDtypeStruct((ROWS, 3, H * HD), bf16),
        ),
        in_specs=[whole, whole],
        out_specs=(whole, whole),
        compiler_params=params,
        name="unpack",
    )(qo, dkv)
    return out, grad_qkv, bias_grad


def solution(mesh):
    fine = Mesh(mesh.devices.reshape(4, 4, 4, 2), ("x", "y", "z", "core"))
    rows = ("y", "z", "core", "x")
    return jax.shard_map(
        per_device,
        mesh=fine,
        in_specs=(P(rows, None, None), P(rows, None), P(), P()),
        out_specs=(P(rows, None), P(rows, None, None), P("x", None)),
        check_vma=False,
    )
```

time: 1190 us -> 147 us (0.12)
  the two profiles are of different devices: /device:TPU:1 before, /device:TPU:2 now
where the time goes in v1:
time: 147 us; the launch traced here: 146 us
  waiting for transfers between devices  55.5 us (38%)
  Pallas kernels  40.8 us (28%)
  starting transfers between devices  24.1 us (16%)
  blocking collectives  17.7 us (12%)
  local copies, waits for them, and re-layouts  4.06 us (3%)
  other arithmetic  3.36 us (2%)
    pallas_call x1, Pallas kernels, per_device(): pl.pallas_call(main_kernel, out_shape=[block] * 4 + [jax.ShapeDtypeStruct...  34.8 us
    ppermute x11, waiting for transfers between devices, shift(): return lax.ppermute(v, axis, [(i, (i + by) % n) for i in range(n)])  29 us
    all_to_all x1, blocking collectives, per_device(): qg = lax.all_to_all(qg, ('y', 'z'), 0, 0, tiled=True)  17.7 us
    ppermute x11, starting transfers between devices, shift(): return lax.ppermute(v, axis, [(i, (i + by) % n) for i in range(n)])  12.8 us
    all_to_all x1, waiting for transfers between devices, per_device(): kv = lax.all_to_all(kv, ('y', 'z'), 0, 0, tiled=True)  9.04 us
    all_to_all x1, waiting for transfers between devices, per_device(): dkv = lax.all_to_all(dkv, ('y', 'z'), 0, 0, tiled=True)  8.91 us
    all_to_all x1, waiting for transfers between devices, per_device(): qo = lax.all_to_all(qo, ('y', 'z'), 0, 0, tiled=True)  8.47 us
    unnamed x12, local copies, waits for them, and re-layouts  4.04 us
  transfers between devices with their start and end apart: 14, of which 9 were waited for; matrix products, arithmetic and copies ran while one was open for 2% of the time, Pallas kernels for 0%

profile of v1, /device:TPU:2, one launch (start us, length us, event | category | flops | bytes accessed | tf_op | source)
XLA Modules:
  0.0 146.2 jit_solution(10330541338423989913)
XLA Ops:
  0.6 0.0 copy-start
  0.7 0.0 copy-start.1
  0.7 0.0 copy-start.2
  0.7 1.6 %copy.7.qkv_ref = bf16[96,3,1024]{2,1,0:T(4,128)(2,1)S(1)} copy(bf16[96,3,1024]{2,0,1:T(8,128)(2,1)} %param.4) | data formatting | bytes 1179648 | tf_op args[0]
  2.3 0.0 copy-done.1
  2.3 0.0 copy-done.2
  2.3 3.7 %pack.1 = (bf16[16,96,128]{2,1,0:T(8,128)(2,1)}, bf16[16,96,128]{2,1,0:T(8,128)(2,1)S(1)}, s32[8]{0:T(128)S(1)}) custom-call(s32[1]{0:T(128)} %bitcast.2.where_ref, s32[96,128]{1,0:T(8,128)S(1)} %bitcast.13, bf16[96,3,1024]{2,1,0:T(4,128)(2,1)S(1)} %copy.7.qkv_ref, bf16[96,1024]{1,0:T(8,128)(2,1)S(1)} %copy-done.1), custom_call_target="tpu_custom_call" | custom-call | tf_op jit(solution)/shard_map/pack/pallas_call | solution.py:260
  6.1 17.7 %all_to_all.20.own_ref = bf16[16,96,128]{2,1,0:T(8,128)(2,1)S(1)} all-to-all(bf16[16,96,128]{2,1,0:T(8,128)(2,1)S(1)} %get-tuple-element.17), channel_id=1, replica_groups=mesh['x'=4,'y'=4,'z'=4,'core'=2] {'y','z'}, dimensions={0} | all-to-all | bytes 786432 | tf_op jit(solution)/shard_map/all_to_all | solution.py:270
  23.7 3.7 %all-to-all-start = ((bf16[16,96,128]{2,1,0:T(8,128)(2,1)}), bf16[16,96,128]{2,1,0:T(8,128)(2,1)S(1)}, u32[]{:S(2)}, u32[]{:S(2)}) async-start(bf16[16,96,128]{2,1,0:T(8,128)(2,1)} %get-tuple-element.16), calls=%async_computation | async-start | bytes 786432 | tf_op jit(solution)/shard_map/all_to_all | solution.py:268
  27.5 0.1 collective-permute-start.3
  27.6 9.0 %all-to-all-done.kv0 = bf16[16,96,128]{2,1,0:T(8,128)(2,1)S(1)} async-done(((bf16[16,96,128]{2,1,0:T(8,128)(2,1)}), bf16[16,96,128]{2,1,0:T(8,128)(2,1)S(1)}, u32[]{:S(2)}, u32[]{:S(2)}) %all-to-all-start) | async-done | bytes 393248 | tf_op jit(solution)/shard_map/all_to_all | solution.py:268
  36.6 1.5 %collective-permute-start.2 = (bf16[16,96,128]{2,1,0:T(8,128)(2,1)S(1)}, bf16[16,96,128]{2,1,0:T(8,128)(2,1)S(1)}, u32[]{:S(2)}, u32[]{:S(2)}) collective-permute-start(bf16[16,96,128]{2,1,0:T(8,128)(2,1)S(1)} %all-to-all-done.kv0), channel_id=1, source_target_pairs={{0,32},{32,64},{64,96},{96,0},{1,33},{33,65},{65,97},{97,1},{2,34}... | collective-permute-start | bytes 1179656 | tf_op jit(solution)/shard_map/ppermute | solution.py:249
  38.1 1.1 collective-permute-start.1
  39.2 2.2 %collective-permute-start = (bf16[16,96,128]{2,1,0:T(8,128)(2,1)S(1)}, bf16[16,96,128]{2,1,0:T(8,128)(2,1)S(1)}, u32[]{:S(2)}, u32[]{:S(2)}) collective-permute-start(bf16[16,96,128]{2,1,0:T(8,128)(2,1)S(1)} %all-to-all-done.kv0), channel_id=1, source_target_pairs={{0,96},{32,0},{64,32},{96,64},{1,97},{33,1},{65,33},{97,65},{2,98}... | collective-permute-start | bytes 1179656 | tf_op jit(solution)/shard_map/ppermute | solution.py:249
  41.4 0.1 pad_add_fusion.where_ref
  41.4 0.0 copy-done
  41.4 0.0 collective-permute-done.3.other_ref
  41.4 7.2 %collective-permute-done.2.kv3 = bf16[16,96,128]{2,1,0:T(8,128)(2,1)S(1)} collective-permute-done((bf16[16,96,128]{2,1,0:T(8,128)(2,1)S(1)}, bf16[16,96,128]{2,1,0:T(8,128)(2,1)S(1)}, u32[]{:S(2)}, u32[]{:S(2)}) %collective-permute-start.2) | collective-permute-done | bytes 393248 | tf_op jit(solution)/shard_map/ppermute | solution.py:249
  48.6 3.0 %collective-permute-done.1.kv2 = bf16[16,96,128]{2,1,0:T(8,128)(2,1)S(1)} collective-permute-done((bf16[16,96,128]{2,1,0:T(8,128)(2,1)S(1)}, bf16[16,96,128]{2,1,0:T(8,128)(2,1)S(1)}, u32[]{:S(2)}, u32[]{:S(2)}) %collective-permute-start.1) | collective-permute-done | bytes 393248 | tf_op jit(solution)/shard_map/ppermute | solution.py:249
  51.6 3.7 %collective-permute-done.kv1 = bf16[16,96,128]{2,1,0:T(8,128)(2,1)S(1)} collective-permute-done((bf16[16,96,128]{2,1,0:T(8,128)(2,1)S(1)}, bf16[16,96,128]{2,1,0:T(8,128)(2,1)S(1)}, u32[]{:S(2)}, u32[]{:S(2)}) %collective-permute-start) | collective-permute-done | bytes 393248 | tf_op jit(solution)/shard_map/ppermute | solution.py:249
  55.3 34.8 %attend.1 = (bf16[16,96,128]{2,1,0:T(8,128)(2,1)S(1)}, bf16[16,96,128]{2,1,0:T(8,128)(2,1)}, bf16[16,96,128]{2,1,0:T(8,128)(2,1)}, bf16[16,96,128]{2,1,0:T(8,128...) custom-call(s32[2]{0:T(128)S(1)} %pad_add_fusion.where_ref, ...), custom_call_target="tpu_custom_call" | custom-call | tf_op jit(solution)/shard_map/attend/pallas_call | solution.py:273
  90.1 0.0 copy-start.3
  90.1 0.6 copy-done.3
  90.7 0.0 copy-start.4
  90.7 0.8 copy-done.4
  91.5 1.3 collective-permute-start.5
  92.8 2.9 %collective-permute-start.6 = (bf16[16,96,128]{2,1,0:T(8,128)(2,1)}, bf16[16,96,128]{2,1,0:T(8,128)(2,1)S(1)}, u32[]{:S(2)}, u32[]{:S(2)}) collective-permute-start(bf16[16,96,128]{2,1,0:T(8,128)(2,1)} %get-tuple-element.22), channel_id=1, source_target_pairs={{0,64},{32,96},{64,0},{96,32},{1,65},{33,97},{65,1},{97,33},{2,66}... | collective-permute-start | bytes 1179656 | tf_op jit(solution)/shard_map/ppermute | solution.py:249
  95.7 0.2 collective-permute-start.7
  95.9 0.8 reduce_sum.9
  96.7 0.1 collective-permute-start.8
  96.8 1.1 collective-permute-done.8
  97.9 1.8 %collective-permute-start.9 = (f32[20]{0:T(128)S(1)}, f32[20]{0:T(128)S(1)}, u32[]{:S(2)}, u32[]{:S(2)}) collective-permute-start(f32[20]{0:T(128)S(1)} %add.57), channel_id=1, source_target_pairs={{0,32},{32,64},{64,96},{96,0},{1,33},{33,65},{65,97},{97,1},{2,34}... | collective-permute-start | bytes 248 | tf_op jit(solution)/shard_map/ppermute | solution.py:249
  99.7 10.7 %collective-permute-done.9 = f32[20]{0:T(128)S(1)} collective-permute-done((f32[20]{0:T(128)S(1)}, f32[20]{0:T(128)S(1)}, u32[]{:S(2)}, u32[]{:S(2)}) %collective-permute-start.9) | collective-permute-done | bytes 112 | tf_op jit(solution)/shard_map/ppermute | solution.py:249
  110.4 1.7 %collective-permute-start.10 = (f32[20]{0:T(128)S(1)}, f32[20]{0:T(128)S(1)}, u32[]{:S(2)}, u32[]{:S(2)}) collective-permute-start(f32[20]{0:T(128)S(1)} %add.58), channel_id=1, source_target_pairs={{0,64},{32,96},{64,0},{96,32},{1,65},{33,97},{65,1},{97,33},{2,66}... | collective-permute-start | bytes 248 | tf_op jit(solution)/shard_map/ppermute | solution.py:249
  112.0 0.0 collective-permute-start.4
  112.1 3.4 %collective-permute-done.10 = f32[20]{0:T(128)S(1)} collective-permute-done((f32[20]{0:T(128)S(1)}, f32[20]{0:T(128)S(1)}, u32[]{:S(2)}, u32[]{:S(2)}) %collective-permute-start.10) | collective-permute-done | bytes 112 | tf_op jit(solution)/shard_map/ppermute | solution.py:249
  115.5 0.0 collective-permute-done.5
  115.5 0.0 collective-permute-done.6
  115.5 0.0 collective-permute-done.7
  115.5 0.2 add_convert_fusion
  115.7 0.8 pad_maximum_fusion
  116.5 4.0 %all-to-all-start.3 = ((bf16[16,112,128]{2,1,0:T(8,128)(2,1)}), bf16[16,112,128]{2,1,0:T(8,128)(2,1)S(1)}, u32[]{:S(2)}, u32[]{:S(2)}) async-start(bf16[16,112,128]{2,1,0:T(8,128)(2,1)} %pad_maximum_fusion), calls=%async_computation.3 | async-start | bytes 917504 | tf_op jit(solution)/shard_map/all_to_all | solution.py:317
  120.6 0.0 collective-permute-done.4
  120.6 0.8 add_convert_fusion.1
  121.4 8.9 %all-to-all-done.3.dkv_ref = bf16[16,112,128]{2,1,0:T(8,128)(2,1)S(1)} async-done(((bf16[16,112,128]{2,1,0:T(8,128)(2,1)}), bf16[16,112,128]{2,1,0:T(8,128)(2,1)S(1)}, u32[]{:S(2)}, u32[]{:S(2)}) %all-to-all-start.3) | async-done | bytes 458784 | tf_op jit(solution)/shard_map/all_to_all | solution.py:317
  130.3 3.6 %all-to-all-start.2 = ((bf16[16,96,128]{2,1,0:T(8,128)(2,1)}), bf16[16,96,128]{2,1,0:T(8,128)(2,1)S(1)}, u32[]{:S(2)}, u32[]{:S(2)}) async-start(bf16[16,96,128]{2,1,0:T(8,128)(2,1)} %add_convert_fusion.1), calls=%async_computation.2 | async-start | bytes 786432 | tf_op jit(solution)/shard_map/all_to_all | solution.py:316
  133.9 0.6 slice_add_fusion
  134.5 8.5 %all-to-all-done.2.qo_ref = bf16[16,96,128]{2,1,0:T(8,128)(2,1)S(1)} async-done(((bf16[16,96,128]{2,1,0:T(8,128)(2,1)}), bf16[16,96,128]{2,1,0:T(8,128)(2,1)S(1)}, u32[]{:S(2)}, u32[]{:S(2)}) %all-to-all-start.2) | async-done | bytes 393248 | tf_op jit(solution)/shard_map/all_to_all | solution.py:316
  142.9 2.2 %unpack.1 = (bf16[96,1024]{1,0:T(8,128)(2,1)}, bf16[96,3,1024]{2,1,0:T(4,128)(2,1)S(1)}) custom-call(bf16[16,96,128]{2,1,0:T(8,128)(2,1)S(1)} %all-to-all-done.2.qo_ref, bf16[16,112,128]{2,1,0:T(8,128)(2,1)S(1)} %all-to-all-done.3.dkv_ref), custom_call_target="tpu_custom_call" | custom-call | tf_op jit(solution)/shard_map/unpack/pallas_call | solution.py:320
  145.2 1.0 copy.8
  (7 shorter events, 0.1 us)
Async XLA Ops:
  0.6 40.8 %copy-start = (f32[16,20]{1,0:T(8,128)S(1)}, f32[16,20]{1,0:T(8,128)}, u32[]{:S(2)}) copy-start(f32[16,20]{1,0:T(8,128)} %param.6) | copy-start | bytes 3844
  0.7 1.6 %copy-start.1 = (bf16[96,1024]{1,0:T(8,128)(2,1)S(1)}, bf16[96,1024]{1,0:T(8,128)(2,1)}, u32[]{:S(2)}) copy-start(bf16[96,1024]{1,0:T(8,128)(2,1)} %g_ref.1) | copy-start | bytes 589828
  0.7 1.6 %copy-start.2 = (s32[12288]{0:T(1024)S(1)}, s32[12288]{0:T(1024)}, u32[]{:S(2)}) copy-start(s32[12288]{0:T(1024)} %param.7) | copy-start | bytes 147460
  23.7 12.9 %all-to-all-start = ((bf16[16,96,128]{2,1,0:T(8,128)(2,1)}), bf16[16,96,128]{2,1,0:T(8,128)(2,1)S(1)}, u32[]{:S(2)}, u32[]{:S(2)}) async-start(bf16[16,96,128]{2,1,0:T(8,128)(2,1)} %get-tuple-element.16), calls=%async_computation | async-start | bytes 786432 | tf_op jit(solution)/shard_map/all_to_all | solution.py:268
  27.5 14.0 %collective-permute-start.3 = (bf16[16,96,128]{2,1,0:T(8,128)(2,1)S(1)}, bf16[16,96,128]{2,1,0:T(8,128)(2,1)S(1)}, u32[]{:S(2)}, u32[]{:S(2)}) collective-permute-start(bf16[16,96,128]{2,1,0:T(8,128)(2,1)S(1)} %all_to_all.20.own_ref), channel_id=1, source_target_pairs={{0,1},{1,0},{2,3},{3,2},{4,5},{5,4},{6,7},{7,6},{8,9},{9,8},{10,11... | collective-permute-start | bytes 1179656 | tf_op jit(solution)/shard_map/ppermute | solution.py:249
  36.6 12.1 %collective-permute-start.2 = (bf16[16,96,128]{2,1,0:T(8,128)(2,1)S(1)}, bf16[16,96,128]{2,1,0:T(8,128)(2,1)S(1)}, u32[]{:S(2)}, u32[]{:S(2)}) collective-permute-start(bf16[16,96,128]{2,1,0:T(8,128)(2,1)S(1)} %all-to-all-done.kv0), channel_id=1, source_target_pairs={{0,32},{32,64},{64,96},{96,0},{1,33},{33,65},{65,97},{97,1},{2,34}... | collective-permute-start | bytes 1179656 | tf_op jit(solution)/shard_map/ppermute | solution.py:249
  38.1 13.6 %collective-permute-start.1 = (bf16[16,96,128]{2,1,0:T(8,128)(2,1)S(1)}, bf16[16,96,128]{2,1,0:T(8,128)(2,1)S(1)}, u32[]{:S(2)}, u32[]{:S(2)}) collective-permute-start(bf16[16,96,128]{2,1,0:T(8,128)(2,1)S(1)} %all-to-all-done.kv0), channel_id=1, source_target_pairs={{0,64},{32,96},{64,0},{96,32},{1,65},{33,97},{65,1},{97,33},{2,66}... | collective-permute-start | bytes 1179656 | tf_op jit(solution)/shard_map/ppermute | solution.py:249
  39.2 16.1 %collective-permute-start = (bf16[16,96,128]{2,1,0:T(8,128)(2,1)S(1)}, bf16[16,96,128]{2,1,0:T(8,128)(2,1)S(1)}, u32[]{:S(2)}, u32[]{:S(2)}) collective-permute-start(bf16[16,96,128]{2,1,0:T(8,128)(2,1)S(1)} %all-to-all-done.kv0), channel_id=1, source_target_pairs={{0,96},{32,0},{64,32},{96,64},{1,97},{33,1},{65,33},{97,65},{2,98}... | collective-permute-start | bytes 1179656 | tf_op jit(solution)/shard_map/ppermute | solution.py:249
  90.1 0.6 copy-start.3
  90.7 0.8 copy-start.4
  91.5 24.0 %collective-permute-start.5 = (bf16[16,96,128]{2,1,0:T(8,128)(2,1)}, bf16[16,96,128]{2,1,0:T(8,128)(2,1)S(1)}, u32[]{:S(2)}, u32[]{:S(2)}) collective-permute-start(bf16[16,96,128]{2,1,0:T(8,128)(2,1)} %get-tuple-element.21), channel_id=1, source_target_pairs={{0,32},{32,64},{64,96},{96,0},{1,33},{33,65},{65,97},{97,1},{2,34}... | collective-permute-start | bytes 1179656 | tf_op jit(solution)/shard_map/ppermute | solution.py:249
  92.8 22.7 %collective-permute-start.6 = (bf16[16,96,128]{2,1,0:T(8,128)(2,1)}, bf16[16,96,128]{2,1,0:T(8,128)(2,1)S(1)}, u32[]{:S(2)}, u32[]{:S(2)}) collective-permute-start(bf16[16,96,128]{2,1,0:T(8,128)(2,1)} %get-tuple-element.22), channel_id=1, source_target_pairs={{0,64},{32,96},{64,0},{96,32},{1,65},{33,97},{65,1},{97,33},{2,66}... | collective-permute-start | bytes 1179656 | tf_op jit(solution)/shard_map/ppermute | solution.py:249
  95.7 19.8 %collective-permute-start.7 = (bf16[16,96,128]{2,1,0:T(8,128)(2,1)}, bf16[16,96,128]{2,1,0:T(8,128)(2,1)S(1)}, u32[]{:S(2)}, u32[]{:S(2)}) collective-permute-start(bf16[16,96,128]{2,1,0:T(8,128)(2,1)} %get-tuple-element.23), channel_id=1, source_target_pairs={{0,96},{32,0},{64,32},{96,64},{1,97},{33,1},{65,33},{97,65},{2,98}... | collective-permute-start | bytes 1179656 | tf_op jit(solution)/shard_map/ppermute | solution.py:249
  96.7 1.2 collective-permute-start.8
  97.9 12.5 %collective-permute-start.9 = (f32[20]{0:T(128)S(1)}, f32[20]{0:T(128)S(1)}, u32[]{:S(2)}, u32[]{:S(2)}) collective-permute-start(f32[20]{0:T(128)S(1)} %add.57), channel_id=1, source_target_pairs={{0,32},{32,64},{64,96},{96,0},{1,33},{33,65},{65,97},{97,1},{2,34}... | collective-permute-start | bytes 248 | tf_op jit(solution)/shard_map/ppermute | solution.py:249
  110.4 5.0 %collective-permute-start.10 = (f32[20]{0:T(128)S(1)}, f32[20]{0:T(128)S(1)}, u32[]{:S(2)}, u32[]{:S(2)}) collective-permute-start(f32[20]{0:T(128)S(1)} %add.58), channel_id=1, source_target_pairs={{0,64},{32,96},{64,0},{96,32},{1,65},{33,97},{65,1},{97,33},{2,66}... | collective-permute-start | bytes 248 | tf_op jit(solution)/shard_map/ppermute | solution.py:249
  112.0 8.5 %collective-permute-start.4 = (bf16[16,96,128]{2,1,0:T(8,128)(2,1)}, bf16[16,96,128]{2,1,0:T(8,128)(2,1)S(1)}, u32[]{:S(2)}, u32[]{:S(2)}) collective-permute-start(bf16[16,96,128]{2,1,0:T(8,128)(2,1)} %copy-done.4), channel_id=1, source_target_pairs={{0,1},{1,0},{2,3},{3,2},{4,5},{5,4},{6,7},{7,6},{8,9},{9,8},{10,11... | collective-permute-start | bytes 1179656 | tf_op jit(solution)/shard_map/ppermute | solution.py:249
  116.5 13.8 %all-to-all-start.3 = ((bf16[16,112,128]{2,1,0:T(8,128)(2,1)}), bf16[16,112,128]{2,1,0:T(8,128)(2,1)S(1)}, u32[]{:S(2)}, u32[]{:S(2)}) async-start(bf16[16,112,128]{2,1,0:T(8,128)(2,1)} %pad_maximum_fusion), calls=%async_computation.3 | async-start | bytes 917504 | tf_op jit(solution)/shard_map/all_to_all | solution.py:317
  130.3 12.6 %all-to-all-start.2 = ((bf16[16,96,128]{2,1,0:T(8,128)(2,1)}), bf16[16,96,128]{2,1,0:T(8,128)(2,1)S(1)}, u32[]{:S(2)}, u32[]{:S(2)}) async-start(bf16[16,96,128]{2,1,0:T(8,128)(2,1)} %add_convert_fusion.1), calls=%async_computation.2 | async-start | bytes 786432 | tf_op jit(solution)/shard_map/all_to_all | solution.py:316

commit v2 on v1

v2 whole, which is shorter than its diff:
```python
import jax
import jax.numpy as jnp
from jax import lax
from jax.experimental import pallas as pl
from jax.experimental.pallas import tpu as pltpu
from jax.sharding import Mesh
from jax.sharding import PartitionSpec as P

HD = 64
H = 16
NB = 20
DOCS = 8
ROWS = 96
SUPER = 384
GROUPS = 16
PAIR = 768
TALL = 192
WIDE = 256
SLOTS = 256
DEPTH = 6
LOW = -1e30
VMEM = pltpu.VMEM
SMEM = pltpu.SMEM
NT = (((1,), (1,)), ((), ()))


def doc_bounds(ids):
    return [jnp.int32(0)] + [
        jnp.sum((ids < d).astype(jnp.float32)).astype(jnp.int32) for d in range(1, DOCS)
    ]


def pack_kernel(where_ref, ids_ref, qkv_ref, g_ref, out_ref, bounds_ref):
    bounds = doc_bounds(ids_ref[...])
    for d in range(DOCS):
        bounds_ref[d] = bounds[d]
    pos = where_ref[0] + lax.broadcasted_iota(jnp.int32, (ROWS, 128), 0)
    length = jnp.zeros((ROWS, 128), jnp.int32)
    ends = bounds[1:] + [jnp.int32(PAIR * GROUPS)]
    for d in range(DOCS):
        length = jnp.where(pos >= bounds[d], ends[d] - bounds[d], length)
    scale = lax.rsqrt(length.astype(jnp.float32))[:, :HD]
    for h in range(H):
        cols = slice(h * HD, (h + 1) * HD)
        out_ref[h, :ROWS] = jnp.concatenate([qkv_ref[1, :, cols], qkv_ref[2, :, cols]], axis=1)
        q = (qkv_ref[0, :, cols].astype(jnp.float32) * 0.0625).astype(jnp.bfloat16)
        g = (g_ref[:, cols].astype(jnp.float32) * scale).astype(jnp.bfloat16)
        out_ref[h, ROWS:] = jnp.concatenate([q, g], axis=1)


EDGES = [(k, k) for k in range(8)] + [(2**p, p + 6) for p in range(3, 13)]


def edges_of(low, high):
    below = [edge for edge in EDGES if edge[0] <= low]
    return below[-1:], [edge for edge in EDGES if low < edge[0] <= high]


def key_lanes(x, j, second):
    if second:
        late = j >= 128
        j = j + jnp.where(late, 128, 256)
    place = j + 2 * ROWS * lax.div(x, 2) + jnp.where(j >= 2 * ROWS, SUPER - 2 * ROWS, 0)
    return place + jnp.where(late, PAIR, 0) if second else place


SLABS = [
    (PAIR * e - (1535 if second else 639), PAIR * e + (319 if second else 767), e, second)
    for second, count in ((False, 9), (True, 10))
    for e in range(count)
]


def distance(x, core, e, second, row):
    i = row + lax.broadcasted_iota(jnp.int32, (16, WIDE), 0)
    j = lax.broadcasted_iota(jnp.int32, (16, WIDE), 1)
    lower = jnp.minimum(x, 3 - x)
    i = i + ROWS * lower + jnp.where(i >= ROWS, ROWS * (2 - 2 * lower), 0)
    return PAIR * e + SUPER * core + i - key_lanes(x, j, second)


def start_of(bounds_ref, pos):
    start = jnp.int32(0)
    for d in range(1, DOCS):
        start = jnp.where(pos >= bounds_ref[d], bounds_ref[d], start)
    return start


def span_of(x, core, g):
    lower = jnp.minimum(x, 3 - x)
    base = PAIR * g + SUPER * core
    return base + ROWS * lower, base + ROWS * (4 - lower) - 1


def table_kernel(where_ref, rab_ref, bounds_ref, table_ref, plan_ref):
    x, core = where_ref[0], where_ref[1]

    def put(at, g, tile, slab):
        plan_ref[at] = g
        plan_ref[SLOTS + at] = tile
        plan_ref[2 * SLOTS + at] = slab

    put(0, 0, 0, 0)

    def of_group(g, count):
        low = lax.div(start_of(bounds_ref, span_of(x, core, g)[0]), PAIR)

        def first(n, count):
            m = lax.div(n, 2)
            put(count + 1, g, m + n, g - n + 1)
            return count + 1

        def second(m, count):
            put(count + 1, g, 3 * m + 2, g - 2 * m + 10)
            return count + 1

        count = lax.fori_loop(low, g + 1, first, count)
        return lax.fori_loop(lax.div(low, 2), lax.div(g + core + 1, 2), second, count)

    count = lax.fori_loop(0, GROUPS, of_group, jnp.int32(0))
    plan_ref[3 * SLOTS] = count
    for extra in range(1, DEPTH + 2):
        put(count + extra, 0, 0, 0)
    table_ref[0] = jnp.full((TALL, WIDE), LOW, jnp.float32)
    for index, (low, high, e, second) in enumerate(SLABS):
        below, inside = edges_of(low, high)

        @pl.loop(0, TALL // 16)
        def _(step):
            row = pl.multiple_of(step * 16, 16)
            d = distance(x, core, e, second, row)
            value = jnp.full((16, WIDE), rab_ref[below[0][1]] * 0.5 if below else LOW, jnp.float32)
            for edge, b in inside:
                value = jnp.where(d >= edge, rab_ref[b] * 0.5, value)
            table_ref[index + 1, pl.ds(row, 16), :] = value


def buckets_kernel(where_ref, sums_ref, bias_ref, buckets):
    x, core = where_ref[0], where_ref[1]
    buckets[...] = jnp.zeros((NB, 8, 128), jnp.float32)

    def fold(v):
        v = v[:, :128] + v[:, 128:]
        return v[:8] + v[8:]

    for index, (low, high, e, second) in enumerate(SLABS):
        below, inside = edges_of(low, high)

        def step(k, carry):
            row = pl.multiple_of(k * 16, 16)
            d = distance(x, core, e, second, row)
            v = sums_ref[index + 1, pl.ds(row, 16), :]
            terms = [fold(v)] if below else []
            terms = terms + [fold(jnp.where(d >= edge, v, 0.0)) for edge, b in inside]
            return tuple(c + t for c, t in zip(carry, terms))

        found = below + inside
        zero = jnp.zeros((8, 128), jnp.float32)
        sums = lax.fori_loop(0, TALL // 16, step, (zero,) * len(found))
        for k, (edge, b) in enumerate(found):
            rest = sums[k + 1] if k + 1 < len(found) else zero
            buckets[b] += sums[k] - rest
    lane = lax.broadcasted_iota(jnp.int32, (8, 128), 1)
    row = jnp.zeros((8, 128), jnp.float32)
    for b in range(NB):
        total = jnp.sum(jnp.sum(buckets[b], axis=0, keepdims=True), axis=1, keepdims=True)
        row = jnp.where(lane == b, total * 0.5, row)
    bias_ref[...] = row


def main_kernel(
    where_ref, bounds_ref, plan_ref, table, own_ref, kvx_ref, kvc_ref, kvxc_ref, qgx_ref,
    keep_ref, give_ref, mine_ref, theirs_ref, biasacc,
    line, kvs, dkv, starts, scales, acc, lhs, qgt, *stages,
):
    x = where_ref[0]
    core = where_ref[1]
    odd = lax.rem(x, 2)
    lower = jnp.minimum(x, 3 - x)

    def aligned(v):
        return pl.multiple_of(v * ROWS, ROWS)

    k_own = aligned(2 * core + odd)
    k_x = aligned(2 * core + 1 - odd)
    k_core = aligned(2 * (1 - core) + odd)
    k_both = aligned(2 * (1 - core) + 1 - odd)
    q_own = aligned((x != lower).astype(jnp.int32))
    q_x = aligned((x == lower).astype(jnp.int32))
    lane = lax.broadcasted_iota(jnp.int32, (TALL, 128), 1)
    left = lane < HD
    row = lax.broadcasted_iota(jnp.int32, (TALL, 128), 0)
    offset = row + jnp.where(row >= ROWS, ROWS * (2 - 2 * lower), 0)

    @pl.loop(0, GROUPS)
    def _(n):
        line[n, pl.ds(k_own, ROWS), :] = own_ref[n, :ROWS]
        line[n, pl.ds(k_x, ROWS), :] = kvx_ref[n]
        line[n, pl.ds(k_core, ROWS), :] = kvc_ref[n]
        line[n, pl.ds(k_both, ROWS), :] = kvxc_ref[n]
        acc[n] = jnp.zeros((TALL, 128), jnp.float32)
        zero = jnp.zeros((ROWS, 128), jnp.bfloat16)
        for at, qg in ((q_own, own_ref[n, ROWS:]), (q_x, qgx_ref[n])):
            lhs[n, pl.ds(at, ROWS), :] = jnp.where(left[:ROWS], qg, zero)
            lhs[n, pl.ds(pl.multiple_of(at + TALL, ROWS), ROWS), :] = jnp.where(left[:ROWS], zero, qg)
        qgt[n] = (lhs[n, pl.ds(0, TALL), :] + lhs[n, pl.ds(TALL, TALL), :]).T
        first, last = span_of(x, core, n)
        pos = first + offset

        def history(d, low):
            begin = bounds_ref[d]
            end = jnp.where(d + 1 < DOCS, bounds_ref[jnp.minimum(d + 1, DOCS - 1)], PAIR * GROUPS)
            inside = pos >= begin
            size = jnp.full((TALL, 128), end - begin, jnp.int32).astype(jnp.float32)
            starts[n] = jnp.where(inside, begin, starts[n])
            scales[n] = jnp.where(left, 0.0625, jnp.where(inside, lax.rsqrt(size), scales[n]))
            return low

        d_first, d_last = jnp.int32(0), jnp.int32(0)
        for d in range(1, DOCS):
            d_first = d_first + (first >= bounds_ref[d]).astype(jnp.int32)
            d_last = d_last + (last >= bounds_ref[d]).astype(jnp.int32)
        starts[n] = jnp.zeros((TALL, 128), jnp.int32)
        scales[n] = jnp.zeros((TALL, 128), jnp.float32)
        lax.fori_loop(d_first, d_last + 1, history, 0)

    @pl.loop(0, GROUPS // 2)
    def _(m):
        kvs[3 * m] = line[2 * m, :WIDE]
        kvs[3 * m + 1] = line[2 * m + 1, :WIDE]
        kvs[3 * m + 2, :128] = line[2 * m, WIDE:]
        kvs[3 * m + 2, 128:] = line[2 * m + 1, WIDE:]
        for r in range(3):
            dkv[3 * m + r] = jnp.zeros((128, WIDE), jnp.float32)

    @pl.loop(0, len(SLABS) + 1)
    def _(e):
        biasacc[e] = jnp.zeros((TALL, WIDE), jnp.float32)

    score, weight = stages[:DEPTH], stages[DEPTH:]
    weight[0][...] = jnp.zeros((2 * TALL, WIDE), jnp.bfloat16)
    j = lax.broadcasted_iota(jnp.int32, (1, WIDE), 1)
    first_lanes, second_lanes = key_lanes(x, j, False), key_lanes(x, j, True)

    def scores(k, s):
        g, n = plan_ref[k], plan_ref[SLOTS + k]
        s[...] = lax.dot_general(lhs[g], kvs[n], NT, preferred_element_type=jnp.float32)

    def weigh(k, s, w_out):
        g, n, e = plan_ref[k], plan_ref[SLOTS + k], plan_ref[2 * SLOTS + k]
        m = lax.div(n, 3)
        key = jnp.where(e > 9, second_lanes, first_lanes)
        key = key + PAIR * (2 * m + (n - 3 * m == 1).astype(jnp.int32))
        begin = jnp.concatenate([starts[g]] * 2, axis=1)
        half = jnp.where(key >= begin, s[pl.ds(0, TALL), :] + table[e], LOW)
        t = jnp.tanh(half)
        u = 1.0 + t
        w = half * u
        ds = s[pl.ds(TALL, TALL), :] * (u + w * (1.0 - t))
        biasacc[e] += ds
        w_out[pl.ds(0, TALL), :] = w.astype(jnp.bfloat16)
        w_out[pl.ds(TALL, TALL), :] = ds.astype(jnp.bfloat16)

    def gather(k, w_in):
        g, n = plan_ref[k], plan_ref[SLOTS + k]
        od = jnp.dot(w_in[...], kvs[n], preferred_element_type=jnp.float32)
        acc[g] += jnp.where(left, od[TALL:], od[:TALL])
        dkv[n, pl.ds(0, HD), :] += jnp.dot(
            qgt[g, pl.ds(0, HD), :], w_in[pl.ds(TALL, TALL), :], preferred_element_type=jnp.float32
        )
        dkv[n, pl.ds(HD, HD), :] += jnp.dot(
            qgt[g, pl.ds(HD, HD), :], w_in[pl.ds(0, TALL), :], preferred_element_type=jnp.float32
        )

    scores(1, score[1])

    @pl.loop(0, lax.div(plan_ref[3 * SLOTS] + DEPTH, DEPTH))
    def _(step):
        for i in range(DEPTH):
            k = DEPTH * step + i
            now, later = (i + 1) % DEPTH, (i + 2) % DEPTH
            gather(k, weight[i])
            weigh(k + 1, score[now], weight[now])
            scores(k + 2, score[later])

    @pl.loop(0, GROUPS // 2)
    def _(m):
        line[2 * m, :WIDE] = dkv[3 * m].astype(jnp.bfloat16).T
        line[2 * m + 1, :WIDE] = dkv[3 * m + 1].astype(jnp.bfloat16).T
        last = dkv[3 * m + 2].astype(jnp.bfloat16).T
        line[2 * m, WIDE:] = last[:128]
        line[2 * m + 1, WIDE:] = last[128:]

    @pl.loop(0, GROUPS)
    def _(n):
        acc[n] = acc[n] * scales[n]
        mine_ref[n] = acc[n, pl.ds(q_own, ROWS), :]
        theirs_ref[n] = acc[n, pl.ds(q_x, ROWS), :].astype(jnp.bfloat16)
        keep_ref[n, :ROWS] = line[n, pl.ds(k_own, ROWS), :]
        keep_ref[n, ROWS:] = line[n, pl.ds(k_x, ROWS), :]
        give_ref[n, :ROWS] = line[n, pl.ds(k_core, ROWS), :]
        give_ref[n, ROWS:] = line[n, pl.ds(k_both, ROWS), :]


def unpack_kernel(in_ref, out_ref, grad_ref):
    for h in range(0, H, 2):
        cols = slice(h * HD, (h + 2) * HD)
        a, b = in_ref[h, :ROWS], in_ref[h + 1, :ROWS]
        grad_ref[0, :, cols] = jnp.concatenate([a[:, :HD], b[:, :HD]], axis=1)
        out_ref[:, cols] = jnp.concatenate([a[:, HD:], b[:, HD:]], axis=1)
        a, b = in_ref[h, ROWS : 2 * ROWS], in_ref[h + 1, ROWS : 2 * ROWS]
        grad_ref[1, :, cols] = jnp.concatenate([a[:, :HD], b[:, :HD]], axis=1)
        grad_ref[2, :, cols] = jnp.concatenate([a[:, HD:], b[:, HD:]], axis=1)


def swap(v, axis, partner):
    return lax.ppermute(v, axis, [(i, p) for i, p in enumerate(partner)])


def per_device(qkv, grad_out, rab, doc_ids):
    bf16, f32 = jnp.bfloat16, jnp.float32
    x, y, z, core = (lax.axis_index(a) for a in ("x", "y", "z", "core"))
    whole = pl.BlockSpec(memory_space=VMEM)
    scalars = pl.BlockSpec(memory_space=SMEM)
    block = jax.ShapeDtypeStruct((H, ROWS, 128), bf16)
    double = jax.ShapeDtypeStruct((H, 2 * ROWS, 128), bf16)
    slabs = jax.ShapeDtypeStruct((len(SLABS) + 1, TALL, WIDE), f32)
    params = pltpu.CompilerParams(vmem_limit_bytes=48 * 2**20)
    first_row = (((y * 4 + z) * 2 + core) * 4 + x) * ROWS
    where = jnp.stack([x, core])
    packed, bounds = pl.pallas_call(
        pack_kernel,
        out_shape=(double, jax.ShapeDtypeStruct((DOCS,), jnp.int32)),
        in_specs=[scalars, whole, whole, whole],
        out_specs=(whole, scalars),
        compiler_params=params,
        name="pack",
    )(first_row.reshape(1), doc_ids.reshape(96, 128), qkv.transpose(1, 0, 2), grad_out)
    own = lax.all_to_all(packed, ("y", "z"), 0, 0, tiled=True)
    kv_own, qg_own = own[:, :ROWS], own[:, ROWS:]
    kv_x = swap(kv_own, "x", (1, 0, 3, 2))
    qg_x = swap(qg_own, "x", (3, 2, 1, 0))
    kv_core = swap(kv_own, "core", (1, 0))
    kv_both = swap(kv_x, "core", (1, 0))
    table_row = lax.dynamic_slice_in_dim(rab, y * 4 + z, 1, 0)[0]
    table, plan = pl.pallas_call(
        table_kernel,
        out_shape=(slabs, jax.ShapeDtypeStruct((3 * SLOTS + 1,), jnp.int32)),
        in_specs=[scalars] * 3,
        out_specs=(whole, scalars),
        compiler_params=params,
        cost_estimate=pl.CostEstimate(flops=10**7, bytes_accessed=3 * 10**6, transcendentals=0),
        name="table",
    )(where, table_row, bounds)
    keep, give, mine, theirs, sums = pl.pallas_call(
        main_kernel,
        out_shape=[double, double, jax.ShapeDtypeStruct((H, ROWS, 128), f32), block, slabs],
        in_specs=[scalars] * 3 + [whole] * 6,
        out_specs=[whole] * 5,
        scratch_shapes=[
            VMEM((GROUPS, SUPER, 128), bf16),
            VMEM((24, WIDE, 128), bf16),
            VMEM((24, 128, WIDE), f32),
            VMEM((GROUPS, TALL, 128), jnp.int32),
            VMEM((GROUPS, TALL, 128), f32),
            VMEM((GROUPS, TALL, 128), f32),
            VMEM((GROUPS, 2 * TALL, 128), bf16),
            VMEM((GROUPS, 128, TALL), bf16),
        ]
        + [VMEM((2 * TALL, WIDE), f32)] * DEPTH
        + [VMEM((2 * TALL, WIDE), bf16)] * DEPTH,
        compiler_params=params,
        name="attend",
    )(where, bounds, plan, table, own, kv_x, kv_core, kv_both, qg_x)
    got = swap(give, "core", (1, 0))
    got_qo = swap(theirs, "x", (3, 2, 1, 0))
    bias = pl.pallas_call(
        buckets_kernel,
        out_shape=jax.ShapeDtypeStruct((8, 128), f32),
        in_specs=[scalars, whole],
        out_specs=whole,
        scratch_shapes=[VMEM((NB, 8, 128), f32)],
        compiler_params=params,
        cost_estimate=pl.CostEstimate(flops=10**7, bytes_accessed=3 * 10**6, transcendentals=0),
        name="buckets",
    )(where, sums)
    dkv = keep.astype(f32) + got.astype(f32)
    got_dkv = swap(dkv[:, ROWS:].astype(bf16), "x", (1, 0, 3, 2))
    bias = bias + swap(bias, "core", (1, 0))
    bias = bias + sum(swap(bias, "x", p) for p in ((1, 0, 3, 2), (3, 2, 1, 0), (2, 3, 0, 1)))
    bias = bias[0]
    hi = lax.reduce_precision(bias, 8, 7)
    mid = lax.reduce_precision(bias - hi, 8, 7)
    lo = bias - hi - mid
    carried = jnp.pad(jnp.stack([hi, mid, lo]).astype(bf16), ((0, 13), (0, 0)))
    results = jnp.concatenate(
        [
            (mine + got_qo.astype(f32)).astype(bf16),
            (dkv[:, :ROWS] + got_dkv.astype(f32)).astype(bf16),
            jnp.broadcast_to(carried[None], (H, 16, 128)),
        ],
        axis=1,
    )
    results = lax.all_to_all(results, ("y", "z"), 0, 0, tiled=True)
    terms = lax.dynamic_slice(results, (x * 4, 2 * ROWS, 0), (4, 3, NB)).astype(f32)
    bias_grad = terms[:, 0] + terms[:, 1] + terms[:, 2]
    out, grad_qkv = pl.pallas_call(
        unpack_kernel,
        out_shape=(
            jax.ShapeDtypeStruct((ROWS, H * HD), bf16),
            jax.ShapeDtypeStruct((3, ROWS, H * HD), bf16),
        ),
        in_specs=[whole],
        out_specs=(whole, whole),
        compiler_params=params,
        name="unpack",
    )(results)
    return out, grad_qkv.transpose(1, 0, 2), bias_grad


def solution(mesh):
    fine = Mesh(mesh.devices.reshape(4, 4, 4, 2), ("x", "y", "z", "core"))
    rows = ("y", "z", "core", "x")
    return jax.shard_map(
        per_device,
        mesh=fine,
        in_specs=(P(rows, None, None), P(rows, None), P(), P()),
        out_specs=(P(rows, None), P(rows, None, None), P("x", None)),
        check_vma=False,
    )
```

time: 147 us -> 113 us (0.77)
  the two profiles are of different devices: /device:TPU:2 before, /device:TPU:0 now
where the time goes in v2:
time: 113 us; the launch traced here: 112 us
  Pallas kernels  33.7 us (30%)
  waiting for transfers between devices  31.8 us (28%)
  blocking collectives  22.1 us (20%)
  starting transfers between devices  15.3 us (14%)
  local copies, waits for them, and re-layouts  6.88 us (6%)
  other arithmetic  2.01 us (2%)
    pallas_call x1, Pallas kernels, per_device(): pl.pallas_call(main_kernel, out_shape=[double, double, jax.ShapeDtypeStru...  22.5 us
    all_to_all x1, blocking collectives, per_device(): own = lax.all_to_all(packed, ('y', 'z'), 0, 0, tiled=True)  22.1 us
    ppermute x11, waiting for transfers between devices, swap(): return lax.ppermute(v, axis, [(i, p) for i, p in enumerate(partner)])  18.6 us
    all_to_all x1, waiting for transfers between devices, per_device(): results = lax.all_to_all(results, ('y', 'z'), 0, 0, tiled=True)  13.2 us
    ppermute x11, starting transfers between devices, swap(): return lax.ppermute(v, axis, [(i, p) for i, p in enumerate(partner)])  11.7 us
    unnamed x12, local copies, waits for them, and re-layouts  6.75 us
    pallas_call x1, Pallas kernels, per_device(): pl.pallas_call(table_kernel, out_shape=(slabs, jax.ShapeDtypeStruct((3 *...  5.16 us
    pallas_call x1, Pallas kernels, per_device(): pl.pallas_call(buckets_kernel, out_shape=jax.ShapeDtypeStruct((8, 128), f...  4.06 us
  transfers between devices with their start and end apart: 12, of which 6 were waited for; matrix products, arithmetic and copies ran while one was open for 0% of the time, Pallas kernels for 8%

profile of v2, /device:TPU:0, one launch (start us, length us, event | category | flops | bytes accessed | tf_op | source)
XLA Modules:
  0.0 112.5 jit_solution(18397856238689648292)
XLA Ops:
  0.6 0.0 copy-start
  0.7 0.0 copy-start.3
  0.7 1.1 copy-done.3
  1.7 0.0 copy-start.4
  1.7 0.9 copy-done.4
  2.7 0.0 copy-start.5
  2.7 0.8 copy-done.5
  3.5 0.8 pack.1
  4.2 22.1 %all_to_all.10.own_ref = bf16[16,192,128]{2,1,0:T(8,128)(2,1)S(1)} all-to-all(bf16[16,192,128]{2,1,0:T(8,128)(2,1)S(1)} %get-tuple-element.17), channel_id=1, replica_groups=mesh['x'=4,'y'=4,'z'=4,'core'=2] {'y','z'}, dimensions={0} | all-to-all | bytes 1572864 | tf_op jit(solution)/shard_map/all_to_all | solution.py:339
  26.3 0.1 fusion.7
  26.3 1.6 %collective-permute-start = (bf16[16,96,128]{2,1,0:T(8,128)(2,1)S(1)}, bf16[16,96,128]{2,1,0:T(8,128)(2,1)S(1)}, u32[]{:S(2)}, u32[]{:S(2)}) collective-permute-start(bf16[16,96,128]{2,1,0:T(8,128)(2,1)S(1)} %get-tuple-element.26), channel_id=1, source_target_pairs={{0,32},{32,0},{64,96},{96,64},{1,33},{33,1},{65,97},{97,65},{2,34}... | collective-permute-start | bytes 1179656 | tf_op jit(solution)/shard_map/ppermute | solution.py:317
  27.9 0.0 collective-permute-start.1
  27.9 2.1 %collective-permute-start.3 = (bf16[16,96,128]{2,1,0:T(8,128)(2,1)S(1)}, bf16[16,96,128]{2,1,0:T(8,128)(2,1)S(1)}, u32[]{:S(2)}, u32[]{:S(2)}) collective-permute-start(bf16[16,96,128]{2,1,0:T(8,128)(2,1)S(1)} %get-tuple-element.25), channel_id=1, source_target_pairs={{0,96},{32,64},{64,32},{96,0},{1,97},{33,65},{65,33},{97,1},{2,98}... | collective-permute-start | bytes 1179656 | tf_op jit(solution)/shard_map/ppermute | solution.py:317
  30.0 6.2 %collective-permute-done.kvx_ref = bf16[16,96,128]{2,1,0:T(8,128)(2,1)S(1)} collective-permute-done((bf16[16,96,128]{2,1,0:T(8,128)(2,1)S(1)}, bf16[16,96,128]{2,1,0:T(8,128)(2,1)S(1)}, u32[]{:S(2)}, u32[]{:S(2)}) %collective-permute-start) | collective-permute-done | bytes 393248 | tf_op jit(solution)/shard_map/ppermute | solution.py:317
  36.2 0.0 collective-permute-start.2
  36.2 0.1 pad_add_fusion.where_ref
  36.3 0.0 copy-done
  36.3 5.2 %table.1 = (f32[20,192,256]{2,1,0:T(8,128)S(1)}, s32[769]{0:T(1024)S(1)}) custom-call(s32[2]{0:T(128)S(1)} %pad_add_fusion.where_ref, f32[20]{0:T(128)S(1)} %dynamic-slice_bitcast_fusion.rab_ref, s32[8]{0:T(128)S(1)} %get-tuple-element.14.bounds_ref), custom_call_target="tpu_custom_call" | custom-call | flops 10000000 | bytes 3000000 | tf_op jit(solution)/shard_map/table/pallas_call | solution.py:346
  41.5 0.0 copy-start.2
  41.5 1.8 %copy-done.2 = f32[20,192,256]{2,1,0:T(8,128)} copy-done((f32[20,192,256]{2,1,0:T(8,128)}, f32[20,192,256]{2,1,0:T(8,128)S(1)}, u32[]{:S(2)}) %copy-start.2) | copy-done | bytes 3932184
  43.4 0.0 collective-permute-done.3.qgx_ref
  43.4 0.0 collective-permute-done.1.kvc_ref
  43.4 0.0 collective-permute-done.2.kvxc_ref
  43.4 22.5 %attend.1 = (bf16[16,192,128]{2,1,0:T(8,128)(2,1)S(1)}, bf16[16,192,128]{2,1,0:T(8,128)(2,1)S(1)}, f32[16,96,128]{2,1,0:T(8,128)S(1)}, bf16[16,96,128]{2,1,0:T(8,128)(2,1)S(1)}, f32[20,192,256]{2,1,0:T(8,128)}) custom-call(s32[2]{0:T(128)S(1)} %pad_add_fusion.where_ref, s32[8]{0:T(128)S(1)} %get-tuple-element.14.bounds_ref, ...), custom_call_target="tpu_custom_call" | custom-call | tf_op jit(solution)/shard_map/attend/pallas_call | solution.py:355
  65.9 1.6 %collective-permute-start.5 = (bf16[16,192,128]{2,1,0:T(8,128)(2,1)S(1)}, bf16[16,192,128]{2,1,0:T(8,128)(2,1)S(1)}, u32[]{:S(2)}, u32[]{:S(2)}) collective-permute-start(bf16[16,192,128]{2,1,0:T(8,128)(2,1)S(1)} %get-tuple-element.21), channel_id=1, source_target_pairs={{0,1},{1,0},{2,3},{3,2},{4,5},{5,4},{6,7},{7,6},{8,9},{9,8},{10,11... | collective-permute-start | bytes 2359304 | tf_op jit(solution)/shard_map/ppermute | solution.py:317
  67.4 0.0 copy-start.1
  67.4 2.1 %copy-done.1 = f32[20,192,256]{2,1,0:T(8,128)S(1)} copy-done((f32[20,192,256]{2,1,0:T(8,128)S(1)}, f32[20,192,256]{2,1,0:T(8,128)}, u32[]{:S(2)}) %copy-start.1) | copy-done | bytes 3932184
  69.5 4.1 %buckets.1 = f32[8,128]{1,0:T(8,128)S(1)} custom-call(s32[2]{0:T(128)S(1)} %pad_add_fusion.where_ref, f32[20,192,256]{2,1,0:T(8,128)S(1)} %copy-done.1), custom_call_target="tpu_custom_call" | custom-call | flops 10000000 | bytes 3000000 | tf_op jit(solution)/shard_map/buckets/pallas_call | solution.py:377
  73.6 0.1 collective-permute-start.7
  73.7 1.2 %collective-permute-done.7 = f32[8,128]{1,0:T(8,128)S(1)} collective-permute-done((f32[8,128]{1,0:T(8,128)S(1)}, f32[8,128]{1,0:T(8,128)S(1)}, u32[]{:S(2)}, u32[]{:S(2)}) %collective-permute-start.7) | collective-permute-done | bytes 4128 | tf_op jit(solution)/shard_map/ppermute | solution.py:317
  74.9 3.0 %collective-permute-start.10 = (f32[8,128]{1,0:T(8,128)S(1)}, f32[8,128]{1,0:T(8,128)S(1)}, u32[]{:S(2)}, u32[]{:S(2)}) collective-permute-start(f32[8,128]{1,0:T(8,128)S(1)} %add.56), channel_id=1, source_target_pairs={{0,64},{32,96},{64,0},{96,32},{1,65},{33,97},{65,1},{97,33},{2,66}... | collective-permute-start | bytes 12296 | tf_op jit(solution)/shard_map/ppermute | solution.py:317
  77.9 1.1 %collective-permute-start.9 = (f32[8,128]{1,0:T(8,128)S(1)}, f32[8,128]{1,0:T(8,128)S(1)}, u32[]{:S(2)}, u32[]{:S(2)}) collective-permute-start(f32[8,128]{1,0:T(8,128)S(1)} %add.56), channel_id=1, source_target_pairs={{0,96},{32,64},{64,32},{96,0},{1,97},{33,65},{65,33},{97,1},{2,98}... | collective-permute-start | bytes 12296 | tf_op jit(solution)/shard_map/ppermute | solution.py:317
  79.0 0.0 collective-permute-start.8
  79.0 2.1 %collective-permute-start.4 = (bf16[16,96,128]{2,1,0:T(8,128)(2,1)S(1)}, bf16[16,96,128]{2,1,0:T(8,128)(2,1)S(1)}, u32[]{:S(2)}, u32[]{:S(2)}) collective-permute-start(bf16[16,96,128]{2,1,0:T(8,128)(2,1)S(1)} %get-tuple-element.19), channel_id=1, source_target_pairs={{0,96},{32,64},{64,32},{96,0},{1,97},{33,65},{65,33},{97,1},{2,98}... | collective-permute-start | bytes 1179656 | tf_op jit(solution)/shard_map/ppermute | solution.py:317
  81.1 0.0 collective-permute-done.10
  81.1 1.6 %collective-permute-done.9 = f32[8,128]{1,0:T(8,128)S(1)} collective-permute-done((f32[8,128]{1,0:T(8,128)S(1)}, f32[8,128]{1,0:T(8,128)S(1)}, u32[]{:S(2)}, u32[]{:S(2)}) %collective-permute-start.9) | collective-permute-done | bytes 4128 | tf_op jit(solution)/shard_map/ppermute | solution.py:317
  82.7 0.0 collective-permute-done.8
  82.8 0.0 collective-permute-done.5
  82.8 0.2 convert_add_fusion
  83.0 0.1 slice.55
  83.0 0.1 collective-permute-start.6
  83.1 7.8 %collective-permute-done.4 = bf16[16,96,128]{2,1,0:T(8,128)(2,1)S(1)} collective-permute-done((bf16[16,96,128]{2,1,0:T(8,128)(2,1)S(1)}, bf16[16,96,128]{2,1,0:T(8,128)(2,1)S(1)}, u32[]{:S(2)}, u32[]{:S(2)}) %collective-permute-start.4) | collective-permute-done | bytes 393248 | tf_op jit(solution)/shard_map/ppermute | solution.py:317
  90.9 0.1 add_convert_fusion
  91.0 1.8 %collective-permute-done.6 = bf16[16,96,128]{2,1,0:T(8,128)(2,1)S(1)} collective-permute-done((bf16[16,96,128]{2,1,0:T(8,128)(2,1)S(1)}, bf16[16,96,128]{2,1,0:T(8,128)(2,1)S(1)}, u32[]{:S(2)}, u32[]{:S(2)}) %collective-permute-start.6) | collective-permute-done | bytes 393248 | tf_op jit(solution)/shard_map/ppermute | solution.py:317
  92.8 0.1 fusion
  92.9 1.0 pad_maximum_fusion
  93.9 3.6 %all-to-all-start.1 = ((bf16[16,208,128]{2,1,0:T(8,128)(2,1)}), bf16[16,208,128]{2,1,0:T(8,128)(2,1)S(1)}, u32[]{:S(2)}, u32[]{:S(2)}) async-start(bf16[16,208,128]{2,1,0:T(8,128)(2,1)} %pad_maximum_fusion), calls=%async_computation.1 | async-start | bytes 1703936 | tf_op jit(solution)/shard_map/all_to_all | solution.py:404
  97.5 13.2 %all-to-all-done.1.in_ref = bf16[16,208,128]{2,1,0:T(8,128)(2,1)S(1)} async-done(((bf16[16,208,128]{2,1,0:T(8,128)(2,1)}), bf16[16,208,128]{2,1,0:T(8,128)(2,1)S(1)}, u32[]{:S(2)}, u32[]{:S(2)}) %all-to-all-start.1) | async-done | bytes 852000 | tf_op jit(solution)/shard_map/all_to_all | solution.py:404
  110.7 0.6 slice_add_fusion.1
  111.3 1.2 %unpack.1 = (bf16[96,1024]{1,0:T(8,128)(2,1)}, bf16[3,96,1024]{2,1,0:T(8,128)(2,1)}) custom-call(bf16[16,208,128]{2,1,0:T(8,128)(2,1)S(1)} %all-to-all-done.1.in_ref), custom_call_target="tpu_custom_call" | custom-call | tf_op jit(solution)/shard_map/unpack/pallas_call | solution.py:407
  (7 shorter events, 0.0 us)
Async XLA Ops:
  0.6 35.7 %copy-start = (f32[16,20]{1,0:T(8,128)S(1)}, f32[16,20]{1,0:T(8,128)}, u32[]{:S(2)}) copy-start(f32[16,20]{1,0:T(8,128)} %param.6) | copy-start | bytes 3844
  0.7 1.1 copy-start.3
  1.7 0.9 copy-start.4
  2.7 0.8 copy-start.5
  26.3 9.9 %collective-permute-start = (bf16[16,96,128]{2,1,0:T(8,128)(2,1)S(1)}, bf16[16,96,128]{2,1,0:T(8,128)(2,1)S(1)}, u32[]{:S(2)}, u32[]{:S(2)}) collective-permute-start(bf16[16,96,128]{2,1,0:T(8,128)(2,1)S(1)} %get-tuple-element.26), channel_id=1, source_target_pairs={{0,32},{32,0},{64,96},{96,64},{1,33},{33,1},{65,97},{97,65},{2,34}... | collective-permute-start | bytes 1179656 | tf_op jit(solution)/shard_map/ppermute | solution.py:317
  27.9 15.4 %collective-permute-start.1 = (bf16[16,96,128]{2,1,0:T(8,128)(2,1)S(1)}, bf16[16,96,128]{2,1,0:T(8,128)(2,1)S(1)}, u32[]{:S(2)}, u32[]{:S(2)}) collective-permute-start(bf16[16,96,128]{2,1,0:T(8,128)(2,1)S(1)} %get-tuple-element.26), channel_id=1, source_target_pairs={{0,1},{1,0},{2,3},{3,2},{4,5},{5,4},{6,7},{7,6},{8,9},{9,8},{10,11... | collective-permute-start | bytes 1179656 | tf_op jit(solution)/shard_map/ppermute | solution.py:317
  27.9 15.4 %collective-permute-start.3 = (bf16[16,96,128]{2,1,0:T(8,128)(2,1)S(1)}, bf16[16,96,128]{2,1,0:T(8,128)(2,1)S(1)}, u32[]{:S(2)}, u32[]{:S(2)}) collective-permute-start(bf16[16,96,128]{2,1,0:T(8,128)(2,1)S(1)} %get-tuple-element.25), channel_id=1, source_target_pairs={{0,96},{32,64},{64,32},{96,0},{1,97},{33,65},{65,33},{97,1},{2,98}... | collective-permute-start | bytes 1179656 | tf_op jit(solution)/shard_map/ppermute | solution.py:317
  36.2 7.1 %collective-permute-start.2 = (bf16[16,96,128]{2,1,0:T(8,128)(2,1)S(1)}, bf16[16,96,128]{2,1,0:T(8,128)(2,1)S(1)}, u32[]{:S(2)}, u32[]{:S(2)}) collective-permute-start(bf16[16,96,128]{2,1,0:T(8,128)(2,1)S(1)} %collective-permute-done.kvx_ref), channel_id=1, source_target_pairs={{0,1},{1,0},{2,3},{3,2},{4,5},{5,4},{6,7},{7,6},{8,9},{9,8},{10,11... | collective-permute-start | bytes 1179656 | tf_op jit(solution)/shard_map/ppermute | solution.py:317
  41.5 1.9 %copy-start.2 = (f32[20,192,256]{2,1,0:T(8,128)}, f32[20,192,256]{2,1,0:T(8,128)S(1)}, u32[]{:S(2)}) copy-start(f32[20,192,256]{2,1,0:T(8,128)S(1)} %get-tuple-element.16.table) | copy-start | bytes 11796484
  65.9 16.9 %collective-permute-start.5 = (bf16[16,192,128]{2,1,0:T(8,128)(2,1)S(1)}, bf16[16,192,128]{2,1,0:T(8,128)(2,1)S(1)}, u32[]{:S(2)}, u32[]{:S(2)}) collective-permute-start(bf16[16,192,128]{2,1,0:T(8,128)(2,1)S(1)} %get-tuple-element.21), channel_id=1, source_target_pairs={{0,1},{1,0},{2,3},{3,2},{4,5},{5,4},{6,7},{7,6},{8,9},{9,8},{10,11... | collective-permute-start | bytes 2359304 | tf_op jit(solution)/shard_map/ppermute | solution.py:317
  67.4 2.1 %copy-start.1 = (f32[20,192,256]{2,1,0:T(8,128)S(1)}, f32[20,192,256]{2,1,0:T(8,128)}, u32[]{:S(2)}) copy-start(f32[20,192,256]{2,1,0:T(8,128)} %get-tuple-element.22.sums_ref) | copy-start | bytes 11796484
  73.6 1.2 %collective-permute-start.7 = (f32[8,128]{1,0:T(8,128)S(1)}, f32[8,128]{1,0:T(8,128)S(1)}, u32[]{:S(2)}, u32[]{:S(2)}) collective-permute-start(f32[8,128]{1,0:T(8,128)S(1)} %buckets.1), channel_id=1, source_target_pairs={{0,1},{1,0},{2,3},{3,2},{4,5},{5,4},{6,7},{7,6},{8,9},{9,8},{10,11... | collective-permute-start | bytes 12296 | tf_op jit(solution)/shard_map/ppermute | solution.py:317
  74.9 6.3 %collective-permute-start.10 = (f32[8,128]{1,0:T(8,128)S(1)}, f32[8,128]{1,0:T(8,128)S(1)}, u32[]{:S(2)}, u32[]{:S(2)}) collective-permute-start(f32[8,128]{1,0:T(8,128)S(1)} %add.56), channel_id=1, source_target_pairs={{0,64},{32,96},{64,0},{96,32},{1,65},{33,97},{65,1},{97,33},{2,66}... | collective-permute-start | bytes 12296 | tf_op jit(solution)/shard_map/ppermute | solution.py:317
  77.9 4.9 %collective-permute-start.9 = (f32[8,128]{1,0:T(8,128)S(1)}, f32[8,128]{1,0:T(8,128)S(1)}, u32[]{:S(2)}, u32[]{:S(2)}) collective-permute-start(f32[8,128]{1,0:T(8,128)S(1)} %add.56), channel_id=1, source_target_pairs={{0,96},{32,64},{64,32},{96,0},{1,97},{33,65},{65,33},{97,1},{2,98}... | collective-permute-start | bytes 12296 | tf_op jit(solution)/shard_map/ppermute | solution.py:317
  79.0 3.7 %collective-permute-start.8 = (f32[8,128]{1,0:T(8,128)S(1)}, f32[8,128]{1,0:T(8,128)S(1)}, u32[]{:S(2)}, u32[]{:S(2)}) collective-permute-start(f32[8,128]{1,0:T(8,128)S(1)} %add.56), channel_id=1, source_target_pairs={{0,32},{32,0},{64,96},{96,64},{1,33},{33,1},{65,97},{97,65},{2,34}... | collective-permute-start | bytes 12296 | tf_op jit(solution)/shard_map/ppermute | solution.py:317
  79.0 11.9 %collective-permute-start.4 = (bf16[16,96,128]{2,1,0:T(8,128)(2,1)S(1)}, bf16[16,96,128]{2,1,0:T(8,128)(2,1)S(1)}, u32[]{:S(2)}, u32[]{:S(2)}) collective-permute-start(bf16[16,96,128]{2,1,0:T(8,128)(2,1)S(1)} %get-tuple-element.19), channel_id=1, source_target_pairs={{0,96},{32,64},{64,32},{96,0},{1,97},{33,65},{65,33},{97,1},{2,98}... | collective-permute-start | bytes 1179656 | tf_op jit(solution)/shard_map/ppermute | solution.py:317
  83.0 9.8 %collective-permute-start.6 = (bf16[16,96,128]{2,1,0:T(8,128)(2,1)S(1)}, bf16[16,96,128]{2,1,0:T(8,128)(2,1)S(1)}, u32[]{:S(2)}, u32[]{:S(2)}) collective-permute-start(bf16[16,96,128]{2,1,0:T(8,128)(2,1)S(1)} %slice.55), channel_id=1, source_target_pairs={{0,32},{32,0},{64,96},{96,64},{1,33},{33,1},{65,97},{97,65},{2,34}... | collective-permute-start | bytes 1179656 | tf_op jit(solution)/shard_map/ppermute | solution.py:317
  93.9 16.8 %all-to-all-start.1 = ((bf16[16,208,128]{2,1,0:T(8,128)(2,1)}), bf16[16,208,128]{2,1,0:T(8,128)(2,1)S(1)}, u32[]{:S(2)}, u32[]{:S(2)}) async-start(bf16[16,208,128]{2,1,0:T(8,128)(2,1)} %pad_maximum_fusion), calls=%async_computation.1 | async-start | bytes 1703936 | tf_op jit(solution)/shard_map/all_to_all | solution.py:404

commit v3 on v2

--- a/solution.py
+++ b/solution.py
@@ -71,12 +71,12 @@
 ]
 
 
-def distance(x, core, e, second, row):
+def distance(x, core, second, row):
     i = row + lax.broadcasted_iota(jnp.int32, (16, WIDE), 0)
     j = lax.broadcasted_iota(jnp.int32, (16, WIDE), 1)
     lower = jnp.minimum(x, 3 - x)
     i = i + ROWS * lower + jnp.where(i >= ROWS, ROWS * (2 - 2 * lower), 0)
-    return PAIR * e + SUPER * core + i - key_lanes(x, j, second)
+    return SUPER * core + i - key_lanes(x, j, second)
 
 
 def start_of(bounds_ref, pos):
@@ -122,16 +122,16 @@
     for extra in range(1, DEPTH + 2):
         put(count + extra, 0, 0, 0)
     table_ref[0] = jnp.full((TALL, WIDE), LOW, jnp.float32)
-    for index, (low, high, e, second) in enumerate(SLABS):
-        below, inside = edges_of(low, high)
-
-        @pl.loop(0, TALL // 16)
-        def _(step):
-            row = pl.multiple_of(step * 16, 16)
-            d = distance(x, core, e, second, row)
+
+    @pl.loop(0, TALL // 16)
+    def _(step):
+        row = pl.multiple_of(step * 16, 16)
+        near = [distance(x, core, second, row) for second in (False, True)]
+        for index, (low, high, e, second) in enumerate(SLABS):
+            below, inside = edges_of(low, high)
             value = jnp.full((16, WIDE), rab_ref[below[0][1]] * 0.5 if below else LOW, jnp.float32)
             for edge, b in inside:
-                value = jnp.where(d >= edge, rab_ref[b] * 0.5, value)
+                value = jnp.where(near[second] >= edge - PAIR * e, rab_ref[b] * 0.5, value)
             table_ref[index + 1, pl.ds(row, 16), :] = value
 
 
@@ -143,23 +143,24 @@
         v = v[:, :128] + v[:, 128:]
         return v[:8] + v[8:]
 
-    for index, (low, high, e, second) in enumerate(SLABS):
-        below, inside = edges_of(low, high)
-
-        def step(k, carry):
-            row = pl.multiple_of(k * 16, 16)
-            d = distance(x, core, e, second, row)
+    @pl.loop(0, TALL // 16)
+    def _(step):
+        row = pl.multiple_of(step * 16, 16)
+        near = [distance(x, core, second, row) for second in (False, True)]
+        totals = [jnp.zeros((8, 128), jnp.float32)] * NB
+        for index, (low, high, e, second) in enumerate(SLABS):
+            below, inside = edges_of(low, high)
             v = sums_ref[index + 1, pl.ds(row, 16), :]
-            terms = [fold(v)] if below else []
-            terms = terms + [fold(jnp.where(d >= edge, v, 0.0)) for edge, b in inside]
-            return tuple(c + t for c, t in zip(carry, terms))
-
-        found = below + inside
-        zero = jnp.zeros((8, 128), jnp.float32)
-        sums = lax.fori_loop(0, TALL // 16, step, (zero,) * len(found))
-        for k, (edge, b) in enumerate(found):
-            rest = sums[k + 1] if k + 1 < len(found) else zero
-            buckets[b] += sums[k] - rest
+            found = [(b, fold(v)) for edge, b in below]
+            for edge, b in inside:
+                found.append((b, fold(jnp.where(near[second] >= edge - PAIR * e, v, 0.0))))
+            for k, (b, total) in enumerate(found):
+                totals[b] = totals[b] + total
+                if k:
+                    totals[found[k - 1][0]] = totals[found[k - 1][0]] - total
+        for b in range(NB):
+            buckets[b] += totals[b]
+
     lane = lax.broadcasted_iota(jnp.int32, (8, 128), 1)
     row = jnp.zeros((8, 128), jnp.float32)
     for b in range(NB):
@@ -325,7 +326,8 @@
     block = jax.ShapeDtypeStruct((H, ROWS, 128), bf16)
     double = jax.ShapeDtypeStruct((H, 2 * ROWS, 128), bf16)
     slabs = jax.ShapeDtypeStruct((len(SLABS) + 1, TALL, WIDE), f32)
-    params = pltpu.CompilerParams(vmem_limit_bytes=48 * 2**20)
+    small = pltpu.CompilerParams(vmem_limit_bytes=8 * 2**20)
+    large = pltpu.CompilerParams(vmem_limit_bytes=34 * 2**20)
     first_row = (((y * 4 + z) * 2 + core) * 4 + x) * ROWS
     where = jnp.stack([x, core])
     packed, bounds = pl.pallas_call(
@@ -333,7 +335,7 @@
         out_shape=(double, jax.ShapeDtypeStruct((DOCS,), jnp.int32)),
         in_specs=[scalars, whole, whole, whole],
         out_specs=(whole, scalars),
-        compiler_params=params,
+        compiler_params=small,
         name="pack",
     )(first_row.reshape(1), doc_ids.reshape(96, 128), qkv.transpose(1, 0, 2), grad_out)
     own = lax.all_to_all(packed, ("y", "z"), 0, 0, tiled=True)
@@ -341,17 +343,18 @@
     kv_x = swap(kv_own, "x", (1, 0, 3, 2))
     qg_x = swap(qg_own, "x", (3, 2, 1, 0))
     kv_core = swap(kv_own, "core", (1, 0))
-    kv_both = swap(kv_x, "core", (1, 0))
     table_row = lax.dynamic_slice_in_dim(rab, y * 4 + z, 1, 0)[0]
     table, plan = pl.pallas_call(
         table_kernel,
         out_shape=(slabs, jax.ShapeDtypeStruct((3 * SLOTS + 1,), jnp.int32)),
         in_specs=[scalars] * 3,
         out_specs=(whole, scalars),
-        compiler_params=params,
-        cost_estimate=pl.CostEstimate(flops=10**7, bytes_accessed=3 * 10**6, transcendentals=0),
+        compiler_params=small,
+        cost_estimate=pl.CostEstimate(flops=0, bytes_accessed=0, transcendentals=0),
         name="table",
     )(where, table_row, bounds)
+    kv_x, qg_x, table, plan = lax.optimization_barrier((kv_x, qg_x, table, plan))
+    kv_both = swap(kv_x, "core", (1, 0))
     keep, give, mine, theirs, sums = pl.pallas_call(
         main_kernel,
         out_shape=[double, double, jax.ShapeDtypeStruct((H, ROWS, 128), f32), block, slabs],
@@ -369,24 +372,24 @@
         ]
         + [VMEM((2 * TALL, WIDE), f32)] * DEPTH
         + [VMEM((2 * TALL, WIDE), bf16)] * DEPTH,
-        compiler_params=params,
+        compiler_params=large,
         name="attend",
     )(where, bounds, plan, table, own, kv_x, kv_core, kv_both, qg_x)
     got = swap(give, "core", (1, 0))
+    dkv = keep.astype(f32) + got.astype(f32)
+    dkv_x = dkv[:, ROWS:].astype(bf16)
     got_qo = swap(theirs, "x", (3, 2, 1, 0))
+    got_dkv = swap(dkv_x, "x", (1, 0, 3, 2))
     bias = pl.pallas_call(
         buckets_kernel,
         out_shape=jax.ShapeDtypeStruct((8, 128), f32),
         in_specs=[scalars, whole],
         out_specs=whole,
         scratch_shapes=[VMEM((NB, 8, 128), f32)],
-        compiler_params=params,
-        cost_estimate=pl.CostEstimate(flops=10**7, bytes_accessed=3 * 10**6, transcendentals=0),
+        compiler_params=small,
+        cost_estimate=pl.CostEstimate(flops=0, bytes_accessed=0, transcendentals=0),
         name="buckets",
     )(where, sums)
-    dkv = keep.astype(f32) + got.astype(f32)
-    got_dkv = swap(dkv[:, ROWS:].astype(bf16), "x", (1, 0, 3, 2))
-    bias = bias + swap(bias, "core", (1, 0))
     bias = bias + sum(swap(bias, "x", p) for p in ((1, 0, 3, 2), (3, 2, 1, 0), (2, 3, 0, 1)))
     bias = bias[0]
     hi = lax.reduce_precision(bias, 8, 7)
@@ -404,6 +407,7 @@
     results = lax.all_to_all(results, ("y", "z"), 0, 0, tiled=True)
     terms = lax.dynamic_slice(results, (x * 4, 2 * ROWS, 0), (4, 3, NB)).astype(f32)
     bias_grad = terms[:, 0] + terms[:, 1] + terms[:, 2]
+    bias_grad = bias_grad + swap(bias_grad, "core", (1, 0))
     out, grad_qkv = pl.pallas_call(
         unpack_kernel,
         out_shape=(
@@ -412,7 +416,7 @@
         ),
         in_specs=[whole],
         out_specs=(whole, whole),
-        compiler_params=params,
+        compiler_params=small,
         name="unpack",
     )(results)
     return out, grad_qkv.transpose(1, 0, 2), bias_grad

time: 113 us -> 105 us (0.929)
  the two profiles are of different devices: /device:TPU:0 before, /device:TPU:1 now
where the time goes in v3:
time: 105 us; the launch traced here: 104 us
  Pallas kernels  31.2 us (30%)
  waiting for transfers between devices  25.3 us (24%)
  blocking collectives  21.8 us (21%)
  starting transfers between devices  19.8 us (19%)
  local copies, waits for them, and re-layouts  2.91 us (3%)
  other arithmetic  2.03 us (2%)
    pallas_call x1, Pallas kernels, per_device(): pl.pallas_call(main_kernel, out_shape=[double, double, jax.ShapeDtypeStru...  23.3 us
    all_to_all x1, blocking collectives, per_device(): own = lax.all_to_all(packed, ('y', 'z'), 0, 0, tiled=True)  21.8 us
    ppermute x11, starting transfers between devices, swap(): return lax.ppermute(v, axis, [(i, p) for i, p in enumerate(partner)])  16.1 us
    ppermute x11, waiting for transfers between devices, swap(): return lax.ppermute(v, axis, [(i, p) for i, p in enumerate(partner)])  12.7 us
    all_to_all x1, waiting for transfers between devices, per_device(): results = lax.all_to_all(results, ('y', 'z'), 0, 0, tiled=True)  12.5 us
    all_to_all x1, starting transfers between devices, per_device(): results = lax.all_to_all(results, ('y', 'z'), 0, 0, tiled=True)  3.62 us
    pallas_call x1, Pallas kernels, per_device(): pl.pallas_call(table_kernel, out_shape=(slabs, jax.ShapeDtypeStruct((3 *...  3.52 us
    unnamed x8, local copies, waits for them, and re-layouts  2.79 us
  transfers between devices with their start and end apart: 12, of which 8 were waited for; matrix products, arithmetic and copies ran while one was open for 0% of the time, Pallas kernels for 7%

profile of v3, /device:TPU:1, one launch (start us, length us, event | category | flops | bytes accessed | tf_op | source)
XLA Modules:
  0.0 103.7 jit_solution(13456987740259844889)
XLA Ops:
  0.6 0.0 copy-start
  0.7 0.0 copy-start.1
  0.7 1.1 %copy-done.1 = bf16[96,3,1024]{2,0,1:T(8,128)(2,1)S(1)} copy-done((bf16[96,3,1024]{2,0,1:T(8,128)(2,1)S(1)}, bf16[96,3,1024]{2,0,1:T(8,128)(2,1)}, u32[]{:S(2)}) %copy-start.1) | copy-done | bytes 589848
  1.7 0.0 copy-start.2
  1.7 0.9 copy-done.2
  2.7 0.0 copy-start.3
  2.7 0.8 copy-done.3
  3.5 0.8 pack.1
  4.2 21.8 %all_to_all.10.own_ref = bf16[16,192,128]{2,1,0:T(8,128)(2,1)S(1)} all-to-all(bf16[16,192,128]{2,1,0:T(8,128)(2,1)S(1)} %get-tuple-element.19), channel_id=1, replica_groups=mesh['x'=4,'y'=4,'z'=4,'core'=2] {'y','z'}, dimensions={0} | all-to-all | bytes 1572864 | tf_op jit(solution)/shard_map/all_to_all | solution.py:341
  26.0 0.1 fusion.7
  26.1 2.6 %collective-permute-start.1 = (bf16[16,96,128]{2,1,0:T(8,128)(2,1)S(1)}, bf16[16,96,128]{2,1,0:T(8,128)(2,1)S(1)}, u32[]{:S(2)}, u32[]{:S(2)}) collective-permute-start(bf16[16,96,128]{2,1,0:T(8,128)(2,1)S(1)} %get-tuple-element.33), channel_id=1, source_target_pairs={{0,96},{32,64},{64,32},{96,0},{1,97},{33,65},{65,33},{97,1},{2,98}... | collective-permute-start | bytes 1179656 | tf_op jit(solution)/shard_map/ppermute | solution.py:318
  28.6 0.0 collective-permute-start
  28.6 0.1 pad_add_fusion.where_ref
  28.7 0.0 copy-done
  28.7 3.5 %table.1 = (f32[20,192,256]{2,1,0:T(8,128)S(1)}, s32[769]{0:T(1024)S(1)}) custom-call(s32[2]{0:T(128)S(1)} %pad_add_fusion.where_ref, f32[20]{0:T(128)S(1)} %dynamic-slice_bitcast_fusion.rab_ref, s32[8]{0:T(128)S(1)} %get-tuple-element.18.bounds_ref), custom_call_target="tpu_custom_call" | custom-call | tf_op jit(solution)/shard_map/table/pallas_call | solution.py:347
  32.2 2.3 %collective-permute-start.2 = (bf16[16,96,128]{2,1,0:T(8,128)(2,1)S(1)}, bf16[16,96,128]{2,1,0:T(8,128)(2,1)S(1)}, u32[]{:S(2)}, u32[]{:S(2)}) collective-permute-start(bf16[16,96,128]{2,1,0:T(8,128)(2,1)S(1)} %get-tuple-element.34), channel_id=1, source_target_pairs={{0,1},{1,0},{2,3},{3,2},{4,5},{5,4},{6,7},{7,6},{8,9},{9,8},{10,11... | collective-permute-start | bytes 1179656 | tf_op jit(solution)/shard_map/ppermute | solution.py:318
  34.5 1.7 %collective-permute-done.1.qgx_ref = bf16[16,96,128]{2,1,0:T(8,128)(2,1)S(1)} collective-permute-done((bf16[16,96,128]{2,1,0:T(8,128)(2,1)S(1)}, bf16[16,96,128]{2,1,0:T(8,128)(2,1)S(1)}, u32[]{:S(2)}, u32[]{:S(2)}) %collective-permute-start.1) | collective-permute-done | bytes 393248 | tf_op jit(solution)/shard_map/ppermute | solution.py:318
  36.2 1.0 collective-permute-done.kvx_ref
  37.2 2.9 %collective-permute-start.3 = (bf16[16,96,128]{2,1,0:T(8,128)(2,1)S(1)}, bf16[16,96,128]{2,1,0:T(8,128)(2,1)S(1)}, u32[]{:S(2)}, u32[]{:S(2)}) collective-permute-start(bf16[16,96,128]{2,1,0:T(8,128)(2,1)S(1)} %collective-permute-done.kvx_ref), channel_id=1, source_target_pairs={{0,1},{1,0},{2,3},{3,2},{4,5},{5,4},{6,7},{7,6},{8,9},{9,8},{10,11... | collective-permute-start | bytes 1179656 | tf_op jit(solution)/shard_map/ppermute | solution.py:318
  40.1 0.0 collective-permute-done.2.kvc_ref
  40.1 1.3 %collective-permute-done.3.kvxc_ref = bf16[16,96,128]{2,1,0:T(8,128)(2,1)S(1)} collective-permute-done((bf16[16,96,128]{2,1,0:T(8,128)(2,1)S(1)}, bf16[16,96,128]{2,1,0:T(8,128)(2,1)S(1)}, u32[]{:S(2)}, u32[]{:S(2)}) %collective-permute-start.3) | collective-permute-done | bytes 393248 | tf_op jit(solution)/shard_map/ppermute | solution.py:318
  41.5 23.3 %attend.1 = (bf16[16,192,128]{2,1,0:T(8,128)(2,1)S(1)}, bf16[16,192,128]{2,1,0:T(8,128)(2,1)S(1)}, f32[16,96,128]{2,1,0:T(8,128)S(1)}, bf16[16,96,128]{2,1,0:T(8,128)(2,1)S(1)}, f32[20,192,256]{2,1,0:T(8,128)S(1)}) custom-call(s32[2]{0:T(128)S(1)} %pad_add_fusion.where_ref, s32[8]{0:T(128)S(1)} %get-tuple-element.18.bounds_ref, ...), custom_call_target="tpu_custom_call" | custom-call | tf_op jit(solution)/shard_map/attend/pallas_call | solution.py:358
  64.8 0.1 collective-permute-start.5
  64.9 2.4 %buckets.1 = f32[8,128]{1,0:T(8,128)S(1)} custom-call(s32[2]{0:T(128)S(1)} %pad_add_fusion.where_ref, f32[20,192,256]{2,1,0:T(8,128)S(1)} %get-tuple-element.30.sums_ref), custom_call_target="tpu_custom_call" | custom-call | tf_op jit(solution)/shard_map/buckets/pallas_call | solution.py:383
  67.3 0.1 collective-permute-start.9
  67.4 1.5 %collective-permute-start.8 = (f32[8,128]{1,0:T(8,128)S(1)}, f32[8,128]{1,0:T(8,128)S(1)}, u32[]{:S(2)}, u32[]{:S(2)}) collective-permute-start(f32[8,128]{1,0:T(8,128)S(1)} %buckets.1), channel_id=1, source_target_pairs={{0,96},{32,64},{64,32},{96,0},{1,97},{33,65},{65,33},{97,1},{2,98}... | collective-permute-start | bytes 12296 | tf_op jit(solution)/shard_map/ppermute | solution.py:318
  68.9 1.1 %collective-permute-start.7 = (f32[8,128]{1,0:T(8,128)S(1)}, f32[8,128]{1,0:T(8,128)S(1)}, u32[]{:S(2)}, u32[]{:S(2)}) collective-permute-start(f32[8,128]{1,0:T(8,128)S(1)} %buckets.1), channel_id=1, source_target_pairs={{0,32},{32,0},{64,96},{96,64},{1,33},{33,1},{65,97},{97,65},{2,34}... | collective-permute-start | bytes 12296 | tf_op jit(solution)/shard_map/ppermute | solution.py:318
  70.1 1.2 %collective-permute-start.4 = (bf16[16,96,128]{2,1,0:T(8,128)(2,1)S(1)}, bf16[16,96,128]{2,1,0:T(8,128)(2,1)S(1)}, u32[]{:S(2)}, u32[]{:S(2)}) collective-permute-start(bf16[16,96,128]{2,1,0:T(8,128)(2,1)S(1)} %get-tuple-element.27), channel_id=1, source_target_pairs={{0,96},{32,64},{64,32},{96,0},{1,97},{33,65},{65,33},{97,1},{2,98}... | collective-permute-start | bytes 1179656 | tf_op jit(solution)/shard_map/ppermute | solution.py:318
  71.3 0.1 collective-permute-done.9
  71.4 0.0 collective-permute-done.8
  71.4 0.3 collective-permute-done.7
  71.7 0.0 collective-permute-done.5
  71.7 0.2 convert_add_fusion
  71.9 0.1 slice.55
  71.9 0.9 collective-permute-start.6
  72.9 7.7 %collective-permute-done.4 = bf16[16,96,128]{2,1,0:T(8,128)(2,1)S(1)} collective-permute-done((bf16[16,96,128]{2,1,0:T(8,128)(2,1)S(1)}, bf16[16,96,128]{2,1,0:T(8,128)(2,1)S(1)}, u32[]{:S(2)}, u32[]{:S(2)}) %collective-permute-start.4) | collective-permute-done | bytes 393248 | tf_op jit(solution)/shard_map/ppermute | solution.py:318
  80.5 0.1 add_convert_fusion
  80.6 0.6 collective-permute-done.6
  81.2 0.1 fusion
  81.3 1.0 pad_maximum_fusion
  82.3 3.6 %all-to-all-start.1 = ((bf16[16,208,128]{2,1,0:T(8,128)(2,1)}), bf16[16,208,128]{2,1,0:T(8,128)(2,1)S(1)}, u32[]{:S(2)}, u32[]{:S(2)}) async-start(bf16[16,208,128]{2,1,0:T(8,128)(2,1)} %pad_maximum_fusion), calls=%async_computation.1 | async-start | bytes 1703936 | tf_op jit(solution)/shard_map/all_to_all | solution.py:407
  85.9 12.5 %all-to-all-done.1.in_ref = bf16[16,208,128]{2,1,0:T(8,128)(2,1)S(1)} async-done(((bf16[16,208,128]{2,1,0:T(8,128)(2,1)}), bf16[16,208,128]{2,1,0:T(8,128)(2,1)S(1)}, u32[]{:S(2)}, u32[]{:S(2)}) %all-to-all-start.1) | async-done | bytes 852000 | tf_op jit(solution)/shard_map/all_to_all | solution.py:407
  98.5 3.5 %collective-permute-start.10 = (f32[4,20]{1,0:T(4,128)S(1)}, f32[4,20]{1,0:T(4,128)S(1)}, u32[]{:S(2)}, u32[]{:S(2)}) collective-permute-start(f32[4,20]{1,0:T(4,128)S(1)} %bitcast.11), channel_id=1, source_target_pairs={{0,1},{1,0},{2,3},{3,2},{4,5},{5,4},{6,7},{7,6},{8,9},{9,8},{10,11... | collective-permute-start | bytes 968 | tf_op jit(solution)/shard_map/ppermute | solution.py:318
  101.9 1.2 %unpack.1 = (bf16[96,1024]{1,0:T(8,128)(2,1)}, bf16[3,96,1024]{2,1,0:T(8,128)(2,1)}) custom-call(bf16[16,208,128]{2,1,0:T(8,128)(2,1)S(1)} %all-to-all-done.1.in_ref), custom_call_target="tpu_custom_call" | custom-call | tf_op jit(solution)/shard_map/unpack/pallas_call | solution.py:411
  103.1 0.0 collective-permute-done.10
  103.1 0.6 add.63
  (7 shorter events, 0.1 us)
Async XLA Ops:
  0.6 28.1 %copy-start = (f32[16,20]{1,0:T(8,128)S(1)}, f32[16,20]{1,0:T(8,128)}, u32[]{:S(2)}) copy-start(f32[16,20]{1,0:T(8,128)} %param.6) | copy-start | bytes 3844
  0.7 1.1 %copy-start.1 = (bf16[96,3,1024]{2,0,1:T(8,128)(2,1)S(1)}, bf16[96,3,1024]{2,0,1:T(8,128)(2,1)}, u32[]{:S(2)}) copy-start(bf16[96,3,1024]{2,0,1:T(8,128)(2,1)} %param.4) | copy-start | bytes 1769476
  1.7 0.9 copy-start.2
  2.7 0.8 copy-start.3
  26.1 10.2 %collective-permute-start.1 = (bf16[16,96,128]{2,1,0:T(8,128)(2,1)S(1)}, bf16[16,96,128]{2,1,0:T(8,128)(2,1)S(1)}, u32[]{:S(2)}, u32[]{:S(2)}) collective-permute-start(bf16[16,96,128]{2,1,0:T(8,128)(2,1)S(1)} %get-tuple-element.33), channel_id=1, source_target_pairs={{0,96},{32,64},{64,32},{96,0},{1,97},{33,65},{65,33},{97,1},{2,98}... | collective-permute-start | bytes 1179656 | tf_op jit(solution)/shard_map/ppermute | solution.py:318
  28.6 8.6 %collective-permute-start = (bf16[16,96,128]{2,1,0:T(8,128)(2,1)S(1)}, bf16[16,96,128]{2,1,0:T(8,128)(2,1)S(1)}, u32[]{:S(2)}, u32[]{:S(2)}) collective-permute-start(bf16[16,96,128]{2,1,0:T(8,128)(2,1)S(1)} %get-tuple-element.34), channel_id=1, source_target_pairs={{0,32},{32,0},{64,96},{96,64},{1,33},{33,1},{65,97},{97,65},{2,34}... | collective-permute-start | bytes 1179656 | tf_op jit(solution)/shard_map/ppermute | solution.py:318
  32.2 7.9 %collective-permute-start.2 = (bf16[16,96,128]{2,1,0:T(8,128)(2,1)S(1)}, bf16[16,96,128]{2,1,0:T(8,128)(2,1)S(1)}, u32[]{:S(2)}, u32[]{:S(2)}) collective-permute-start(bf16[16,96,128]{2,1,0:T(8,128)(2,1)S(1)} %get-tuple-element.34), channel_id=1, source_target_pairs={{0,1},{1,0},{2,3},{3,2},{4,5},{5,4},{6,7},{7,6},{8,9},{9,8},{10,11... | collective-permute-start | bytes 1179656 | tf_op jit(solution)/shard_map/ppermute | solution.py:318
  37.2 4.3 %collective-permute-start.3 = (bf16[16,96,128]{2,1,0:T(8,128)(2,1)S(1)}, bf16[16,96,128]{2,1,0:T(8,128)(2,1)S(1)}, u32[]{:S(2)}, u32[]{:S(2)}) collective-permute-start(bf16[16,96,128]{2,1,0:T(8,128)(2,1)S(1)} %collective-permute-done.kvx_ref), channel_id=1, source_target_pairs={{0,1},{1,0},{2,3},{3,2},{4,5},{5,4},{6,7},{7,6},{8,9},{9,8},{10,11... | collective-permute-start | bytes 1179656 | tf_op jit(solution)/shard_map/ppermute | solution.py:318
  64.8 6.9 %collective-permute-start.5 = (bf16[16,192,128]{2,1,0:T(8,128)(2,1)S(1)}, bf16[16,192,128]{2,1,0:T(8,128)(2,1)S(1)}, u32[]{:S(2)}, u32[]{:S(2)}) collective-permute-start(bf16[16,192,128]{2,1,0:T(8,128)(2,1)S(1)} %get-tuple-element.29), channel_id=1, source_target_pairs={{0,1},{1,0},{2,3},{3,2},{4,5},{5,4},{6,7},{7,6},{8,9},{9,8},{10,11... | collective-permute-start | bytes 2359304 | tf_op jit(solution)/shard_map/ppermute | solution.py:318
  67.3 4.0 %collective-permute-start.9 = (f32[8,128]{1,0:T(8,128)S(1)}, f32[8,128]{1,0:T(8,128)S(1)}, u32[]{:S(2)}, u32[]{:S(2)}) collective-permute-start(f32[8,128]{1,0:T(8,128)S(1)} %buckets.1), channel_id=1, source_target_pairs={{0,64},{32,96},{64,0},{96,32},{1,65},{33,97},{65,1},{97,33},{2,66}... | collective-permute-start | bytes 12296 | tf_op jit(solution)/shard_map/ppermute | solution.py:318
  67.4 4.0 %collective-permute-start.8 = (f32[8,128]{1,0:T(8,128)S(1)}, f32[8,128]{1,0:T(8,128)S(1)}, u32[]{:S(2)}, u32[]{:S(2)}) collective-permute-start(f32[8,128]{1,0:T(8,128)S(1)} %buckets.1), channel_id=1, source_target_pairs={{0,96},{32,64},{64,32},{96,0},{1,97},{33,65},{65,33},{97,1},{2,98}... | collective-permute-start | bytes 12296 | tf_op jit(solution)/shard_map/ppermute | solution.py:318
  68.9 2.8 %collective-permute-start.7 = (f32[8,128]{1,0:T(8,128)S(1)}, f32[8,128]{1,0:T(8,128)S(1)}, u32[]{:S(2)}, u32[]{:S(2)}) collective-permute-start(f32[8,128]{1,0:T(8,128)S(1)} %buckets.1), channel_id=1, source_target_pairs={{0,32},{32,0},{64,96},{96,64},{1,33},{33,1},{65,97},{97,65},{2,34}... | collective-permute-start | bytes 12296 | tf_op jit(solution)/shard_map/ppermute | solution.py:318
  70.1 10.5 %collective-permute-start.4 = (bf16[16,96,128]{2,1,0:T(8,128)(2,1)S(1)}, bf16[16,96,128]{2,1,0:T(8,128)(2,1)S(1)}, u32[]{:S(2)}, u32[]{:S(2)}) collective-permute-start(bf16[16,96,128]{2,1,0:T(8,128)(2,1)S(1)} %get-tuple-element.27), channel_id=1, source_target_pairs={{0,96},{32,64},{64,32},{96,0},{1,97},{33,65},{65,33},{97,1},{2,98}... | collective-permute-start | bytes 1179656 | tf_op jit(solution)/shard_map/ppermute | solution.py:318
  71.9 9.3 %collective-permute-start.6 = (bf16[16,96,128]{2,1,0:T(8,128)(2,1)S(1)}, bf16[16,96,128]{2,1,0:T(8,128)(2,1)S(1)}, u32[]{:S(2)}, u32[]{:S(2)}) collective-permute-start(bf16[16,96,128]{2,1,0:T(8,128)(2,1)S(1)} %slice.55), channel_id=1, source_target_pairs={{0,32},{32,0},{64,96},{96,64},{1,33},{33,1},{65,97},{97,65},{2,34}... | collective-permute-start | bytes 1179656 | tf_op jit(solution)/shard_map/ppermute | solution.py:318
  82.3 16.2 %all-to-all-start.1 = ((bf16[16,208,128]{2,1,0:T(8,128)(2,1)}), bf16[16,208,128]{2,1,0:T(8,128)(2,1)S(1)}, u32[]{:S(2)}, u32[]{:S(2)}) async-start(bf16[16,208,128]{2,1,0:T(8,128)(2,1)} %pad_maximum_fusion), calls=%async_computation.1 | async-start | bytes 1703936 | tf_op jit(solution)/shard_map/all_to_all | solution.py:407
  98.5 4.6 %collective-permute-start.10 = (f32[4,20]{1,0:T(4,128)S(1)}, f32[4,20]{1,0:T(4,128)S(1)}, u32[]{:S(2)}, u32[]{:S(2)}) collective-permute-start(f32[4,20]{1,0:T(4,128)S(1)} %bitcast.11), channel_id=1, source_target_pairs={{0,1},{1,0},{2,3},{3,2},{4,5},{5,4},{6,7},{7,6},{8,9},{9,8},{10,11... | collective-permute-start | bytes 968 | tf_op jit(solution)/shard_map/ppermute | solution.py:318

commit v4 on v3

v4 whole, which is shorter than its diff:
```python
import jax
import jax.numpy as jnp
from jax import lax
from jax.experimental import pallas as pl
from jax.experimental.pallas import tpu as pltpu
from jax.sharding import Mesh
from jax.sharding import PartitionSpec as P

HD = 64
H = 16
NB = 20
DOCS = 8
ROWS = 96
SUPER = 384
GROUPS = 16
PAIR = 768
TALL = 192
WIDE = 256
CHUNK = 128
SLOTS = 256
DEPTH = 6
LOW = -1e30
VMEM = pltpu.VMEM
SMEM = pltpu.SMEM
NT = (((1,), (1,)), ((), ()))


def doc_bounds(ids):
    return [jnp.int32(0)] + [
        jnp.sum((ids < d).astype(jnp.float32)).astype(jnp.int32) for d in range(1, DOCS)
    ]


def pack_kernel(where_ref, ids, qkv, g_in, out_ref, bounds_ref, ids_ref, qkv_ref, g_ref, sems):
    copies = [
        pltpu.make_async_copy(source, target, sems.at[k])
        for k, (source, target) in enumerate(((ids, ids_ref), (qkv, qkv_ref), (g_in, g_ref)))
    ]
    for copy in copies:
        copy.start()
    copies[0].wait()
    bounds = doc_bounds(ids_ref[...])
    for d in range(DOCS):
        bounds_ref[d] = bounds[d]
    pos = where_ref[0] + lax.broadcasted_iota(jnp.int32, (ROWS, 128), 0)
    length = jnp.zeros((ROWS, 128), jnp.int32)
    ends = bounds[1:] + [jnp.int32(PAIR * GROUPS)]
    for d in range(DOCS):
        length = jnp.where(pos >= bounds[d], ends[d] - bounds[d], length)
    scale = lax.rsqrt(length.astype(jnp.float32))[:, :HD]
    copies[1].wait()
    copies[2].wait()
    for h in range(H):
        cols = slice(h * HD, (h + 1) * HD)
        out_ref[h, :ROWS] = jnp.concatenate([qkv_ref[1, :, cols], qkv_ref[2, :, cols]], axis=1)
        q = (qkv_ref[0, :, cols].astype(jnp.float32) * 0.0625).astype(jnp.bfloat16)
        g = (g_ref[:, cols].astype(jnp.float32) * scale).astype(jnp.bfloat16)
        out_ref[h, ROWS:] = jnp.concatenate([q, g], axis=1)


EDGES = [(k, k) for k in range(8)] + [(2**p, p + 6) for p in range(3, 13)]


def edges_of(low, high):
    below = [edge for edge in EDGES if edge[0] <= low]
    return below[-1:], [edge for edge in EDGES if low < edge[0] <= high]


def key_place(x, c, lane):
    j = CHUNK * c + lane
    return j + 2 * ROWS * lax.div(x, 2) + jnp.where(j >= 2 * ROWS, SUPER - 2 * ROWS, 0)


SLABS = [
    (c, e, PAIR * e - (319, 639, 767)[c], PAIR * e + PAIR - 1 - (0, 128, 448)[c])
    for c in range(3)
    for e in range(9)
]


def distance(x, core, c, row):
    i = row + lax.broadcasted_iota(jnp.int32, (16, CHUNK), 0)
    lane = lax.broadcasted_iota(jnp.int32, (16, CHUNK), 1)
    lower = jnp.minimum(x, 3 - x)
    i = i + ROWS * lower + jnp.where(i >= ROWS, ROWS * (2 - 2 * lower), 0)
    return SUPER * core + i - key_place(x, c, lane)


def start_of(bounds_ref, pos):
    start = jnp.int32(0)
    for d in range(1, DOCS):
        start = jnp.where(pos >= bounds_ref[d], bounds_ref[d], start)
    return start


def span_of(x, core, g):
    lower = jnp.minimum(x, 3 - x)
    base = PAIR * g + SUPER * core
    return base + ROWS * lower, base + ROWS * (4 - lower) - 1


def table_kernel(where_ref, rab_ref, bounds_ref, table_ref, starts_ref, scales_ref, plan_ref):
    x, core = where_ref[0], where_ref[1]
    column = 2 * ROWS * lax.div(x, 2)

    def of_group(g, at):
        first, last = span_of(x, core, g)
        begin = start_of(bounds_ref, first)

        def of_pair(n, at):
            for c, (low, high) in enumerate(((0, 127), (128, 447), (448, 575))):
                place = PAIR * n + column
                live = (place + high >= begin) & (place + low <= last)
                plan_ref[lax.div(at, 2)] = g
                plan_ref[SLOTS + at] = 3 * n + c
                plan_ref[3 * SLOTS + at] = 9 * c + g - n + 1
                at = at + live.astype(jnp.int32)
            return at

        at = lax.fori_loop(lax.div(begin, PAIR), g + 1, of_pair, at)
        plan_ref[SLOTS + at] = 0
        plan_ref[3 * SLOTS + at] = 0
        return at + lax.rem(at, 2)

    at = lax.fori_loop(0, GROUPS, of_group, jnp.int32(2))
    tiles = lax.div(at, 2)
    plan_ref[5 * SLOTS] = tiles - 1
    plan_ref[0] = 0
    for extra in range(DEPTH + 1):
        plan_ref[tiles + extra] = 0
    for half in range(2):
        plan_ref[SLOTS + half] = 0
        plan_ref[3 * SLOTS + half] = 0
        for extra in range(DEPTH + 1):
            plan_ref[SLOTS + at + 2 * extra + half] = 0
            plan_ref[3 * SLOTS + at + 2 * extra + half] = 0

    table_ref[0] = jnp.full((TALL, CHUNK), LOW, jnp.float32)

    @pl.loop(0, TALL // 16)
    def _(step):
        row = pl.multiple_of(step * 16, 16)
        near = [distance(x, core, c, row) for c in range(3)]
        for index, (c, e, low, high) in enumerate(SLABS):
            below, inside = edges_of(low, high)
            value = jnp.full((16, CHUNK), rab_ref[below[0][1]] * 0.5 if below else LOW, jnp.float32)
            for edge, b in inside:
                value = jnp.where(near[c] >= edge - PAIR * e, rab_ref[b] * 0.5, value)
            table_ref[index + 1, pl.ds(row, 16), :] = value

    left = lax.broadcasted_iota(jnp.int32, (TALL, 128), 1) < HD
    row = lax.broadcasted_iota(jnp.int32, (TALL, 128), 0)
    offset = row + jnp.where(row >= ROWS, ROWS * (2 - 2 * jnp.minimum(x, 3 - x)), 0)

    @pl.loop(0, GROUPS)
    def _(g):
        first, last = span_of(x, core, g)
        pos = first + offset
        d_first, d_last = jnp.int32(0), jnp.int32(0)
        for d in range(1, DOCS):
            d_first = d_first + (first >= bounds_ref[d]).astype(jnp.int32)
            d_last = d_last + (last >= bounds_ref[d]).astype(jnp.int32)
        starts_ref[g] = jnp.zeros((TALL, 128), jnp.int32)
        scales_ref[g] = jnp.zeros((TALL, 128), jnp.float32)

        def history(d, carry):
            begin = bounds_ref[d]
            end = jnp.where(d + 1 < DOCS, bounds_ref[jnp.minimum(d + 1, DOCS - 1)], PAIR * GROUPS)
            inside = pos >= begin
            size = jnp.full((TALL, 128), end - begin, jnp.int32).astype(jnp.float32)
            starts_ref[g] = jnp.where(inside, begin, starts_ref[g])
            scales_ref[g] = jnp.where(
                left, 0.0625, jnp.where(inside, lax.rsqrt(size), scales_ref[g])
            )
            return carry

        lax.fori_loop(d_first, d_last + 1, history, 0)


def buckets_kernel(where_ref, sums_ref, bias_ref, buckets):
    x, core = where_ref[0], where_ref[1]
    buckets[...] = jnp.zeros((NB, 8, 128), jnp.float32)

    @pl.loop(0, TALL // 16)
    def _(step):
        row = pl.multiple_of(step * 16, 16)
        near = [distance(x, core, c, row) for c in range(3)]
        totals = [jnp.zeros((8, 128), jnp.float32)] * NB
        for index, (c, e, low, high) in enumerate(SLABS):
            below, inside = edges_of(low, high)
            v = sums_ref[index + 1, pl.ds(row, 16), :]
            found = [(b, v[:8] + v[8:]) for edge, b in below]
            for edge, b in inside:
                part = jnp.where(near[c] >= edge - PAIR * e, v, 0.0)
                found.append((b, part[:8] + part[8:]))
            for k, (b, total) in enumerate(found):
                totals[b] = totals[b] + total
                if k:
                    totals[found[k - 1][0]] = totals[found[k - 1][0]] - total
        for b in range(NB):
            buckets[b] += totals[b]

    lane = lax.broadcasted_iota(jnp.int32, (8, 128), 1)
    row = jnp.zeros((8, 128), jnp.float32)
    for b in range(NB):
        total = jnp.sum(jnp.sum(buckets[b], axis=0, keepdims=True), axis=1, keepdims=True)
        row = jnp.where(lane == b, total * 0.5, row)
    bias_ref[...] = row


def main_kernel(
    where_ref, plan_ref, table, starts, scales, own_ref, kvx_ref, kvc_ref, kvxc_ref, qgx_ref,
    keep_ref, give_ref, mine_ref, theirs_ref, biasacc,
    line, dkv, acc, lhs, qgt, *stages,
):
    x = where_ref[0]
    core = where_ref[1]
    odd = lax.rem(x, 2)
    lower = jnp.minimum(x, 3 - x)

    def aligned(v):
        return pl.multiple_of(v * ROWS, ROWS)

    k_own = aligned(2 * core + odd)
    k_x = aligned(2 * core + 1 - odd)
    k_core = aligned(2 * (1 - core) + odd)
    k_both = aligned(2 * (1 - core) + 1 - odd)
    q_own = aligned((x != lower).astype(jnp.int32))
    q_x = aligned((x == lower).astype(jnp.int32))
    lane = lax.broadcasted_iota(jnp.int32, (TALL, 128), 1)
    left = lane < HD

    def chunk(k):
        return pl.ds(pl.multiple_of(CHUNK * k, CHUNK), CHUNK)

    def block(n, at):
        return pl.ds(pl.multiple_of(SUPER * n + at, ROWS), ROWS)

    @pl.loop(0, GROUPS)
    def _(n):
        line[block(n, k_own), :] = own_ref[n, :ROWS]
        line[block(n, k_x), :] = kvx_ref[n]
        line[block(n, k_core), :] = kvc_ref[n]
        line[block(n, k_both), :] = kvxc_ref[n]
        for c in range(3):
            dkv[3 * n + c] = jnp.zeros((128, CHUNK), jnp.float32)
        acc[n] = jnp.zeros((TALL, 128), jnp.float32)
        zero = jnp.zeros((ROWS, 128), jnp.bfloat16)
        for at, qg in ((q_own, own_ref[n, ROWS:]), (q_x, qgx_ref[n])):
            lhs[n, pl.ds(at, ROWS), :] = jnp.where(left[:ROWS], qg, zero)
            lhs[n, pl.ds(pl.multiple_of(at + TALL, ROWS), ROWS), :] = jnp.where(left[:ROWS], zero, qg)
        qgt[n] = (lhs[n, pl.ds(0, TALL), :] + lhs[n, pl.ds(TALL, TALL), :]).T

    @pl.loop(0, len(SLABS) + 1)
    def _(e):
        biasacc[e] = jnp.zeros((TALL, CHUNK), jnp.float32)

    score, weight = stages[:DEPTH], stages[DEPTH:]
    weight[0][...] = jnp.zeros((2 * TALL, WIDE), jnp.bfloat16)
    lanes = lax.broadcasted_iota(jnp.int32, (1, CHUNK), 1)
    places = [key_place(x, c, lanes) for c in range(3)]
    halves = (slice(0, CHUNK), slice(CHUNK, WIDE))

    def entry(k):
        chunks = [plan_ref[SLOTS + 2 * k + half] for half in range(2)]
        slabs = [plan_ref[3 * SLOTS + 2 * k + half] for half in range(2)]
        return plan_ref[k], chunks, slabs

    def scores(k, s):
        g, chunks, slabs = entry(k)
        for cols, n in zip(halves, chunks):
            s[:, cols] = lax.dot_general(
                lhs[g], line[chunk(n), :], NT, preferred_element_type=jnp.float32
            )

    def weigh(k, s, w_out):
        g, chunks, slabs = entry(k)
        for cols, n, e in zip(halves, chunks, slabs):
            pair = lax.div(n, 3)
            c = n - 3 * pair
            key = PAIR * pair + jnp.where(c == 0, places[0], jnp.where(c == 1, places[1], places[2]))
            half = s[pl.ds(0, TALL), cols] + table[e]
            half = jnp.where(key >= starts[g], half, LOW)
            t = jnp.tanh(half)
            u = 1.0 + t
            w = half * u
            ds = s[pl.ds(TALL, TALL), cols] * (u + w * (1.0 - t))
            biasacc[e] += ds
            w_out[pl.ds(0, TALL), cols] = w.astype(jnp.bfloat16)
            w_out[pl.ds(TALL, TALL), cols] = ds.astype(jnp.bfloat16)

    def gather(k, w_in):
        g, chunks, slabs = entry(k)
        keyvals = jnp.concatenate([line[chunk(n), :] for n in chunks], axis=0)
        od = jnp.dot(w_in[...], keyvals, preferred_element_type=jnp.float32)
        acc[g] += jnp.where(left, od[TALL:], od[:TALL])
        for rows, low in ((pl.ds(0, HD), TALL), (pl.ds(HD, HD), 0)):
            part = jnp.dot(
                qgt[g, rows, :], w_in[pl.ds(low, TALL), :], preferred_element_type=jnp.float32
            )
            for cols, n in zip(halves, chunks):
                dkv[n, rows, :] += part[:, cols]

    scores(1, score[1])

    @pl.loop(0, lax.div(plan_ref[5 * SLOTS] + DEPTH, DEPTH))
    def _(step):
        for i in range(DEPTH):
            k = DEPTH * step + i
            now, later = (i + 1) % DEPTH, (i + 2) % DEPTH
            gather(k, weight[i])
            weigh(k + 1, score[now], weight[now])
            scores(k + 2, score[later])

    @pl.loop(0, GROUPS)
    def _(n):
        for c in range(3):
            line[chunk(3 * n + c), :] = dkv[3 * n + c].astype(jnp.bfloat16).T
        acc[n] = acc[n] * scales[n]
        mine_ref[n] = acc[n, pl.ds(q_own, ROWS), :]
        theirs_ref[n] = acc[n, pl.ds(q_x, ROWS), :].astype(jnp.bfloat16)
        keep_ref[n, :ROWS] = line[block(n, k_own), :]
        keep_ref[n, ROWS:] = line[block(n, k_x), :]
        give_ref[n, :ROWS] = line[block(n, k_core), :]
        give_ref[n, ROWS:] = line[block(n, k_both), :]


def unpack_kernel(in_ref, out_ref, grad_ref):
    for h in range(0, H, 2):
        cols = slice(h * HD, (h + 2) * HD)
        a, b = in_ref[h, :ROWS], in_ref[h + 1, :ROWS]
        grad_ref[0, :, cols] = jnp.concatenate([a[:, :HD], b[:, :HD]], axis=1)
        out_ref[:, cols] = jnp.concatenate([a[:, HD:], b[:, HD:]], axis=1)
        a, b = in_ref[h, ROWS : 2 * ROWS], in_ref[h + 1, ROWS : 2 * ROWS]
        grad_ref[1, :, cols] = jnp.concatenate([a[:, :HD], b[:, :HD]], axis=1)
        grad_ref[2, :, cols] = jnp.concatenate([a[:, HD:], b[:, HD:]], axis=1)


def swap(v, axis, partner):
    return lax.ppermute(v, axis, [(i, p) for i, p in enumerate(partner)])


def per_device(qkv, grad_out, rab, doc_ids):
    bf16, f32 = jnp.bfloat16, jnp.float32
    x, y, z, core = (lax.axis_index(a) for a in ("x", "y", "z", "core"))
    whole = pl.BlockSpec(memory_space=VMEM)
    scalars = pl.BlockSpec(memory_space=SMEM)
    block = jax.ShapeDtypeStruct((H, ROWS, 128), bf16)
    double = jax.ShapeDtypeStruct((H, 2 * ROWS, 128), bf16)
    slabs = jax.ShapeDtypeStruct((len(SLABS) + 1, TALL, CHUNK), f32)
    small = pltpu.CompilerParams(vmem_limit_bytes=8 * 2**20)
    large = pltpu.CompilerParams(vmem_limit_bytes=34 * 2**20)
    first_row = (((y * 4 + z) * 2 + core) * 4 + x) * ROWS
    where = jnp.stack([x, core])
    packed, bounds = pl.pallas_call(
        pack_kernel,
        out_shape=(double, jax.ShapeDtypeStruct((DOCS,), jnp.int32)),
        in_specs=[scalars] + [pl.BlockSpec(memory_space=pltpu.HBM)] * 3,
        out_specs=(whole, scalars),
        scratch_shapes=[
            VMEM((96, 128), jnp.int32),
            VMEM((3, ROWS, H * HD), bf16),
            VMEM((ROWS, H * HD), bf16),
            pltpu.SemaphoreType.DMA((3,)),
        ],
        compiler_params=pltpu.CompilerParams(vmem_limit_bytes=63 * 2**20),
        name="pack",
    )(first_row.reshape(1), doc_ids.reshape(96, 128), qkv.transpose(1, 0, 2), grad_out)
    own = lax.all_to_all(packed, ("y", "z"), 0, 0, tiled=True)
    kv_own, qg_own = own[:, :ROWS], own[:, ROWS:]
    kv_x = swap(kv_own, "x", (1, 0, 3, 2))
    qg_x = swap(qg_own, "x", (3, 2, 1, 0))
    kv_core = swap(kv_own, "core", (1, 0))
    table_row = lax.dynamic_slice_in_dim(rab, y * 4 + z, 1, 0)[0]
    table, starts, scales, plan = pl.pallas_call(
        table_kernel,
        out_shape=(
            slabs,
            jax.ShapeDtypeStruct((GROUPS, TALL, 128), jnp.int32),
            jax.ShapeDtypeStruct((GROUPS, TALL, 128), f32),
            jax.ShapeDtypeStruct((5 * SLOTS + 1,), jnp.int32),
        ),
        in_specs=[scalars] * 3,
        out_specs=(whole, whole, whole, scalars),
        compiler_params=small,
        cost_estimate=pl.CostEstimate(flops=0, bytes_accessed=0, transcendentals=0),
        name="table",
    )(where, table_row, bounds)
    kv_x, qg_x, table, starts, scales, plan = lax.optimization_barrier(
        (kv_x, qg_x, table, starts, scales, plan)
    )
    kv_both = swap(kv_x, "core", (1, 0))
    keep, give, mine, theirs, sums = pl.pallas_call(
        main_kernel,
        out_shape=[double, double, jax.ShapeDtypeStruct((H, ROWS, 128), f32), block, slabs],
        in_specs=[scalars] * 2 + [whole] * 8,
        out_specs=[whole] * 5,
        scratch_shapes=[
            VMEM((GROUPS * SUPER, 128), bf16),
            VMEM((3 * GROUPS, 128, CHUNK), f32),
            VMEM((GROUPS, TALL, 128), f32),
            VMEM((GROUPS, 2 * TALL, 128), bf16),
            VMEM((GROUPS, 128, TALL), bf16),
        ]
        + [VMEM((2 * TALL, WIDE), f32)] * DEPTH
        + [VMEM((2 * TALL, WIDE), bf16)] * DEPTH,
        compiler_params=large,
        name="attend",
    )(where, plan, table, starts, scales, own, kv_x, kv_core, kv_both, qg_x)
    got = swap(give, "core", (1, 0))
    dkv = keep.astype(f32) + got.astype(f32)
    dkv_x = dkv[:, ROWS:].astype(bf16)
    got_qo = swap(theirs, "x", (3, 2, 1, 0))
    got_dkv = swap(dkv_x, "x", (1, 0, 3, 2))
    bias = pl.pallas_call(
        buckets_kernel,
        out_shape=jax.ShapeDtypeStruct((8, 128), f32),
        in_specs=[scalars, whole],
        out_specs=whole,
        scratch_shapes=[VMEM((NB, 8, 128), f32)],
        compiler_params=small,
        cost_estimate=pl.CostEstimate(flops=0, bytes_accessed=0, transcendentals=0),
        name="buckets",
    )(where, sums)
    bias = bias + sum(swap(bias, "x", p) for p in ((1, 0, 3, 2), (3, 2, 1, 0), (2, 3, 0, 1)))
    bias = bias[0]
    hi = lax.reduce_precision(bias, 8, 7)
    mid = lax.reduce_precision(bias - hi, 8, 7)
    lo = bias - hi - mid
    carried = jnp.pad(jnp.stack([hi, mid, lo]).astype(bf16), ((0, 13), (0, 0)))
    results = jnp.concatenate(
        [
            (mine + got_qo.astype(f32)).astype(bf16),
            (dkv[:, :ROWS] + got_dkv.astype(f32)).astype(bf16),
            jnp.broadcast_to(carried[None], (H, 16, 128)),
        ],
        axis=1,
    )
    results = lax.all_to_all(results, ("y", "z"), 0, 0, tiled=True)
    terms = lax.dynamic_slice(results, (x * 4, 2 * ROWS, 0), (4, 3, NB)).astype(f32)
    bias_grad = terms[:, 0] + terms[:, 1] + terms[:, 2]
    bias_grad = bias_grad + swap(bias_grad, "core", (1, 0))
    out, grad_qkv = pl.pallas_call(
        unpack_kernel,
        out_shape=(
            jax.ShapeDtypeStruct((ROWS, H * HD), bf16),
            jax.ShapeDtypeStruct((3, ROWS, H * HD), bf16),
        ),
        in_specs=[whole],
        out_specs=(whole, whole),
        compiler_params=small,
        name="unpack",
    )(results)
    return out, grad_qkv.transpose(1, 0, 2), bias_grad


def solution(mesh):
    fine = Mesh(mesh.devices.reshape(4, 4, 4, 2), ("x", "y", "z", "core"))
    rows = ("y", "z", "core", "x")
    return jax.shard_map(
        per_device,
        mesh=fine,
        in_specs=(P(rows, None, None), P(rows, None), P(), P()),
        out_specs=(P(rows, None), P(rows, None, None), P("x", None)),
        check_vma=False,
    )
```

time: 105 us -> 101 us (0.962); the launches traced: 104 us -> 101 us
  starting transfers between devices: 19.8 us -> 22.9 us
  local copies, waits for them, and re-layouts: 2.91 us -> 0.14 us
  Pallas kernels: 31.2 us -> 29.5 us
  waiting for transfers between devices: 25.3 us -> 24 us
    pallas_call x1, Pallas kernels: 23.3 us -> 19.9 us  [per_device(): pl.pallas_call(main_kernel, out_shape=[double, double, jax.ShapeDtypeStru...]
    ppermute x11, starting transfers between devices: 16.1 us -> 19.3 us  [swap(): return lax.ppermute(v, axis, [(i, p) for i, p in enumerate(partner)])]
    unnamed x8 -> x4, local copies, waits for them, and re-layouts: 2.79 us -> 0.01 us
    pallas_call x1, Pallas kernels: 0.78 us -> 2.36 us  [per_device(): pl.pallas_call(pack_kernel, out_shape=(double, jax.ShapeDtypeStruct((DOCS...]
    ppermute x11, waiting for transfers between devices: 12.7 us -> 11.2 us  [swap(): return lax.ppermute(v, axis, [(i, p) for i, p in enumerate(partner)])]
where the time goes in v4:
time: 101 us
  Pallas kernels  29.5 us (29%)
  waiting for transfers between devices  24 us (24%)
  starting transfers between devices  22.9 us (23%)
  blocking collectives  22 us (22%)
  other arithmetic  2.02 us (2%)
    all_to_all x1, blocking collectives, per_device(): own = lax.all_to_all(packed, ('y', 'z'), 0, 0, tiled=True)  22 us
    pallas_call x1, Pallas kernels, per_device(): pl.pallas_call(main_kernel, out_shape=[double, double, jax.ShapeDtypeStru...  19.9 us
    ppermute x11, starting transfers between devices, swap(): return lax.ppermute(v, axis, [(i, p) for i, p in enumerate(partner)])  19.3 us
    all_to_all x1, waiting for transfers between devices, per_device(): results = lax.all_to_all(results, ('y', 'z'), 0, 0, tiled=True)  12.8 us
    ppermute x11, waiting for transfers between devices, swap(): return lax.ppermute(v, axis, [(i, p) for i, p in enumerate(partner)])  11.2 us
    pallas_call x1, Pallas kernels, per_device(): pl.pallas_call(table_kernel, out_shape=(slabs, jax.ShapeDtypeStruct((GROU...  4.36 us
    all_to_all x1, starting transfers between devices, per_device(): results = lax.all_to_all(results, ('y', 'z'), 0, 0, tiled=True)  3.62 us
    pallas_call x1, Pallas kernels, per_device(): pl.pallas_call(pack_kernel, out_shape=(double, jax.ShapeDtypeStruct((DOCS...  2.36 us
  transfers between devices with their start and end apart: 12, of which 8 were waited for; matrix products, arithmetic and copies ran while one was open for 0% of the time, Pallas kernels for 7%

profile of v4, /device:TPU:1, one launch (start us, length us, event | category | flops | bytes accessed | tf_op | source)
XLA Modules:
  0.0 101.3 jit_solution(18012210245934882574)
XLA Ops:
  0.6 0.0 copy-start
  0.7 2.4 %pack.1 = (bf16[16,192,128]{2,1,0:T(8,128)(2,1)}, s32[8]{0:T(128)}) custom-call(s32[1]{0:T(128)} %bitcast.2.where_ref, s32[96,128]{1,0:T(8,128)} %bitcast.10, bf16[3,96,1024]{2,1,0:T(8,128)(2,1)} %bitcast.9, bf16[96,1024]{1,0:T(8,128)(2,1)} %g_in.1), custom_call_target="tpu_custom_call" | custom-call | tf_op jit(solution)/shard_map/pack/pallas_call | solution.py:355
  3.0 0.0 copy-start.1
  3.0 22.0 %all_to_all.10.own_ref = bf16[16,192,128]{2,1,0:T(8,128)(2,1)S(1)} all-to-all(bf16[16,192,128]{2,1,0:T(8,128)(2,1)} %get-tuple-element.22), channel_id=1, replica_groups=mesh['x'=4,'y'=4,'z'=4,'core'=2] {'y','z'}, dimensions={0} | all-to-all | bytes 1572864 | tf_op jit(solution)/shard_map/all_to_all | solution.py:369
  25.0 0.1 fusion.7
  25.1 2.6 %collective-permute-start.1 = (bf16[16,96,128]{2,1,0:T(8,128)(2,1)S(1)}, bf16[16,96,128]{2,1,0:T(8,128)(2,1)S(1)}, u32[]{:S(2)}, u32[]{:S(2)}) collective-permute-start(bf16[16,96,128]{2,1,0:T(8,128)(2,1)S(1)} %get-tuple-element.41), channel_id=1, source_target_pairs={{0,96},{32,64},{64,32},{96,0},{1,97},{33,65},{65,33},{97,1},{2,98}... | collective-permute-start | bytes 1179656 | tf_op jit(solution)/shard_map/ppermute | solution.py:340
  27.6 0.0 collective-permute-start
  27.6 0.1 pad_add_fusion.where_ref
  27.7 0.0 copy-done
  27.7 0.0 copy-done.1
  27.7 4.4 %table.1 = (f32[28,192,128]{2,1,0:T(8,128)S(1)}, s32[16,192,128]{2,1,0:T(8,128)S(1)}, f32[16,192,128]{2,1,0:T(8,128)S(1)}, s32[1281]{0:T(1024)S(1)}) custom-call(s32[2]{0:T(128)S(1)} %pad_add_fusion.where_ref, f32[20]{0:T(128)S(1)} %dynamic-slice_bitcast_fusion.rab_ref, s32[8]{0:T(128)S(1)} %copy-done.1), custom_call_target="tpu_custom_call" | custom-call | tf_op jit(solution)/shard_map/table/pallas_call | solution.py:375
  32.1 2.6 %collective-permute-start.2 = (bf16[16,96,128]{2,1,0:T(8,128)(2,1)S(1)}, bf16[16,96,128]{2,1,0:T(8,128)(2,1)S(1)}, u32[]{:S(2)}, u32[]{:S(2)}) collective-permute-start(bf16[16,96,128]{2,1,0:T(8,128)(2,1)S(1)} %get-tuple-element.42), channel_id=1, source_target_pairs={{0,1},{1,0},{2,3},{3,2},{4,5},{5,4},{6,7},{7,6},{8,9},{9,8},{10,11... | collective-permute-start | bytes 1179656 | tf_op jit(solution)/shard_map/ppermute | solution.py:340
  34.7 0.5 collective-permute-done.1.qgx_ref
  35.2 1.0 collective-permute-done.kvx_ref
  36.2 2.9 %collective-permute-start.3 = (bf16[16,96,128]{2,1,0:T(8,128)(2,1)S(1)}, bf16[16,96,128]{2,1,0:T(8,128)(2,1)S(1)}, u32[]{:S(2)}, u32[]{:S(2)}) collective-permute-start(bf16[16,96,128]{2,1,0:T(8,128)(2,1)S(1)} %collective-permute-done.kvx_ref), channel_id=1, source_target_pairs={{0,1},{1,0},{2,3},{3,2},{4,5},{5,4},{6,7},{7,6},{8,9},{9,8},{10,11... | collective-permute-start | bytes 1179656 | tf_op jit(solution)/shard_map/ppermute | solution.py:340
  39.2 0.0 collective-permute-done.2.kvc_ref
  39.2 1.3 %collective-permute-done.3.kvxc_ref = bf16[16,96,128]{2,1,0:T(8,128)(2,1)S(1)} collective-permute-done((bf16[16,96,128]{2,1,0:T(8,128)(2,1)S(1)}, bf16[16,96,128]{2,1,0:T(8,128)(2,1)S(1)}, u32[]{:S(2)}, u32[]{:S(2)}) %collective-permute-start.3) | collective-permute-done | bytes 393248 | tf_op jit(solution)/shard_map/ppermute | solution.py:340
  40.5 19.9 %attend.1 = (bf16[16,192,128]{2,1,0:T(8,128)(2,1)S(1)}, bf16[16,192,128]{2,1,0:T(8,128)(2,1)S(1)}, f32[16,96,128]{2,1,0:T(8,128)S(1)}, bf16[16,96,128]{2,1,0:T(8,128)(2,1)S(1)}, f32[28,192,128]{2,1,0:T(8,128)S(1)}) custom-call(s32[2]{0:T(128)S(1)} %pad_add_fusion.where_ref, s32[1281]{0:T(1024)S(1)} %get-tuple-element.28.plan_ref, ...), custom_call_target="tpu_custom_call" | custom-call | tf_op jit(solution)/shard_map/attend/pallas_call | solution.py:393
  60.4 2.8 %collective-permute-start.5 = (bf16[16,192,128]{2,1,0:T(8,128)(2,1)S(1)}, bf16[16,192,128]{2,1,0:T(8,128)(2,1)S(1)}, u32[]{:S(2)}, u32[]{:S(2)}) collective-permute-start(bf16[16,192,128]{2,1,0:T(8,128)(2,1)S(1)} %get-tuple-element.37), channel_id=1, source_target_pairs={{0,1},{1,0},{2,3},{3,2},{4,5},{5,4},{6,7},{7,6},{8,9},{9,8},{10,11... | collective-permute-start | bytes 2359304 | tf_op jit(solution)/shard_map/ppermute | solution.py:340
  63.2 1.7 %buckets.1 = f32[8,128]{1,0:T(8,128)S(1)} custom-call(s32[2]{0:T(128)S(1)} %pad_add_fusion.where_ref, f32[28,192,128]{2,1,0:T(8,128)S(1)} %get-tuple-element.38.sums_ref), custom_call_target="tpu_custom_call" | custom-call | tf_op jit(solution)/shard_map/buckets/pallas_call | solution.py:415
  64.9 0.1 collective-permute-start.9
  65.0 1.3 %collective-permute-start.8 = (f32[8,128]{1,0:T(8,128)S(1)}, f32[8,128]{1,0:T(8,128)S(1)}, u32[]{:S(2)}, u32[]{:S(2)}) collective-permute-start(f32[8,128]{1,0:T(8,128)S(1)} %buckets.1), channel_id=1, source_target_pairs={{0,96},{32,64},{64,32},{96,0},{1,97},{33,65},{65,33},{97,1},{2,98}... | collective-permute-start | bytes 12296 | tf_op jit(solution)/shard_map/ppermute | solution.py:340
  66.2 1.4 %collective-permute-start.7 = (f32[8,128]{1,0:T(8,128)S(1)}, f32[8,128]{1,0:T(8,128)S(1)}, u32[]{:S(2)}, u32[]{:S(2)}) collective-permute-start(f32[8,128]{1,0:T(8,128)S(1)} %buckets.1), channel_id=1, source_target_pairs={{0,32},{32,0},{64,96},{96,64},{1,33},{33,1},{65,97},{97,65},{2,34}... | collective-permute-start | bytes 12296 | tf_op jit(solution)/shard_map/ppermute | solution.py:340
  67.6 1.2 %collective-permute-start.4 = (bf16[16,96,128]{2,1,0:T(8,128)(2,1)S(1)}, bf16[16,96,128]{2,1,0:T(8,128)(2,1)S(1)}, u32[]{:S(2)}, u32[]{:S(2)}) collective-permute-start(bf16[16,96,128]{2,1,0:T(8,128)(2,1)S(1)} %get-tuple-element.35), channel_id=1, source_target_pairs={{0,96},{32,64},{64,32},{96,0},{1,97},{33,65},{65,33},{97,1},{2,98}... | collective-permute-start | bytes 1179656 | tf_op jit(solution)/shard_map/ppermute | solution.py:340
  68.8 0.1 collective-permute-done.9
  68.9 0.0 collective-permute-done.8
  68.9 0.1 collective-permute-done.7
  69.0 0.0 collective-permute-done.5
  69.0 0.2 convert_add_fusion
  69.2 0.1 slice.55
  69.3 1.3 %collective-permute-start.6 = (bf16[16,96,128]{2,1,0:T(8,128)(2,1)S(1)}, bf16[16,96,128]{2,1,0:T(8,128)(2,1)S(1)}, u32[]{:S(2)}, u32[]{:S(2)}) collective-permute-start(bf16[16,96,128]{2,1,0:T(8,128)(2,1)S(1)} %slice.55), channel_id=1, source_target_pairs={{0,32},{32,0},{64,96},{96,64},{1,33},{33,1},{65,97},{97,65},{2,34}... | collective-permute-start | bytes 1179656 | tf_op jit(solution)/shard_map/ppermute | solution.py:340
  70.6 8.0 %collective-permute-done.4 = bf16[16,96,128]{2,1,0:T(8,128)(2,1)S(1)} collective-permute-done((bf16[16,96,128]{2,1,0:T(8,128)(2,1)S(1)}, bf16[16,96,128]{2,1,0:T(8,128)(2,1)S(1)}, u32[]{:S(2)}, u32[]{:S(2)}) %collective-permute-start.4) | collective-permute-done | bytes 393248 | tf_op jit(solution)/shard_map/ppermute | solution.py:340
  78.6 0.1 add_convert_fusion
  78.7 0.1 collective-permute-done.6
  78.8 0.1 fusion
  78.9 1.0 pad_maximum_fusion
  79.9 3.6 %all-to-all-start.1 = ((bf16[16,208,128]{2,1,0:T(8,128)(2,1)}), bf16[16,208,128]{2,1,0:T(8,128)(2,1)S(1)}, u32[]{:S(2)}, u32[]{:S(2)}) async-start(bf16[16,208,128]{2,1,0:T(8,128)(2,1)} %pad_maximum_fusion), calls=%async_computation.1 | async-start | bytes 1703936 | tf_op jit(solution)/shard_map/all_to_all | solution.py:439
  83.5 12.8 %all-to-all-done.1.in_ref = bf16[16,208,128]{2,1,0:T(8,128)(2,1)S(1)} async-done(((bf16[16,208,128]{2,1,0:T(8,128)(2,1)}), bf16[16,208,128]{2,1,0:T(8,128)(2,1)S(1)}, u32[]{:S(2)}, u32[]{:S(2)}) %all-to-all-start.1) | async-done | bytes 852000 | tf_op jit(solution)/shard_map/all_to_all | solution.py:439
  96.3 3.2 %collective-permute-start.10 = (f32[4,20]{1,0:T(4,128)S(1)}, f32[4,20]{1,0:T(4,128)S(1)}, u32[]{:S(2)}, u32[]{:S(2)}) collective-permute-start(f32[4,20]{1,0:T(4,128)S(1)} %bitcast.11), channel_id=1, source_target_pairs={{0,1},{1,0},{2,3},{3,2},{4,5},{5,4},{6,7},{7,6},{8,9},{9,8},{10,11... | collective-permute-start | bytes 968 | tf_op jit(solution)/shard_map/ppermute | solution.py:340
  99.5 1.2 %unpack.1 = (bf16[96,1024]{1,0:T(8,128)(2,1)}, bf16[3,96,1024]{2,1,0:T(8,128)(2,1)}) custom-call(bf16[16,208,128]{2,1,0:T(8,128)(2,1)S(1)} %all-to-all-done.1.in_ref), custom_call_target="tpu_custom_call" | custom-call | tf_op jit(solution)/shard_map/unpack/pallas_call | solution.py:443
  100.7 0.0 collective-permute-done.10
  100.7 0.6 add.63
  (7 shorter events, 0.1 us)
Async XLA Ops:
  0.6 27.1 %copy-start = (f32[16,20]{1,0:T(8,128)S(1)}, f32[16,20]{1,0:T(8,128)}, u32[]{:S(2)}) copy-start(f32[16,20]{1,0:T(8,128)} %param.6) | copy-start | bytes 3844
  3.0 24.7 %copy-start.1 = (s32[8]{0:T(128)S(1)}, s32[8]{0:T(128)}, u32[]{:S(2)}) copy-start(s32[8]{0:T(128)} %get-tuple-element.23.bounds_ref) | copy-start | bytes 100
  25.1 10.2 %collective-permute-start.1 = (bf16[16,96,128]{2,1,0:T(8,128)(2,1)S(1)}, bf16[16,96,128]{2,1,0:T(8,128)(2,1)S(1)}, u32[]{:S(2)}, u32[]{:S(2)}) collective-permute-start(bf16[16,96,128]{2,1,0:T(8,128)(2,1)S(1)} %get-tuple-element.41), channel_id=1, source_target_pairs={{0,96},{32,64},{64,32},{96,0},{1,97},{33,65},{65,33},{97,1},{2,98}... | collective-permute-start | bytes 1179656 | tf_op jit(solution)/shard_map/ppermute | solution.py:340
  27.6 8.6 %collective-permute-start = (bf16[16,96,128]{2,1,0:T(8,128)(2,1)S(1)}, bf16[16,96,128]{2,1,0:T(8,128)(2,1)S(1)}, u32[]{:S(2)}, u32[]{:S(2)}) collective-permute-start(bf16[16,96,128]{2,1,0:T(8,128)(2,1)S(1)} %get-tuple-element.42), channel_id=1, source_target_pairs={{0,32},{32,0},{64,96},{96,64},{1,33},{33,1},{65,97},{97,65},{2,34}... | collective-permute-start | bytes 1179656 | tf_op jit(solution)/shard_map/ppermute | solution.py:340
  32.1 7.1 %collective-permute-start.2 = (bf16[16,96,128]{2,1,0:T(8,128)(2,1)S(1)}, bf16[16,96,128]{2,1,0:T(8,128)(2,1)S(1)}, u32[]{:S(2)}, u32[]{:S(2)}) collective-permute-start(bf16[16,96,128]{2,1,0:T(8,128)(2,1)S(1)} %get-tuple-element.42), channel_id=1, source_target_pairs={{0,1},{1,0},{2,3},{3,2},{4,5},{5,4},{6,7},{7,6},{8,9},{9,8},{10,11... | collective-permute-start | bytes 1179656 | tf_op jit(solution)/shard_map/ppermute | solution.py:340
  36.2 4.3 %collective-permute-start.3 = (bf16[16,96,128]{2,1,0:T(8,128)(2,1)S(1)}, bf16[16,96,128]{2,1,0:T(8,128)(2,1)S(1)}, u32[]{:S(2)}, u32[]{:S(2)}) collective-permute-start(bf16[16,96,128]{2,1,0:T(8,128)(2,1)S(1)} %collective-permute-done.kvx_ref), channel_id=1, source_target_pairs={{0,1},{1,0},{2,3},{3,2},{4,5},{5,4},{6,7},{7,6},{8,9},{9,8},{10,11... | collective-permute-start | bytes 1179656 | tf_op jit(solution)/shard_map/ppermute | solution.py:340
  60.4 8.6 %collective-permute-start.5 = (bf16[16,192,128]{2,1,0:T(8,128)(2,1)S(1)}, bf16[16,192,128]{2,1,0:T(8,128)(2,1)S(1)}, u32[]{:S(2)}, u32[]{:S(2)}) collective-permute-start(bf16[16,192,128]{2,1,0:T(8,128)(2,1)S(1)} %get-tuple-element.37), channel_id=1, source_target_pairs={{0,1},{1,0},{2,3},{3,2},{4,5},{5,4},{6,7},{7,6},{8,9},{9,8},{10,11... | collective-permute-start | bytes 2359304 | tf_op jit(solution)/shard_map/ppermute | solution.py:340
  64.9 4.0 %collective-permute-start.9 = (f32[8,128]{1,0:T(8,128)S(1)}, f32[8,128]{1,0:T(8,128)S(1)}, u32[]{:S(2)}, u32[]{:S(2)}) collective-permute-start(f32[8,128]{1,0:T(8,128)S(1)} %buckets.1), channel_id=1, source_target_pairs={{0,64},{32,96},{64,0},{96,32},{1,65},{33,97},{65,1},{97,33},{2,66}... | collective-permute-start | bytes 12296 | tf_op jit(solution)/shard_map/ppermute | solution.py:340
  65.0 4.0 %collective-permute-start.8 = (f32[8,128]{1,0:T(8,128)S(1)}, f32[8,128]{1,0:T(8,128)S(1)}, u32[]{:S(2)}, u32[]{:S(2)}) collective-permute-start(f32[8,128]{1,0:T(8,128)S(1)} %buckets.1), channel_id=1, source_target_pairs={{0,96},{32,64},{64,32},{96,0},{1,97},{33,65},{65,33},{97,1},{2,98}... | collective-permute-start | bytes 12296 | tf_op jit(solution)/shard_map/ppermute | solution.py:340
  66.2 2.8 %collective-permute-start.7 = (f32[8,128]{1,0:T(8,128)S(1)}, f32[8,128]{1,0:T(8,128)S(1)}, u32[]{:S(2)}, u32[]{:S(2)}) collective-permute-start(f32[8,128]{1,0:T(8,128)S(1)} %buckets.1), channel_id=1, source_target_pairs={{0,32},{32,0},{64,96},{96,64},{1,33},{33,1},{65,97},{97,65},{2,34}... | collective-permute-start | bytes 12296 | tf_op jit(solution)/shard_map/ppermute | solution.py:340
  67.6 11.0 %collective-permute-start.4 = (bf16[16,96,128]{2,1,0:T(8,128)(2,1)S(1)}, bf16[16,96,128]{2,1,0:T(8,128)(2,1)S(1)}, u32[]{:S(2)}, u32[]{:S(2)}) collective-permute-start(bf16[16,96,128]{2,1,0:T(8,128)(2,1)S(1)} %get-tuple-element.35), channel_id=1, source_target_pairs={{0,96},{32,64},{64,32},{96,0},{1,97},{33,65},{65,33},{97,1},{2,98}... | collective-permute-start | bytes 1179656 | tf_op jit(solution)/shard_map/ppermute | solution.py:340
  69.3 9.5 %collective-permute-start.6 = (bf16[16,96,128]{2,1,0:T(8,128)(2,1)S(1)}, bf16[16,96,128]{2,1,0:T(8,128)(2,1)S(1)}, u32[]{:S(2)}, u32[]{:S(2)}) collective-permute-start(bf16[16,96,128]{2,1,0:T(8,128)(2,1)S(1)} %slice.55), channel_id=1, source_target_pairs={{0,32},{32,0},{64,96},{96,64},{1,33},{33,1},{65,97},{97,65},{2,34}... | collective-permute-start | bytes 1179656 | tf_op jit(solution)/shard_map/ppermute | solution.py:340
  79.9 16.4 %all-to-all-start.1 = ((bf16[16,208,128]{2,1,0:T(8,128)(2,1)}), bf16[16,208,128]{2,1,0:T(8,128)(2,1)S(1)}, u32[]{:S(2)}, u32[]{:S(2)}) async-start(bf16[16,208,128]{2,1,0:T(8,128)(2,1)} %pad_maximum_fusion), calls=%async_computation.1 | async-start | bytes 1703936 | tf_op jit(solution)/shard_map/all_to_all | solution.py:439
  96.3 4.4 %collective-permute-start.10 = (f32[4,20]{1,0:T(4,128)S(1)}, f32[4,20]{1,0:T(4,128)S(1)}, u32[]{:S(2)}, u32[]{:S(2)}) collective-permute-start(f32[4,20]{1,0:T(4,128)S(1)} %bitcast.11), channel_id=1, source_target_pairs={{0,1},{1,0},{2,3},{3,2},{4,5},{5,4},{6,7},{7,6},{8,9},{9,8},{10,11... | collective-permute-start | bytes 968 | tf_op jit(solution)/shard_map/ppermute | solution.py:340

commit v5 on v4

--- a/solution.py
+++ b/solution.py
@@ -323,6 +323,35 @@
         keep_ref[n, ROWS:] = line[block(n, k_x), :]
         give_ref[n, :ROWS] = line[block(n, k_core), :]
         give_ref[n, ROWS:] = line[block(n, k_both), :]
+
+
+def combine_kernel(mine_ref, got_qo_ref, dkv_ref, got_dkv_ref, out_ref):
+    @pl.loop(0, GROUPS)
+    def _(n):
+        qo = mine_ref[n] + got_qo_ref[n].astype(jnp.float32)
+        out_ref[n, :ROWS] = qo.astype(jnp.bfloat16)
+        dkv = dkv_ref[n, :ROWS] + got_dkv_ref[n].astype(jnp.float32)
+        out_ref[n, ROWS : 2 * ROWS] = dkv.astype(jnp.bfloat16)
+
+
+def bias_kernel(in_ref, b0_ref, b1_ref, b2_ref, b3_ref, out_ref, terms_ref, sem):
+    total = b0_ref[...] + b1_ref[...] + b2_ref[...] + b3_ref[...]
+    high = total.astype(jnp.bfloat16)
+    rest = total - high.astype(jnp.float32)
+    middle = rest.astype(jnp.bfloat16)
+    low = rest - middle.astype(jnp.float32)
+    row = lax.broadcasted_iota(jnp.int32, (8, 128), 0)
+    terms = jnp.where(
+        row == 0,
+        high.astype(jnp.float32),
+        jnp.where(row == 1, middle.astype(jnp.float32), jnp.where(row == 2, low, 0.0)),
+    )
+    terms = jnp.concatenate([terms, jnp.zeros((8, 128), jnp.float32)], axis=0)
+    for n in range(GROUPS):
+        terms_ref[n] = terms.astype(jnp.bfloat16)
+    copy = pltpu.make_async_copy(terms_ref, out_ref.at[:, pl.ds(2 * ROWS, 16), :], sem)
+    copy.start()
+    copy.wait()
 
 
 def unpack_kernel(in_ref, out_ref, grad_ref):
@@ -422,20 +451,26 @@
         cost_estimate=pl.CostEstimate(flops=0, bytes_accessed=0, transcendentals=0),
         name="buckets",
     )(where, sums)
-    bias = bias + sum(swap(bias, "x", p) for p in ((1, 0, 3, 2), (3, 2, 1, 0), (2, 3, 0, 1)))
-    bias = bias[0]
-    hi = lax.reduce_precision(bias, 8, 7)
-    mid = lax.reduce_precision(bias - hi, 8, 7)
-    lo = bias - hi - mid
-    carried = jnp.pad(jnp.stack([hi, mid, lo]).astype(bf16), ((0, 13), (0, 0)))
-    results = jnp.concatenate(
-        [
-            (mine + got_qo.astype(f32)).astype(bf16),
-            (dkv[:, :ROWS] + got_dkv.astype(f32)).astype(bf16),
-            jnp.broadcast_to(carried[None], (H, 16, 128)),
-        ],
-        axis=1,
-    )
+    others = [swap(bias, "x", p) for p in ((1, 0, 3, 2), (3, 2, 1, 0), (2, 3, 0, 1))]
+    results = pl.pallas_call(
+        combine_kernel,
+        out_shape=jax.ShapeDtypeStruct((H, 2 * ROWS + 16, 128), bf16),
+        in_specs=[whole] * 4,
+        out_specs=whole,
+        compiler_params=small,
+        cost_estimate=pl.CostEstimate(flops=0, bytes_accessed=10**7, transcendentals=0),
+        name="combine",
+    )(mine, got_qo, dkv, got_dkv)
+    results = pl.pallas_call(
+        bias_kernel,
+        out_shape=jax.ShapeDtypeStruct((H, 2 * ROWS + 16, 128), bf16),
+        in_specs=[pl.BlockSpec(memory_space=pl.ANY)] + [whole] * 4,
+        out_specs=pl.BlockSpec(memory_space=pl.ANY),
+        scratch_shapes=[VMEM((GROUPS, 16, 128), bf16), pltpu.SemaphoreType.DMA(())],
+        input_output_aliases={0: 0},
+        compiler_params=small,
+        name="bias",
+    )(results, bias, *others)
     results = lax.all_to_all(results, ("y", "z"), 0, 0, tiled=True)
     terms = lax.dynamic_slice(results, (x * 4, 2 * ROWS, 0), (4, 3, NB)).astype(f32)
     bias_grad = terms[:, 0] + terms[:, 1] + terms[:, 2]

time: 101 us -> 98.9 us (0.979)
  waiting for transfers between devices: 24 us -> 21.2 us
  other arithmetic: 2.02 us -> 0.85 us
    ppermute x11, waiting for transfers between devices: 11.2 us -> 7.9 us  [swap(): return lax.ppermute(v, axis, [(i, p) for i, p in enumerate(partner)])]
    pallas_call x0 -> x2, Pallas kernels: none -> 1.78 us  [the longest x1 1.12 us: per_device(): pl.pallas_call(combine_kernel, out_shape=jax.ShapeDtypeStruct((H, 2 * ROW...]
    pallas_call x1, Pallas kernels: 19.9 us -> 18.8 us  [per_device(): pl.pallas_call(main_kernel, out_shape=[double, double, jax.ShapeDtypeStru...]
  transfers between devices with their start and end apart: 12 -> 12, of which waited for: 8 -> 7; matrix products, arithmetic and copies ran while one was open for 0% -> 0% of each run, Pallas kernels for 7% -> 8%
where the time goes in v5:
time: 98.9 us; the launch traced here: 98.6 us
  Pallas kernels  30 us (30%)
  starting transfers between devices  23.6 us (24%)
  blocking collectives  22 us (22%)
  waiting for transfers between devices  21.2 us (21%)
    all_to_all x1, blocking collectives, per_device(): own = lax.all_to_all(packed, ('y', 'z'), 0, 0, tiled=True)  22 us
    ppermute x11, starting transfers between devices, swap(): return lax.ppermute(v, axis, [(i, p) for i, p in enumerate(partner)])  20 us
    pallas_call x1, Pallas kernels, per_device(): pl.pallas_call(main_kernel, out_shape=[double, double, jax.ShapeDtypeStru...  18.8 us
    all_to_all x1, waiting for transfers between devices, per_device(): results = lax.all_to_all(results, ('y', 'z'), 0, 0, tiled=True)  13.3 us
    ppermute x11, waiting for transfers between devices, swap(): return lax.ppermute(v, axis, [(i, p) for i, p in enumerate(partner)])  7.9 us
    pallas_call x1, Pallas kernels, per_device(): pl.pallas_call(table_kernel, out_shape=(slabs, jax.ShapeDtypeStruct((GROU...  4.27 us
    all_to_all x1, starting transfers between devices, per_device(): results = lax.all_to_all(results, ('y', 'z'), 0, 0, tiled=True)  3.64 us
    pallas_call x1, Pallas kernels, per_device(): pl.pallas_call(pack_kernel, out_shape=(double, jax.ShapeDtypeStruct((DOCS...  2.37 us
  transfers between devices with their start and end apart: 12, of which 7 were waited for; matrix products, arithmetic and copies ran while one was open for 0% of the time, Pallas kernels for 8%

profile of v5, /device:TPU:1, one launch (start us, length us, event | category | flops | bytes accessed | tf_op | source)
XLA Modules:
  0.0 98.6 jit_solution(17378851206790444333)
XLA Ops:
  0.6 0.0 copy-start
  0.7 2.4 %pack.1 = (bf16[16,192,128]{2,1,0:T(8,128)(2,1)}, s32[8]{0:T(128)}) custom-call(s32[1]{0:T(128)} %bitcast.2.where_ref, s32[96,128]{1,0:T(8,128)} %bitcast.10, bf16[3,96,1024]{2,1,0:T(8,128)(2,1)} %bitcast.9, bf16[96,1024]{1,0:T(8,128)(2,1)} %g_in.1), custom_call_target="tpu_custom_call" | custom-call | tf_op jit(solution)/shard_map/pack/pallas_call | solution.py:384
  3.0 0.0 copy-start.1
  3.0 22.0 %all_to_all.10.own_ref = bf16[16,192,128]{2,1,0:T(8,128)(2,1)S(1)} all-to-all(bf16[16,192,128]{2,1,0:T(8,128)(2,1)} %get-tuple-element.22), channel_id=1, replica_groups=mesh['x'=4,'y'=4,'z'=4,'core'=2] {'y','z'}, dimensions={0} | all-to-all | bytes 1572864 | tf_op jit(solution)/shard_map/all_to_all | solution.py:398
  25.0 0.1 fusion
  25.1 2.6 %collective-permute-start.1 = (bf16[16,96,128]{2,1,0:T(8,128)(2,1)S(1)}, bf16[16,96,128]{2,1,0:T(8,128)(2,1)S(1)}, u32[]{:S(2)}, u32[]{:S(2)}) collective-permute-start(bf16[16,96,128]{2,1,0:T(8,128)(2,1)S(1)} %get-tuple-element.41), channel_id=1, source_target_pairs={{0,96},{32,64},{64,32},{96,0},{1,97},{33,65},{65,33},{97,1},{2,98}... | collective-permute-start | bytes 1179656 | tf_op jit(solution)/shard_map/ppermute | solution.py:369
  27.6 0.0 collective-permute-start
  27.6 0.1 pad_add_fusion.where_ref
  27.7 0.0 copy-done
  27.7 0.0 copy-done.1
  27.7 4.3 %table.1 = (f32[28,192,128]{2,1,0:T(8,128)S(1)}, s32[16,192,128]{2,1,0:T(8,128)S(1)}, f32[16,192,128]{2,1,0:T(8,128)S(1)}, s32[1281]{0:T(1024)S(1)}) custom-call(s32[2]{0:T(128)S(1)} %pad_add_fusion.where_ref, f32[20]{0:T(128)S(1)} %dynamic-slice_bitcast_fusion.rab_ref, s32[8]{0:T(128)S(1)} %copy-done.1), custom_call_target="tpu_custom_call" | custom-call | tf_op jit(solution)/shard_map/table/pallas_call | solution.py:404
  32.0 2.7 %collective-permute-start.2 = (bf16[16,96,128]{2,1,0:T(8,128)(2,1)S(1)}, bf16[16,96,128]{2,1,0:T(8,128)(2,1)S(1)}, u32[]{:S(2)}, u32[]{:S(2)}) collective-permute-start(bf16[16,96,128]{2,1,0:T(8,128)(2,1)S(1)} %get-tuple-element.42), channel_id=1, source_target_pairs={{0,1},{1,0},{2,3},{3,2},{4,5},{5,4},{6,7},{7,6},{8,9},{9,8},{10,11... | collective-permute-start | bytes 1179656 | tf_op jit(solution)/shard_map/ppermute | solution.py:369
  34.7 0.6 collective-permute-done.1.qgx_ref
  35.2 1.0 %collective-permute-done.kvx_ref = bf16[16,96,128]{2,1,0:T(8,128)(2,1)S(1)} collective-permute-done((bf16[16,96,128]{2,1,0:T(8,128)(2,1)S(1)}, bf16[16,96,128]{2,1,0:T(8,128)(2,1)S(1)}, u32[]{:S(2)}, u32[]{:S(2)}) %collective-permute-start) | collective-permute-done | bytes 393248 | tf_op jit(solution)/shard_map/ppermute | solution.py:369
  36.2 2.9 %collective-permute-start.3 = (bf16[16,96,128]{2,1,0:T(8,128)(2,1)S(1)}, bf16[16,96,128]{2,1,0:T(8,128)(2,1)S(1)}, u32[]{:S(2)}, u32[]{:S(2)}) collective-permute-start(bf16[16,96,128]{2,1,0:T(8,128)(2,1)S(1)} %collective-permute-done.kvx_ref), channel_id=1, source_target_pairs={{0,1},{1,0},{2,3},{3,2},{4,5},{5,4},{6,7},{7,6},{8,9},{9,8},{10,11... | collective-permute-start | bytes 1179656 | tf_op jit(solution)/shard_map/ppermute | solution.py:369
  39.2 0.0 collective-permute-done.2.kvc_ref
  39.2 1.3 %collective-permute-done.3.kvxc_ref = bf16[16,96,128]{2,1,0:T(8,128)(2,1)S(1)} collective-permute-done((bf16[16,96,128]{2,1,0:T(8,128)(2,1)S(1)}, bf16[16,96,128]{2,1,0:T(8,128)(2,1)S(1)}, u32[]{:S(2)}, u32[]{:S(2)}) %collective-permute-start.3) | collective-permute-done | bytes 393248 | tf_op jit(solution)/shard_map/ppermute | solution.py:369
  40.5 18.8 %attend.1 = (bf16[16,192,128]{2,1,0:T(8,128)(2,1)S(1)}, bf16[16,192,128]{2,1,0:T(8,128)(2,1)S(1)}, f32[16,96,128]{2,1,0:T(8,128)S(1)}, bf16[16,96,128]{2,1,0:T(8,128)(2,1)S(1)}, f32[28,192,128]{2,1,0:T(8,128)S(1)}) custom-call(s32[2]{0:T(128)S(1)} %pad_add_fusion.where_ref, s32[1281]{0:T(1024)S(1)} %get-tuple-element.28.plan_ref, ...), custom_call_target="tpu_custom_call" | custom-call | tf_op jit(solution)/shard_map/attend/pallas_call | solution.py:422
  59.3 1.6 %collective-permute-start.5 = (bf16[16,192,128]{2,1,0:T(8,128)(2,1)S(1)}, bf16[16,192,128]{2,1,0:T(8,128)(2,1)S(1)}, u32[]{:S(2)}, u32[]{:S(2)}) collective-permute-start(bf16[16,192,128]{2,1,0:T(8,128)(2,1)S(1)} %get-tuple-element.37), channel_id=1, source_target_pairs={{0,1},{1,0},{2,3},{3,2},{4,5},{5,4},{6,7},{7,6},{8,9},{9,8},{10,11... | collective-permute-start | bytes 2359304 | tf_op jit(solution)/shard_map/ppermute | solution.py:369
  60.8 3.6 %collective-permute-start.4 = (bf16[16,96,128]{2,1,0:T(8,128)(2,1)S(1)}, bf16[16,96,128]{2,1,0:T(8,128)(2,1)S(1)}, u32[]{:S(2)}, u32[]{:S(2)}) collective-permute-start(bf16[16,96,128]{2,1,0:T(8,128)(2,1)S(1)} %get-tuple-element.35), channel_id=1, source_target_pairs={{0,96},{32,64},{64,32},{96,0},{1,97},{33,65},{65,33},{97,1},{2,98}... | collective-permute-start | bytes 1179656 | tf_op jit(solution)/shard_map/ppermute | solution.py:369
  64.4 0.0 collective-permute-done.5
  64.4 0.2 convert_add_fusion.dkv_ref
  64.6 0.1 slice.37
  64.7 0.1 collective-permute-start.6
  64.8 1.7 %buckets.1.b0_ref = f32[8,128]{1,0:T(8,128)S(1)} custom-call(s32[2]{0:T(128)S(1)} %pad_add_fusion.where_ref, f32[28,192,128]{2,1,0:T(8,128)S(1)} %get-tuple-element.38.sums_ref), custom_call_target="tpu_custom_call" | custom-call | tf_op jit(solution)/shard_map/buckets/pallas_call | solution.py:444
  66.4 3.1 %collective-permute-start.9 = (f32[8,128]{1,0:T(8,128)S(1)}, f32[8,128]{1,0:T(8,128)S(1)}, u32[]{:S(2)}, u32[]{:S(2)}) collective-permute-start(f32[8,128]{1,0:T(8,128)S(1)} %buckets.1.b0_ref), channel_id=1, source_target_pairs={{0,64},{32,96},{64,0},{96,32},{1,65},{33,97},{65,1},{97,33},{2,66}... | collective-permute-start | bytes 12296 | tf_op jit(solution)/shard_map/ppermute | solution.py:369
  69.6 0.8 collective-permute-start.8
  70.4 0.0 collective-permute-start.7
  70.4 3.4 %collective-permute-done.4.got_qo_ref = bf16[16,96,128]{2,1,0:T(8,128)(2,1)S(1)} collective-permute-done((bf16[16,96,128]{2,1,0:T(8,128)(2,1)S(1)}, bf16[16,96,128]{2,1,0:T(8,128)(2,1)S(1)}, u32[]{:S(2)}, u32[]{:S(2)}) %collective-permute-start.4) | collective-permute-done | bytes 393248 | tf_op jit(solution)/shard_map/ppermute | solution.py:369
  73.8 1.3 %collective-permute-done.6.got_dkv_ref = bf16[16,96,128]{2,1,0:T(8,128)(2,1)S(1)} collective-permute-done((bf16[16,96,128]{2,1,0:T(8,128)(2,1)S(1)}, bf16[16,96,128]{2,1,0:T(8,128)(2,1)S(1)}, u32[]{:S(2)}, u32[]{:S(2)}) %collective-permute-start.6) | collective-permute-done | bytes 393248 | tf_op jit(solution)/shard_map/ppermute | solution.py:369
  75.1 1.1 %combine.1.in_ref = bf16[16,208,128]{2,1,0:T(8,128)(2,1)} custom-call(f32[16,96,128]{2,1,0:T(8,128)S(1)} %get-tuple-element.34.mine_ref, bf16[16,96,128]{2,1,0:T(8,128)(2,1)S(1)} %collective-permute-done.4.got_qo_ref, f32[16,192,128]{2,1,0:T(8,128)S(1)} %convert_add_fusion.dkv_ref, bf16[16,96,128]{2,1,0:T(8,128)(2,1)S(1)} %collective-permute-done.6.got_dkv_ref), custom_call_target="tpu_custom_call" | custom-call | bytes 10000000 | tf_op jit(solution)/shard_map/combine/pallas_call | solution.py:455
  76.2 0.3 collective-permute-done.9.b3_ref
  76.5 0.0 collective-permute-done.8.b2_ref
  76.5 0.0 collective-permute-done.7.b1_ref
  76.5 0.7 bias.1
  77.2 3.6 %all-to-all-start.1 = ((bf16[16,208,128]{2,1,0:T(8,128)(2,1)}), bf16[16,208,128]{2,1,0:T(8,128)(2,1)S(1)}, u32[]{:S(2)}, u32[]{:S(2)}) async-start(bf16[16,208,128]{2,1,0:T(8,128)(2,1)} %bias.1), calls=%async_computation.1 | async-start | bytes 1703936 | tf_op jit(solution)/shard_map/all_to_all | solution.py:474
  80.8 13.3 %all-to-all-done.1.in_ref = bf16[16,208,128]{2,1,0:T(8,128)(2,1)S(1)} async-done(((bf16[16,208,128]{2,1,0:T(8,128)(2,1)}), bf16[16,208,128]{2,1,0:T(8,128)(2,1)S(1)}, u32[]{:S(2)}, u32[]{:S(2)}) %all-to-all-start.1) | async-done | bytes 852000 | tf_op jit(solution)/shard_map/all_to_all | solution.py:474
  94.1 2.7 %collective-permute-start.10 = (f32[4,20]{1,0:T(4,128)S(1)}, f32[4,20]{1,0:T(4,128)S(1)}, u32[]{:S(2)}, u32[]{:S(2)}) collective-permute-start(f32[4,20]{1,0:T(4,128)S(1)} %bitcast.11), channel_id=1, source_target_pairs={{0,1},{1,0},{2,3},{3,2},{4,5},{5,4},{6,7},{7,6},{8,9},{9,8},{10,11... | collective-permute-start | bytes 968 | tf_op jit(solution)/shard_map/ppermute | solution.py:369
  96.8 1.2 %unpack.1 = (bf16[96,1024]{1,0:T(8,128)(2,1)}, bf16[3,96,1024]{2,1,0:T(8,128)(2,1)}) custom-call(bf16[16,208,128]{2,1,0:T(8,128)(2,1)S(1)} %all-to-all-done.1.in_ref), custom_call_target="tpu_custom_call" | custom-call | tf_op jit(solution)/shard_map/unpack/pallas_call | solution.py:478
  98.0 0.0 collective-permute-done.10
  98.0 0.6 add.41
  (3 shorter events, 0.0 us)
Async XLA Ops:
  0.6 27.1 %copy-start = (f32[16,20]{1,0:T(8,128)S(1)}, f32[16,20]{1,0:T(8,128)}, u32[]{:S(2)}) copy-start(f32[16,20]{1,0:T(8,128)} %param.6) | copy-start | bytes 3844
  3.0 24.7 %copy-start.1 = (s32[8]{0:T(128)S(1)}, s32[8]{0:T(128)}, u32[]{:S(2)}) copy-start(s32[8]{0:T(128)} %get-tuple-element.23.bounds_ref) | copy-start | bytes 100
  25.1 10.2 %collective-permute-start.1 = (bf16[16,96,128]{2,1,0:T(8,128)(2,1)S(1)}, bf16[16,96,128]{2,1,0:T(8,128)(2,1)S(1)}, u32[]{:S(2)}, u32[]{:S(2)}) collective-permute-start(bf16[16,96,128]{2,1,0:T(8,128)(2,1)S(1)} %get-tuple-element.41), channel_id=1, source_target_pairs={{0,96},{32,64},{64,32},{96,0},{1,97},{33,65},{65,33},{97,1},{2,98}... | collective-permute-start | bytes 1179656 | tf_op jit(solution)/shard_map/ppermute | solution.py:369
  27.6 8.6 %collective-permute-start = (bf16[16,96,128]{2,1,0:T(8,128)(2,1)S(1)}, bf16[16,96,128]{2,1,0:T(8,128)(2,1)S(1)}, u32[]{:S(2)}, u32[]{:S(2)}) collective-permute-start(bf16[16,96,128]{2,1,0:T(8,128)(2,1)S(1)} %get-tuple-element.42), channel_id=1, source_target_pairs={{0,32},{32,0},{64,96},{96,64},{1,33},{33,1},{65,97},{97,65},{2,34}... | collective-permute-start | bytes 1179656 | tf_op jit(solution)/shard_map/ppermute | solution.py:369
  32.0 7.2 %collective-permute-start.2 = (bf16[16,96,128]{2,1,0:T(8,128)(2,1)S(1)}, bf16[16,96,128]{2,1,0:T(8,128)(2,1)S(1)}, u32[]{:S(2)}, u32[]{:S(2)}) collective-permute-start(bf16[16,96,128]{2,1,0:T(8,128)(2,1)S(1)} %get-tuple-element.42), channel_id=1, source_target_pairs={{0,1},{1,0},{2,3},{3,2},{4,5},{5,4},{6,7},{7,6},{8,9},{9,8},{10,11... | collective-permute-start | bytes 1179656 | tf_op jit(solution)/shard_map/ppermute | solution.py:369
  36.2 4.3 %collective-permute-start.3 = (bf16[16,96,128]{2,1,0:T(8,128)(2,1)S(1)}, bf16[16,96,128]{2,1,0:T(8,128)(2,1)S(1)}, u32[]{:S(2)}, u32[]{:S(2)}) collective-permute-start(bf16[16,96,128]{2,1,0:T(8,128)(2,1)S(1)} %collective-permute-done.kvx_ref), channel_id=1, source_target_pairs={{0,1},{1,0},{2,3},{3,2},{4,5},{5,4},{6,7},{7,6},{8,9},{9,8},{10,11... | collective-permute-start | bytes 1179656 | tf_op jit(solution)/shard_map/ppermute | solution.py:369
  59.3 5.1 %collective-permute-start.5 = (bf16[16,192,128]{2,1,0:T(8,128)(2,1)S(1)}, bf16[16,192,128]{2,1,0:T(8,128)(2,1)S(1)}, u32[]{:S(2)}, u32[]{:S(2)}) collective-permute-start(bf16[16,192,128]{2,1,0:T(8,128)(2,1)S(1)} %get-tuple-element.37), channel_id=1, source_target_pairs={{0,1},{1,0},{2,3},{3,2},{4,5},{5,4},{6,7},{7,6},{8,9},{9,8},{10,11... | collective-permute-start | bytes 2359304 | tf_op jit(solution)/shard_map/ppermute | solution.py:369
  60.8 12.9 %collective-permute-start.4 = (bf16[16,96,128]{2,1,0:T(8,128)(2,1)S(1)}, bf16[16,96,128]{2,1,0:T(8,128)(2,1)S(1)}, u32[]{:S(2)}, u32[]{:S(2)}) collective-permute-start(bf16[16,96,128]{2,1,0:T(8,128)(2,1)S(1)} %get-tuple-element.35), channel_id=1, source_target_pairs={{0,96},{32,64},{64,32},{96,0},{1,97},{33,65},{65,33},{97,1},{2,98}... | collective-permute-start | bytes 1179656 | tf_op jit(solution)/shard_map/ppermute | solution.py:369
  64.7 10.4 %collective-permute-start.6 = (bf16[16,96,128]{2,1,0:T(8,128)(2,1)S(1)}, bf16[16,96,128]{2,1,0:T(8,128)(2,1)S(1)}, u32[]{:S(2)}, u32[]{:S(2)}) collective-permute-start(bf16[16,96,128]{2,1,0:T(8,128)(2,1)S(1)} %slice.37), channel_id=1, source_target_pairs={{0,32},{32,0},{64,96},{96,64},{1,33},{33,1},{65,97},{97,65},{2,34}... | collective-permute-start | bytes 1179656 | tf_op jit(solution)/shard_map/ppermute | solution.py:369
  66.4 10.0 %collective-permute-start.9 = (f32[8,128]{1,0:T(8,128)S(1)}, f32[8,128]{1,0:T(8,128)S(1)}, u32[]{:S(2)}, u32[]{:S(2)}) collective-permute-start(f32[8,128]{1,0:T(8,128)S(1)} %buckets.1.b0_ref), channel_id=1, source_target_pairs={{0,64},{32,96},{64,0},{96,32},{1,65},{33,97},{65,1},{97,33},{2,66}... | collective-permute-start | bytes 12296 | tf_op jit(solution)/shard_map/ppermute | solution.py:369
  69.6 6.9 %collective-permute-start.8 = (f32[8,128]{1,0:T(8,128)S(1)}, f32[8,128]{1,0:T(8,128)S(1)}, u32[]{:S(2)}, u32[]{:S(2)}) collective-permute-start(f32[8,128]{1,0:T(8,128)S(1)} %buckets.1.b0_ref), channel_id=1, source_target_pairs={{0,96},{32,64},{64,32},{96,0},{1,97},{33,65},{65,33},{97,1},{2,98}... | collective-permute-start | bytes 12296 | tf_op jit(solution)/shard_map/ppermute | solution.py:369
  70.4 6.1 %collective-permute-start.7 = (f32[8,128]{1,0:T(8,128)S(1)}, f32[8,128]{1,0:T(8,128)S(1)}, u32[]{:S(2)}, u32[]{:S(2)}) collective-permute-start(f32[8,128]{1,0:T(8,128)S(1)} %buckets.1.b0_ref), channel_id=1, source_target_pairs={{0,32},{32,0},{64,96},{96,64},{1,33},{33,1},{65,97},{97,65},{2,34}... | collective-permute-start | bytes 12296 | tf_op jit(solution)/shard_map/ppermute | solution.py:369
  77.2 17.0 %all-to-all-start.1 = ((bf16[16,208,128]{2,1,0:T(8,128)(2,1)}), bf16[16,208,128]{2,1,0:T(8,128)(2,1)S(1)}, u32[]{:S(2)}, u32[]{:S(2)}) async-start(bf16[16,208,128]{2,1,0:T(8,128)(2,1)} %bias.1), calls=%async_computation.1 | async-start | bytes 1703936 | tf_op jit(solution)/shard_map/all_to_all | solution.py:474
  94.1 3.8 %collective-permute-start.10 = (f32[4,20]{1,0:T(4,128)S(1)}, f32[4,20]{1,0:T(4,128)S(1)}, u32[]{:S(2)}, u32[]{:S(2)}) collective-permute-start(f32[4,20]{1,0:T(4,128)S(1)} %bitcast.11), channel_id=1, source_target_pairs={{0,1},{1,0},{2,3},{3,2},{4,5},{5,4},{6,7},{7,6},{8,9},{9,8},{10,11... | collective-permute-start | bytes 968 | tf_op jit(solution)/shard_map/ppermute | solution.py:369

commit v6 on v5

--- a/solution.py
+++ b/solution.py
@@ -236,7 +236,7 @@
     def block(n, at):
         return pl.ds(pl.multiple_of(SUPER * n + at, ROWS), ROWS)
 
-    @pl.loop(0, GROUPS)
+    @pl.loop(0, GROUPS, unroll=8)
     def _(n):
         line[block(n, k_own), :] = own_ref[n, :ROWS]
         line[block(n, k_x), :] = kvx_ref[n]
@@ -251,7 +251,7 @@
             lhs[n, pl.ds(pl.multiple_of(at + TALL, ROWS), ROWS), :] = jnp.where(left[:ROWS], zero, qg)
         qgt[n] = (lhs[n, pl.ds(0, TALL), :] + lhs[n, pl.ds(TALL, TALL), :]).T
 
-    @pl.loop(0, len(SLABS) + 1)
+    @pl.loop(0, len(SLABS) + 1, unroll=7)
     def _(e):
         biasacc[e] = jnp.zeros((TALL, CHUNK), jnp.float32)
 
@@ -312,7 +312,7 @@
             weigh(k + 1, score[now], weight[now])
             scores(k + 2, score[later])
 
-    @pl.loop(0, GROUPS)
+    @pl.loop(0, GROUPS, unroll=4)
     def _(n):
         for c in range(3):
             line[chunk(3 * n + c), :] = dkv[3 * n + c].astype(jnp.bfloat16).T
@@ -326,7 +326,7 @@
 
 
 def combine_kernel(mine_ref, got_qo_ref, dkv_ref, got_dkv_ref, out_ref):
-    @pl.loop(0, GROUPS)
+    @pl.loop(0, GROUPS, unroll=4)
     def _(n):
         qo = mine_ref[n] + got_qo_ref[n].astype(jnp.float32)
         out_ref[n, :ROWS] = qo.astype(jnp.bfloat16)
@@ -397,8 +397,8 @@
     )(first_row.reshape(1), doc_ids.reshape(96, 128), qkv.transpose(1, 0, 2), grad_out)
     own = lax.all_to_all(packed, ("y", "z"), 0, 0, tiled=True)
     kv_own, qg_own = own[:, :ROWS], own[:, ROWS:]
+    qg_x = swap(qg_own, "x", (3, 2, 1, 0))
     kv_x = swap(kv_own, "x", (1, 0, 3, 2))
-    qg_x = swap(qg_own, "x", (3, 2, 1, 0))
     kv_core = swap(kv_own, "core", (1, 0))
     table_row = lax.dynamic_slice_in_dim(rab, y * 4 + z, 1, 0)[0]
     table, starts, scales, plan = pl.pallas_call(

time: 98.9 us -> 95.7 us (0.968)
  starting transfers between devices: 23.6 us -> 21.2 us
    ppermute x11, starting transfers between devices: 20 us -> 17.6 us  [swap(): return lax.ppermute(v, axis, [(i, p) for i, p in enumerate(partner)])]
  transfers between devices with their start and end apart: 12 -> 12, of which waited for: 7 -> 7; matrix products, arithmetic and copies ran while one was open for 0% -> 0% of each run, Pallas kernels for 8% -> 9%
where the time goes in v6:
time: 95.7 us; the launch traced here: 95.9 us
  Pallas kernels  29.4 us (31%)
  blocking collectives  22 us (23%)
  waiting for transfers between devices  21.6 us (23%)
  starting transfers between devices  21.2 us (22%)
    all_to_all x1, blocking collectives, per_device(): own = lax.all_to_all(packed, ('y', 'z'), 0, 0, tiled=True)  22 us
    pallas_call x1, Pallas kernels, per_device(): pl.pallas_call(main_kernel, out_shape=[double, double, jax.ShapeDtypeStru...  18.1 us
    ppermute x11, starting transfers between devices, swap(): return lax.ppermute(v, axis, [(i, p) for i, p in enumerate(partner)])  17.6 us
    all_to_all x1, waiting for transfers between devices, per_device(): results = lax.all_to_all(results, ('y', 'z'), 0, 0, tiled=True)  13.3 us
    ppermute x11, waiting for transfers between devices, swap(): return lax.ppermute(v, axis, [(i, p) for i, p in enumerate(partner)])  8.27 us
    pallas_call x1, Pallas kernels, per_device(): pl.pallas_call(table_kernel, out_shape=(slabs, jax.ShapeDtypeStruct((GROU...  4.39 us
    all_to_all x1, starting transfers between devices, per_device(): results = lax.all_to_all(results, ('y', 'z'), 0, 0, tiled=True)  3.64 us
    pallas_call x1, Pallas kernels, per_device(): pl.pallas_call(pack_kernel, out_shape=(double, jax.ShapeDtypeStruct((DOCS...  2.37 us
  transfers between devices with their start and end apart: 12, of which 7 were waited for; matrix products, arithmetic and copies ran while one was open for 0% of the time, Pallas kernels for 9%

profile of v6, /device:TPU:1, one launch (start us, length us, event | category | flops | bytes accessed | tf_op | source)
XLA Modules:
  0.0 95.9 jit_solution(14178648007044404962)
XLA Ops:
  0.6 0.0 copy-start
  0.7 2.4 %pack.1 = (bf16[16,192,128]{2,1,0:T(8,128)(2,1)}, s32[8]{0:T(128)}) custom-call(s32[1]{0:T(128)} %bitcast.2.where_ref, s32[96,128]{1,0:T(8,128)} %bitcast.10, bf16[3,96,1024]{2,1,0:T(8,128)(2,1)} %bitcast.9, bf16[96,1024]{1,0:T(8,128)(2,1)} %g_in.1), custom_call_target="tpu_custom_call" | custom-call | tf_op jit(solution)/shard_map/pack/pallas_call | solution.py:384
  3.0 0.0 copy-start.1
  3.0 22.0 %all_to_all.10.own_ref = bf16[16,192,128]{2,1,0:T(8,128)(2,1)S(1)} all-to-all(bf16[16,192,128]{2,1,0:T(8,128)(2,1)} %get-tuple-element.22), channel_id=1, replica_groups=mesh['x'=4,'y'=4,'z'=4,'core'=2] {'y','z'}, dimensions={0} | all-to-all | bytes 1572864 | tf_op jit(solution)/shard_map/all_to_all | solution.py:398
  25.0 0.1 fusion
  25.1 2.6 %collective-permute-start.1 = (bf16[16,96,128]{2,1,0:T(8,128)(2,1)S(1)}, bf16[16,96,128]{2,1,0:T(8,128)(2,1)S(1)}, u32[]{:S(2)}, u32[]{:S(2)}) collective-permute-start(bf16[16,96,128]{2,1,0:T(8,128)(2,1)S(1)} %get-tuple-element.41), channel_id=1, source_target_pairs={{0,96},{32,64},{64,32},{96,0},{1,97},{33,65},{65,33},{97,1},{2,98}... | collective-permute-start | bytes 1179656 | tf_op jit(solution)/shard_map/ppermute | solution.py:369
  27.6 0.0 collective-permute-start
  27.6 0.1 pad_add_fusion.where_ref
  27.7 0.0 copy-done
  27.7 0.0 copy-done.1
  27.7 4.4 %table.1 = (f32[28,192,128]{2,1,0:T(8,128)S(1)}, s32[16,192,128]{2,1,0:T(8,128)S(1)}, f32[16,192,128]{2,1,0:T(8,128)S(1)}, s32[1281]{0:T(1024)S(1)}) custom-call(s32[2]{0:T(128)S(1)} %pad_add_fusion.where_ref, f32[20]{0:T(128)S(1)} %dynamic-slice_bitcast_fusion.rab_ref, s32[8]{0:T(128)S(1)} %copy-done.1), custom_call_target="tpu_custom_call" | custom-call | tf_op jit(solution)/shard_map/table/pallas_call | solution.py:404
  32.1 2.6 %collective-permute-start.2 = (bf16[16,96,128]{2,1,0:T(8,128)(2,1)S(1)}, bf16[16,96,128]{2,1,0:T(8,128)(2,1)S(1)}, u32[]{:S(2)}, u32[]{:S(2)}) collective-permute-start(bf16[16,96,128]{2,1,0:T(8,128)(2,1)S(1)} %get-tuple-element.42), channel_id=1, source_target_pairs={{0,1},{1,0},{2,3},{3,2},{4,5},{5,4},{6,7},{7,6},{8,9},{9,8},{10,11... | collective-permute-start | bytes 1179656 | tf_op jit(solution)/shard_map/ppermute | solution.py:369
  34.7 0.5 collective-permute-done.1.qgx_ref
  35.2 1.0 %collective-permute-done.kvx_ref = bf16[16,96,128]{2,1,0:T(8,128)(2,1)S(1)} collective-permute-done((bf16[16,96,128]{2,1,0:T(8,128)(2,1)S(1)}, bf16[16,96,128]{2,1,0:T(8,128)(2,1)S(1)}, u32[]{:S(2)}, u32[]{:S(2)}) %collective-permute-start) | collective-permute-done | bytes 393248 | tf_op jit(solution)/shard_map/ppermute | solution.py:369
  36.2 2.9 %collective-permute-start.3 = (bf16[16,96,128]{2,1,0:T(8,128)(2,1)S(1)}, bf16[16,96,128]{2,1,0:T(8,128)(2,1)S(1)}, u32[]{:S(2)}, u32[]{:S(2)}) collective-permute-start(bf16[16,96,128]{2,1,0:T(8,128)(2,1)S(1)} %collective-permute-done.kvx_ref), channel_id=1, source_target_pairs={{0,1},{1,0},{2,3},{3,2},{4,5},{5,4},{6,7},{7,6},{8,9},{9,8},{10,11... | collective-permute-start | bytes 1179656 | tf_op jit(solution)/shard_map/ppermute | solution.py:369
  39.2 0.0 collective-permute-done.2.kvc_ref
  39.2 1.3 %collective-permute-done.3.kvxc_ref = bf16[16,96,128]{2,1,0:T(8,128)(2,1)S(1)} collective-permute-done((bf16[16,96,128]{2,1,0:T(8,128)(2,1)S(1)}, bf16[16,96,128]{2,1,0:T(8,128)(2,1)S(1)}, u32[]{:S(2)}, u32[]{:S(2)}) %collective-permute-start.3) | collective-permute-done | bytes 393248 | tf_op jit(solution)/shard_map/ppermute | solution.py:369
  40.5 18.1 %attend.1 = (bf16[16,192,128]{2,1,0:T(8,128)(2,1)S(1)}, bf16[16,192,128]{2,1,0:T(8,128)(2,1)S(1)}, f32[16,96,128]{2,1,0:T(8,128)S(1)}, bf16[16,96,128]{2,1,0:T(8,128)(2,1)S(1)}, f32[28,192,128]{2,1,0:T(8,128)S(1)}) custom-call(s32[2]{0:T(128)S(1)} %pad_add_fusion.where_ref, s32[1281]{0:T(1024)S(1)} %get-tuple-element.28.plan_ref, ...), custom_call_target="tpu_custom_call" | custom-call | tf_op jit(solution)/shard_map/attend/pallas_call | solution.py:422
  58.6 1.6 %collective-permute-start.5 = (bf16[16,192,128]{2,1,0:T(8,128)(2,1)S(1)}, bf16[16,192,128]{2,1,0:T(8,128)(2,1)S(1)}, u32[]{:S(2)}, u32[]{:S(2)}) collective-permute-start(bf16[16,192,128]{2,1,0:T(8,128)(2,1)S(1)} %get-tuple-element.37), channel_id=1, source_target_pairs={{0,1},{1,0},{2,3},{3,2},{4,5},{5,4},{6,7},{7,6},{8,9},{9,8},{10,11... | collective-permute-start | bytes 2359304 | tf_op jit(solution)/shard_map/ppermute | solution.py:369
  60.2 1.2 %collective-permute-start.4 = (bf16[16,96,128]{2,1,0:T(8,128)(2,1)S(1)}, bf16[16,96,128]{2,1,0:T(8,128)(2,1)S(1)}, u32[]{:S(2)}, u32[]{:S(2)}) collective-permute-start(bf16[16,96,128]{2,1,0:T(8,128)(2,1)S(1)} %get-tuple-element.35), channel_id=1, source_target_pairs={{0,96},{32,64},{64,32},{96,0},{1,97},{33,65},{65,33},{97,1},{2,98}... | collective-permute-start | bytes 1179656 | tf_op jit(solution)/shard_map/ppermute | solution.py:369
  61.4 0.7 collective-permute-done.5
  62.1 0.2 convert_add_fusion.dkv_ref
  62.3 0.1 slice.37
  62.4 0.1 collective-permute-start.6
  62.5 1.7 %buckets.1.b0_ref = f32[8,128]{1,0:T(8,128)S(1)} custom-call(s32[2]{0:T(128)S(1)} %pad_add_fusion.where_ref, f32[28,192,128]{2,1,0:T(8,128)S(1)} %get-tuple-element.38.sums_ref), custom_call_target="tpu_custom_call" | custom-call | tf_op jit(solution)/shard_map/buckets/pallas_call | solution.py:444
  64.1 2.5 %collective-permute-start.9 = (f32[8,128]{1,0:T(8,128)S(1)}, f32[8,128]{1,0:T(8,128)S(1)}, u32[]{:S(2)}, u32[]{:S(2)}) collective-permute-start(f32[8,128]{1,0:T(8,128)S(1)} %buckets.1.b0_ref), channel_id=1, source_target_pairs={{0,64},{32,96},{64,0},{96,32},{1,65},{33,97},{65,1},{97,33},{2,66}... | collective-permute-start | bytes 12296 | tf_op jit(solution)/shard_map/ppermute | solution.py:369
  66.6 1.5 %collective-permute-start.8 = (f32[8,128]{1,0:T(8,128)S(1)}, f32[8,128]{1,0:T(8,128)S(1)}, u32[]{:S(2)}, u32[]{:S(2)}) collective-permute-start(f32[8,128]{1,0:T(8,128)S(1)} %buckets.1.b0_ref), channel_id=1, source_target_pairs={{0,96},{32,64},{64,32},{96,0},{1,97},{33,65},{65,33},{97,1},{2,98}... | collective-permute-start | bytes 12296 | tf_op jit(solution)/shard_map/ppermute | solution.py:369
  68.1 0.0 collective-permute-start.7
  68.1 4.0 %collective-permute-done.4.got_qo_ref = bf16[16,96,128]{2,1,0:T(8,128)(2,1)S(1)} collective-permute-done((bf16[16,96,128]{2,1,0:T(8,128)(2,1)S(1)}, bf16[16,96,128]{2,1,0:T(8,128)(2,1)S(1)}, u32[]{:S(2)}, u32[]{:S(2)}) %collective-permute-start.4) | collective-permute-done | bytes 393248 | tf_op jit(solution)/shard_map/ppermute | solution.py:369
  72.1 0.7 collective-permute-done.6.got_dkv_ref
  72.8 1.1 %combine.1.in_ref = bf16[16,208,128]{2,1,0:T(8,128)(2,1)} custom-call(f32[16,96,128]{2,1,0:T(8,128)S(1)} %get-tuple-element.34.mine_ref, bf16[16,96,128]{2,1,0:T(8,128)(2,1)S(1)} %collective-permute-done.4.got_qo_ref, f32[16,192,128]{2,1,0:T(8,128)S(1)} %convert_add_fusion.dkv_ref, bf16[16,96,128]{2,1,0:T(8,128)(2,1)S(1)} %collective-permute-done.6.got_dkv_ref), custom_call_target="tpu_custom_call" | custom-call | bytes 10000000 | tf_op jit(solution)/shard_map/combine/pallas_call | solution.py:455
  73.8 0.0 collective-permute-done.9.b3_ref
  73.8 0.0 collective-permute-done.8.b2_ref
  73.9 0.0 collective-permute-done.7.b1_ref
  73.9 0.7 bias.1
  74.5 3.6 %all-to-all-start.1 = ((bf16[16,208,128]{2,1,0:T(8,128)(2,1)}), bf16[16,208,128]{2,1,0:T(8,128)(2,1)S(1)}, u32[]{:S(2)}, u32[]{:S(2)}) async-start(bf16[16,208,128]{2,1,0:T(8,128)(2,1)} %bias.1), calls=%async_computation.1 | async-start | bytes 1703936 | tf_op jit(solution)/shard_map/all_to_all | solution.py:474
  78.2 13.3 %all-to-all-done.1.in_ref = bf16[16,208,128]{2,1,0:T(8,128)(2,1)S(1)} async-done(((bf16[16,208,128]{2,1,0:T(8,128)(2,1)}), bf16[16,208,128]{2,1,0:T(8,128)(2,1)S(1)}, u32[]{:S(2)}, u32[]{:S(2)}) %all-to-all-start.1) | async-done | bytes 852000 | tf_op jit(solution)/shard_map/all_to_all | solution.py:474
  91.5 2.7 %collective-permute-start.10 = (f32[4,20]{1,0:T(4,128)S(1)}, f32[4,20]{1,0:T(4,128)S(1)}, u32[]{:S(2)}, u32[]{:S(2)}) collective-permute-start(f32[4,20]{1,0:T(4,128)S(1)} %bitcast.11), channel_id=1, source_target_pairs={{0,1},{1,0},{2,3},{3,2},{4,5},{5,4},{6,7},{7,6},{8,9},{9,8},{10,11... | collective-permute-start | bytes 968 | tf_op jit(solution)/shard_map/ppermute | solution.py:369
  94.2 1.2 %unpack.1 = (bf16[96,1024]{1,0:T(8,128)(2,1)}, bf16[3,96,1024]{2,1,0:T(8,128)(2,1)}) custom-call(bf16[16,208,128]{2,1,0:T(8,128)(2,1)S(1)} %all-to-all-done.1.in_ref), custom_call_target="tpu_custom_call" | custom-call | tf_op jit(solution)/shard_map/unpack/pallas_call | solution.py:478
  95.3 0.0 collective-permute-done.10
  95.4 0.6 add.41
  (3 shorter events, 0.0 us)
Async XLA Ops:
  0.6 27.1 %copy-start = (f32[16,20]{1,0:T(8,128)S(1)}, f32[16,20]{1,0:T(8,128)}, u32[]{:S(2)}) copy-start(f32[16,20]{1,0:T(8,128)} %param.6) | copy-start | bytes 3844
  3.0 24.7 %copy-start.1 = (s32[8]{0:T(128)S(1)}, s32[8]{0:T(128)}, u32[]{:S(2)}) copy-start(s32[8]{0:T(128)} %get-tuple-element.23.bounds_ref) | copy-start | bytes 100
  25.1 10.2 %collective-permute-start.1 = (bf16[16,96,128]{2,1,0:T(8,128)(2,1)S(1)}, bf16[16,96,128]{2,1,0:T(8,128)(2,1)S(1)}, u32[]{:S(2)}, u32[]{:S(2)}) collective-permute-start(bf16[16,96,128]{2,1,0:T(8,128)(2,1)S(1)} %get-tuple-element.41), channel_id=1, source_target_pairs={{0,96},{32,64},{64,32},{96,0},{1,97},{33,65},{65,33},{97,1},{2,98}... | collective-permute-start | bytes 1179656 | tf_op jit(solution)/shard_map/ppermute | solution.py:369
  27.6 8.6 %collective-permute-start = (bf16[16,96,128]{2,1,0:T(8,128)(2,1)S(1)}, bf16[16,96,128]{2,1,0:T(8,128)(2,1)S(1)}, u32[]{:S(2)}, u32[]{:S(2)}) collective-permute-start(bf16[16,96,128]{2,1,0:T(8,128)(2,1)S(1)} %get-tuple-element.42), channel_id=1, source_target_pairs={{0,32},{32,0},{64,96},{96,64},{1,33},{33,1},{65,97},{97,65},{2,34}... | collective-permute-start | bytes 1179656 | tf_op jit(solution)/shard_map/ppermute | solution.py:369
  32.1 7.0 %collective-permute-start.2 = (bf16[16,96,128]{2,1,0:T(8,128)(2,1)S(1)}, bf16[16,96,128]{2,1,0:T(8,128)(2,1)S(1)}, u32[]{:S(2)}, u32[]{:S(2)}) collective-permute-start(bf16[16,96,128]{2,1,0:T(8,128)(2,1)S(1)} %get-tuple-element.42), channel_id=1, source_target_pairs={{0,1},{1,0},{2,3},{3,2},{4,5},{5,4},{6,7},{7,6},{8,9},{9,8},{10,11... | collective-permute-start | bytes 1179656 | tf_op jit(solution)/shard_map/ppermute | solution.py:369
  36.2 4.3 %collective-permute-start.3 = (bf16[16,96,128]{2,1,0:T(8,128)(2,1)S(1)}, bf16[16,96,128]{2,1,0:T(8,128)(2,1)S(1)}, u32[]{:S(2)}, u32[]{:S(2)}) collective-permute-start(bf16[16,96,128]{2,1,0:T(8,128)(2,1)S(1)} %collective-permute-done.kvx_ref), channel_id=1, source_target_pairs={{0,1},{1,0},{2,3},{3,2},{4,5},{5,4},{6,7},{7,6},{8,9},{9,8},{10,11... | collective-permute-start | bytes 1179656 | tf_op jit(solution)/shard_map/ppermute | solution.py:369
  58.6 3.5 %collective-permute-start.5 = (bf16[16,192,128]{2,1,0:T(8,128)(2,1)S(1)}, bf16[16,192,128]{2,1,0:T(8,128)(2,1)S(1)}, u32[]{:S(2)}, u32[]{:S(2)}) collective-permute-start(bf16[16,192,128]{2,1,0:T(8,128)(2,1)S(1)} %get-tuple-element.37), channel_id=1, source_target_pairs={{0,1},{1,0},{2,3},{3,2},{4,5},{5,4},{6,7},{7,6},{8,9},{9,8},{10,11... | collective-permute-start | bytes 2359304 | tf_op jit(solution)/shard_map/ppermute | solution.py:369
  60.2 11.9 %collective-permute-start.4 = (bf16[16,96,128]{2,1,0:T(8,128)(2,1)S(1)}, bf16[16,96,128]{2,1,0:T(8,128)(2,1)S(1)}, u32[]{:S(2)}, u32[]{:S(2)}) collective-permute-start(bf16[16,96,128]{2,1,0:T(8,128)(2,1)S(1)} %get-tuple-element.35), channel_id=1, source_target_pairs={{0,96},{32,64},{64,32},{96,0},{1,97},{33,65},{65,33},{97,1},{2,98}... | collective-permute-start | bytes 1179656 | tf_op jit(solution)/shard_map/ppermute | solution.py:369
  62.4 10.4 %collective-permute-start.6 = (bf16[16,96,128]{2,1,0:T(8,128)(2,1)S(1)}, bf16[16,96,128]{2,1,0:T(8,128)(2,1)S(1)}, u32[]{:S(2)}, u32[]{:S(2)}) collective-permute-start(bf16[16,96,128]{2,1,0:T(8,128)(2,1)S(1)} %slice.37), channel_id=1, source_target_pairs={{0,32},{32,0},{64,96},{96,64},{1,33},{33,1},{65,97},{97,65},{2,34}... | collective-permute-start | bytes 1179656 | tf_op jit(solution)/shard_map/ppermute | solution.py:369
  64.1 9.7 %collective-permute-start.9 = (f32[8,128]{1,0:T(8,128)S(1)}, f32[8,128]{1,0:T(8,128)S(1)}, u32[]{:S(2)}, u32[]{:S(2)}) collective-permute-start(f32[8,128]{1,0:T(8,128)S(1)} %buckets.1.b0_ref), channel_id=1, source_target_pairs={{0,64},{32,96},{64,0},{96,32},{1,65},{33,97},{65,1},{97,33},{2,66}... | collective-permute-start | bytes 12296 | tf_op jit(solution)/shard_map/ppermute | solution.py:369
  66.6 7.2 %collective-permute-start.8 = (f32[8,128]{1,0:T(8,128)S(1)}, f32[8,128]{1,0:T(8,128)S(1)}, u32[]{:S(2)}, u32[]{:S(2)}) collective-permute-start(f32[8,128]{1,0:T(8,128)S(1)} %buckets.1.b0_ref), channel_id=1, source_target_pairs={{0,96},{32,64},{64,32},{96,0},{1,97},{33,65},{65,33},{97,1},{2,98}... | collective-permute-start | bytes 12296 | tf_op jit(solution)/shard_map/ppermute | solution.py:369
  68.1 5.8 %collective-permute-start.7 = (f32[8,128]{1,0:T(8,128)S(1)}, f32[8,128]{1,0:T(8,128)S(1)}, u32[]{:S(2)}, u32[]{:S(2)}) collective-permute-start(f32[8,128]{1,0:T(8,128)S(1)} %buckets.1.b0_ref), channel_id=1, source_target_pairs={{0,32},{32,0},{64,96},{96,64},{1,33},{33,1},{65,97},{97,65},{2,34}... | collective-permute-start | bytes 12296 | tf_op jit(solution)/shard_map/ppermute | solution.py:369
  74.5 17.0 %all-to-all-start.1 = ((bf16[16,208,128]{2,1,0:T(8,128)(2,1)}), bf16[16,208,128]{2,1,0:T(8,128)(2,1)S(1)}, u32[]{:S(2)}, u32[]{:S(2)}) async-start(bf16[16,208,128]{2,1,0:T(8,128)(2,1)} %bias.1), calls=%async_computation.1 | async-start | bytes 1703936 | tf_op jit(solution)/shard_map/all_to_all | solution.py:474
  91.5 3.8 %collective-permute-start.10 = (f32[4,20]{1,0:T(4,128)S(1)}, f32[4,20]{1,0:T(4,128)S(1)}, u32[]{:S(2)}, u32[]{:S(2)}) collective-permute-start(f32[4,20]{1,0:T(4,128)S(1)} %bitcast.11), channel_id=1, source_target_pairs={{0,1},{1,0},{2,3},{3,2},{4,5},{5,4},{6,7},{7,6},{8,9},{9,8},{10,11... | collective-permute-start | bytes 968 | tf_op jit(solution)/shard_map/ppermute | solution.py:369

commit v7 on v6

--- a/solution.py
+++ b/solution.py
@@ -268,9 +268,10 @@
 
     def scores(k, s):
         g, chunks, slabs = entry(k)
-        for cols, n in zip(halves, chunks):
-            s[:, cols] = lax.dot_general(
-                lhs[g], line[chunk(n), :], NT, preferred_element_type=jnp.float32
+        keyvals = jnp.concatenate([line[chunk(n), :] for n in chunks], axis=0)
+        for rows in (pl.ds(0, TALL), pl.ds(TALL, TALL)):
+            s[rows, :] = lax.dot_general(
+                lhs[g, rows, :], keyvals, NT, preferred_element_type=jnp.float32
             )
 
     def weigh(k, s, w_out):

time: 95.7 us -> 96.9 us (1.013)
  starting transfers between devices: 21.2 us -> 22.5 us
    ppermute x11, starting transfers between devices: 17.6 us -> 18.9 us  [swap(): return lax.ppermute(v, axis, [(i, p) for i, p in enumerate(partner)])]
  transfers between devices with their start and end apart: 12 -> 12, of which waited for: 7 -> 7; matrix products, arithmetic and copies ran while one was open for 0% -> 0% of each run, Pallas kernels for 9% -> 8%
where the time goes in v7:
time: 96.9 us; the launch traced here: 96.7 us
  Pallas kernels  28.9 us (30%)
  starting transfers between devices  22.5 us (23%)
  blocking collectives  22 us (23%)
  waiting for transfers between devices  21.5 us (22%)
    all_to_all x1, blocking collectives, per_device(): own = lax.all_to_all(packed, ('y', 'z'), 0, 0, tiled=True)  22 us
    ppermute x11, starting transfers between devices, swap(): return lax.ppermute(v, axis, [(i, p) for i, p in enumerate(partner)])  18.9 us
    pallas_call x1, Pallas kernels, per_device(): pl.pallas_call(main_kernel, out_shape=[double, double, jax.ShapeDtypeStru...  17.7 us
    all_to_all x1, waiting for transfers between devices, per_device(): results = lax.all_to_all(results, ('y', 'z'), 0, 0, tiled=True)  13.3 us
    ppermute x11, waiting for transfers between devices, swap(): return lax.ppermute(v, axis, [(i, p) for i, p in enumerate(partner)])  8.2 us
    pallas_call x1, Pallas kernels, per_device(): pl.pallas_call(table_kernel, out_shape=(slabs, jax.ShapeDtypeStruct((GROU...  4.27 us
    all_to_all x1, starting transfers between devices, per_device(): results = lax.all_to_all(results, ('y', 'z'), 0, 0, tiled=True)  3.64 us
    pallas_call x1, Pallas kernels, per_device(): pl.pallas_call(pack_kernel, out_shape=(double, jax.ShapeDtypeStruct((DOCS...  2.37 us
  transfers between devices with their start and end apart: 12, of which 7 were waited for; matrix products, arithmetic and copies ran while one was open for 0% of the time, Pallas kernels for 8%

profile of v7, /device:TPU:1, one launch (start us, length us, event | category | flops | bytes accessed | tf_op | source)
XLA Modules:
  0.0 96.7 jit_solution(8781622069064424607)
XLA Ops:
  0.6 0.0 copy-start
  0.7 2.4 %pack.1 = (bf16[16,192,128]{2,1,0:T(8,128)(2,1)}, s32[8]{0:T(128)}) custom-call(s32[1]{0:T(128)} %bitcast.2.where_ref, s32[96,128]{1,0:T(8,128)} %bitcast.10, bf16[3,96,1024]{2,1,0:T(8,128)(2,1)} %bitcast.9, bf16[96,1024]{1,0:T(8,128)(2,1)} %g_in.1), custom_call_target="tpu_custom_call" | custom-call | tf_op jit(solution)/shard_map/pack/pallas_call | solution.py:385
  3.0 0.0 copy-start.1
  3.0 22.0 %all_to_all.10.own_ref = bf16[16,192,128]{2,1,0:T(8,128)(2,1)S(1)} all-to-all(bf16[16,192,128]{2,1,0:T(8,128)(2,1)} %get-tuple-element.22), channel_id=1, replica_groups=mesh['x'=4,'y'=4,'z'=4,'core'=2] {'y','z'}, dimensions={0} | all-to-all | bytes 1572864 | tf_op jit(solution)/shard_map/all_to_all | solution.py:399
  25.0 0.1 fusion
  25.1 2.6 %collective-permute-start.1 = (bf16[16,96,128]{2,1,0:T(8,128)(2,1)S(1)}, bf16[16,96,128]{2,1,0:T(8,128)(2,1)S(1)}, u32[]{:S(2)}, u32[]{:S(2)}) collective-permute-start(bf16[16,96,128]{2,1,0:T(8,128)(2,1)S(1)} %get-tuple-element.41), channel_id=1, source_target_pairs={{0,96},{32,64},{64,32},{96,0},{1,97},{33,65},{65,33},{97,1},{2,98}... | collective-permute-start | bytes 1179656 | tf_op jit(solution)/shard_map/ppermute | solution.py:370
  27.6 0.0 collective-permute-start
  27.6 0.1 pad_add_fusion.where_ref
  27.7 0.0 copy-done
  27.7 0.0 copy-done.1
  27.7 4.3 %table.1 = (f32[28,192,128]{2,1,0:T(8,128)S(1)}, s32[16,192,128]{2,1,0:T(8,128)S(1)}, f32[16,192,128]{2,1,0:T(8,128)S(1)}, s32[1281]{0:T(1024)S(1)}) custom-call(s32[2]{0:T(128)S(1)} %pad_add_fusion.where_ref, f32[20]{0:T(128)S(1)} %dynamic-slice_bitcast_fusion.rab_ref, s32[8]{0:T(128)S(1)} %copy-done.1), custom_call_target="tpu_custom_call" | custom-call | tf_op jit(solution)/shard_map/table/pallas_call | solution.py:405
  32.0 2.8 %collective-permute-start.2 = (bf16[16,96,128]{2,1,0:T(8,128)(2,1)S(1)}, bf16[16,96,128]{2,1,0:T(8,128)(2,1)S(1)}, u32[]{:S(2)}, u32[]{:S(2)}) collective-permute-start(bf16[16,96,128]{2,1,0:T(8,128)(2,1)S(1)} %get-tuple-element.42), channel_id=1, source_target_pairs={{0,1},{1,0},{2,3},{3,2},{4,5},{5,4},{6,7},{7,6},{8,9},{9,8},{10,11... | collective-permute-start | bytes 1179656 | tf_op jit(solution)/shard_map/ppermute | solution.py:370
  34.8 0.5 collective-permute-done.1.qgx_ref
  35.2 1.0 %collective-permute-done.kvx_ref = bf16[16,96,128]{2,1,0:T(8,128)(2,1)S(1)} collective-permute-done((bf16[16,96,128]{2,1,0:T(8,128)(2,1)S(1)}, bf16[16,96,128]{2,1,0:T(8,128)(2,1)S(1)}, u32[]{:S(2)}, u32[]{:S(2)}) %collective-permute-start) | collective-permute-done | bytes 393248 | tf_op jit(solution)/shard_map/ppermute | solution.py:370
  36.2 2.9 %collective-permute-start.3 = (bf16[16,96,128]{2,1,0:T(8,128)(2,1)S(1)}, bf16[16,96,128]{2,1,0:T(8,128)(2,1)S(1)}, u32[]{:S(2)}, u32[]{:S(2)}) collective-permute-start(bf16[16,96,128]{2,1,0:T(8,128)(2,1)S(1)} %collective-permute-done.kvx_ref), channel_id=1, source_target_pairs={{0,1},{1,0},{2,3},{3,2},{4,5},{5,4},{6,7},{7,6},{8,9},{9,8},{10,11... | collective-permute-start | bytes 1179656 | tf_op jit(solution)/shard_map/ppermute | solution.py:370
  39.2 0.0 collective-permute-done.2.kvc_ref
  39.2 1.3 %collective-permute-done.3.kvxc_ref = bf16[16,96,128]{2,1,0:T(8,128)(2,1)S(1)} collective-permute-done((bf16[16,96,128]{2,1,0:T(8,128)(2,1)S(1)}, bf16[16,96,128]{2,1,0:T(8,128)(2,1)S(1)}, u32[]{:S(2)}, u32[]{:S(2)}) %collective-permute-start.3) | collective-permute-done | bytes 393248 | tf_op jit(solution)/shard_map/ppermute | solution.py:370
  40.5 17.7 %attend.1 = (bf16[16,192,128]{2,1,0:T(8,128)(2,1)S(1)}, bf16[16,192,128]{2,1,0:T(8,128)(2,1)S(1)}, f32[16,96,128]{2,1,0:T(8,128)S(1)}, bf16[16,96,128]{2,1,0:T(8,128)(2,1)S(1)}, f32[28,192,128]{2,1,0:T(8,128)S(1)}) custom-call(s32[2]{0:T(128)S(1)} %pad_add_fusion.where_ref, s32[1281]{0:T(1024)S(1)} %get-tuple-element.28.plan_ref, ...), custom_call_target="tpu_custom_call" | custom-call | tf_op jit(solution)/shard_map/attend/pallas_call | solution.py:423
  58.2 2.7 %collective-permute-start.5 = (bf16[16,192,128]{2,1,0:T(8,128)(2,1)S(1)}, bf16[16,192,128]{2,1,0:T(8,128)(2,1)S(1)}, u32[]{:S(2)}, u32[]{:S(2)}) collective-permute-start(bf16[16,192,128]{2,1,0:T(8,128)(2,1)S(1)} %get-tuple-element.37), channel_id=1, source_target_pairs={{0,1},{1,0},{2,3},{3,2},{4,5},{5,4},{6,7},{7,6},{8,9},{9,8},{10,11... | collective-permute-start | bytes 2359304 | tf_op jit(solution)/shard_map/ppermute | solution.py:370
  60.9 1.2 %collective-permute-start.4 = (bf16[16,96,128]{2,1,0:T(8,128)(2,1)S(1)}, bf16[16,96,128]{2,1,0:T(8,128)(2,1)S(1)}, u32[]{:S(2)}, u32[]{:S(2)}) collective-permute-start(bf16[16,96,128]{2,1,0:T(8,128)(2,1)S(1)} %get-tuple-element.35), channel_id=1, source_target_pairs={{0,96},{32,64},{64,32},{96,0},{1,97},{33,65},{65,33},{97,1},{2,98}... | collective-permute-start | bytes 1179656 | tf_op jit(solution)/shard_map/ppermute | solution.py:370
  62.2 0.7 collective-permute-done.5
  62.8 0.2 convert_add_fusion.dkv_ref
  63.0 0.1 slice.37
  63.1 0.1 collective-permute-start.6
  63.2 1.7 %buckets.1.b0_ref = f32[8,128]{1,0:T(8,128)S(1)} custom-call(s32[2]{0:T(128)S(1)} %pad_add_fusion.where_ref, f32[28,192,128]{2,1,0:T(8,128)S(1)} %get-tuple-element.38.sums_ref), custom_call_target="tpu_custom_call" | custom-call | tf_op jit(solution)/shard_map/buckets/pallas_call | solution.py:445
  64.9 2.5 %collective-permute-start.9 = (f32[8,128]{1,0:T(8,128)S(1)}, f32[8,128]{1,0:T(8,128)S(1)}, u32[]{:S(2)}, u32[]{:S(2)}) collective-permute-start(f32[8,128]{1,0:T(8,128)S(1)} %buckets.1.b0_ref), channel_id=1, source_target_pairs={{0,64},{32,96},{64,0},{96,32},{1,65},{33,97},{65,1},{97,33},{2,66}... | collective-permute-start | bytes 12296 | tf_op jit(solution)/shard_map/ppermute | solution.py:370
  67.3 1.5 %collective-permute-start.8 = (f32[8,128]{1,0:T(8,128)S(1)}, f32[8,128]{1,0:T(8,128)S(1)}, u32[]{:S(2)}, u32[]{:S(2)}) collective-permute-start(f32[8,128]{1,0:T(8,128)S(1)} %buckets.1.b0_ref), channel_id=1, source_target_pairs={{0,96},{32,64},{64,32},{96,0},{1,97},{33,65},{65,33},{97,1},{2,98}... | collective-permute-start | bytes 12296 | tf_op jit(solution)/shard_map/ppermute | solution.py:370
  68.8 0.0 collective-permute-start.7
  68.8 4.0 %collective-permute-done.4.got_qo_ref = bf16[16,96,128]{2,1,0:T(8,128)(2,1)S(1)} collective-permute-done((bf16[16,96,128]{2,1,0:T(8,128)(2,1)S(1)}, bf16[16,96,128]{2,1,0:T(8,128)(2,1)S(1)}, u32[]{:S(2)}, u32[]{:S(2)}) %collective-permute-start.4) | collective-permute-done | bytes 393248 | tf_op jit(solution)/shard_map/ppermute | solution.py:370
  72.8 0.7 collective-permute-done.6.got_dkv_ref
  73.5 1.1 %combine.1.in_ref = bf16[16,208,128]{2,1,0:T(8,128)(2,1)} custom-call(f32[16,96,128]{2,1,0:T(8,128)S(1)} %get-tuple-element.34.mine_ref, bf16[16,96,128]{2,1,0:T(8,128)(2,1)S(1)} %collective-permute-done.4.got_qo_ref, f32[16,192,128]{2,1,0:T(8,128)S(1)} %convert_add_fusion.dkv_ref, bf16[16,96,128]{2,1,0:T(8,128)(2,1)S(1)} %collective-permute-done.6.got_dkv_ref), custom_call_target="tpu_custom_call" | custom-call | bytes 10000000 | tf_op jit(solution)/shard_map/combine/pallas_call | solution.py:456
  74.6 0.0 collective-permute-done.9.b3_ref
  74.6 0.0 collective-permute-done.8.b2_ref
  74.6 0.0 collective-permute-done.7.b1_ref
  74.6 0.7 bias.1
  75.3 3.6 %all-to-all-start.1 = ((bf16[16,208,128]{2,1,0:T(8,128)(2,1)}), bf16[16,208,128]{2,1,0:T(8,128)(2,1)S(1)}, u32[]{:S(2)}, u32[]{:S(2)}) async-start(bf16[16,208,128]{2,1,0:T(8,128)(2,1)} %bias.1), calls=%async_computation.1 | async-start | bytes 1703936 | tf_op jit(solution)/shard_map/all_to_all | solution.py:475
  78.9 13.3 %all-to-all-done.1.in_ref = bf16[16,208,128]{2,1,0:T(8,128)(2,1)S(1)} async-done(((bf16[16,208,128]{2,1,0:T(8,128)(2,1)}), bf16[16,208,128]{2,1,0:T(8,128)(2,1)S(1)}, u32[]{:S(2)}, u32[]{:S(2)}) %all-to-all-start.1) | async-done | bytes 852000 | tf_op jit(solution)/shard_map/all_to_all | solution.py:475
  92.2 2.7 %collective-permute-start.10 = (f32[4,20]{1,0:T(4,128)S(1)}, f32[4,20]{1,0:T(4,128)S(1)}, u32[]{:S(2)}, u32[]{:S(2)}) collective-permute-start(f32[4,20]{1,0:T(4,128)S(1)} %bitcast.11), channel_id=1, source_target_pairs={{0,1},{1,0},{2,3},{3,2},{4,5},{5,4},{6,7},{7,6},{8,9},{9,8},{10,11... | collective-permute-start | bytes 968 | tf_op jit(solution)/shard_map/ppermute | solution.py:370
  94.9 1.2 %unpack.1 = (bf16[96,1024]{1,0:T(8,128)(2,1)}, bf16[3,96,1024]{2,1,0:T(8,128)(2,1)}) custom-call(bf16[16,208,128]{2,1,0:T(8,128)(2,1)S(1)} %all-to-all-done.1.in_ref), custom_call_target="tpu_custom_call" | custom-call | tf_op jit(solution)/shard_map/unpack/pallas_call | solution.py:479
  96.1 0.0 collective-permute-done.10
  96.1 0.6 add.41
  (3 shorter events, 0.0 us)
Async XLA Ops:
  0.6 27.1 %copy-start = (f32[16,20]{1,0:T(8,128)S(1)}, f32[16,20]{1,0:T(8,128)}, u32[]{:S(2)}) copy-start(f32[16,20]{1,0:T(8,128)} %param.6) | copy-start | bytes 3844
  3.0 24.7 %copy-start.1 = (s32[8]{0:T(128)S(1)}, s32[8]{0:T(128)}, u32[]{:S(2)}) copy-start(s32[8]{0:T(128)} %get-tuple-element.23.bounds_ref) | copy-start | bytes 100
  25.1 10.2 %collective-permute-start.1 = (bf16[16,96,128]{2,1,0:T(8,128)(2,1)S(1)}, bf16[16,96,128]{2,1,0:T(8,128)(2,1)S(1)}, u32[]{:S(2)}, u32[]{:S(2)}) collective-permute-start(bf16[16,96,128]{2,1,0:T(8,128)(2,1)S(1)} %get-tuple-element.41), channel_id=1, source_target_pairs={{0,96},{32,64},{64,32},{96,0},{1,97},{33,65},{65,33},{97,1},{2,98}... | collective-permute-start | bytes 1179656 | tf_op jit(solution)/shard_map/ppermute | solution.py:370
  27.6 8.6 %collective-permute-start = (bf16[16,96,128]{2,1,0:T(8,128)(2,1)S(1)}, bf16[16,96,128]{2,1,0:T(8,128)(2,1)S(1)}, u32[]{:S(2)}, u32[]{:S(2)}) collective-permute-start(bf16[16,96,128]{2,1,0:T(8,128)(2,1)S(1)} %get-tuple-element.42), channel_id=1, source_target_pairs={{0,32},{32,0},{64,96},{96,64},{1,33},{33,1},{65,97},{97,65},{2,34}... | collective-permute-start | bytes 1179656 | tf_op jit(solution)/shard_map/ppermute | solution.py:370
  32.0 7.2 %collective-permute-start.2 = (bf16[16,96,128]{2,1,0:T(8,128)(2,1)S(1)}, bf16[16,96,128]{2,1,0:T(8,128)(2,1)S(1)}, u32[]{:S(2)}, u32[]{:S(2)}) collective-permute-start(bf16[16,96,128]{2,1,0:T(8,128)(2,1)S(1)} %get-tuple-element.42), channel_id=1, source_target_pairs={{0,1},{1,0},{2,3},{3,2},{4,5},{5,4},{6,7},{7,6},{8,9},{9,8},{10,11... | collective-permute-start | bytes 1179656 | tf_op jit(solution)/shard_map/ppermute | solution.py:370
  36.2 4.3 %collective-permute-start.3 = (bf16[16,96,128]{2,1,0:T(8,128)(2,1)S(1)}, bf16[16,96,128]{2,1,0:T(8,128)(2,1)S(1)}, u32[]{:S(2)}, u32[]{:S(2)}) collective-permute-start(bf16[16,96,128]{2,1,0:T(8,128)(2,1)S(1)} %collective-permute-done.kvx_ref), channel_id=1, source_target_pairs={{0,1},{1,0},{2,3},{3,2},{4,5},{5,4},{6,7},{7,6},{8,9},{9,8},{10,11... | collective-permute-start | bytes 1179656 | tf_op jit(solution)/shard_map/ppermute | solution.py:370
  58.2 4.6 %collective-permute-start.5 = (bf16[16,192,128]{2,1,0:T(8,128)(2,1)S(1)}, bf16[16,192,128]{2,1,0:T(8,128)(2,1)S(1)}, u32[]{:S(2)}, u32[]{:S(2)}) collective-permute-start(bf16[16,192,128]{2,1,0:T(8,128)(2,1)S(1)} %get-tuple-element.37), channel_id=1, source_target_pairs={{0,1},{1,0},{2,3},{3,2},{4,5},{5,4},{6,7},{7,6},{8,9},{9,8},{10,11... | collective-permute-start | bytes 2359304 | tf_op jit(solution)/shard_map/ppermute | solution.py:370
  60.9 11.9 %collective-permute-start.4 = (bf16[16,96,128]{2,1,0:T(8,128)(2,1)S(1)}, bf16[16,96,128]{2,1,0:T(8,128)(2,1)S(1)}, u32[]{:S(2)}, u32[]{:S(2)}) collective-permute-start(bf16[16,96,128]{2,1,0:T(8,128)(2,1)S(1)} %get-tuple-element.35), channel_id=1, source_target_pairs={{0,96},{32,64},{64,32},{96,0},{1,97},{33,65},{65,33},{97,1},{2,98}... | collective-permute-start | bytes 1179656 | tf_op jit(solution)/shard_map/ppermute | solution.py:370
  63.1 10.4 %collective-permute-start.6 = (bf16[16,96,128]{2,1,0:T(8,128)(2,1)S(1)}, bf16[16,96,128]{2,1,0:T(8,128)(2,1)S(1)}, u32[]{:S(2)}, u32[]{:S(2)}) collective-permute-start(bf16[16,96,128]{2,1,0:T(8,128)(2,1)S(1)} %slice.37), channel_id=1, source_target_pairs={{0,32},{32,0},{64,96},{96,64},{1,33},{33,1},{65,97},{97,65},{2,34}... | collective-permute-start | bytes 1179656 | tf_op jit(solution)/shard_map/ppermute | solution.py:370
  64.9 9.7 %collective-permute-start.9 = (f32[8,128]{1,0:T(8,128)S(1)}, f32[8,128]{1,0:T(8,128)S(1)}, u32[]{:S(2)}, u32[]{:S(2)}) collective-permute-start(f32[8,128]{1,0:T(8,128)S(1)} %buckets.1.b0_ref), channel_id=1, source_target_pairs={{0,64},{32,96},{64,0},{96,32},{1,65},{33,97},{65,1},{97,33},{2,66}... | collective-permute-start | bytes 12296 | tf_op jit(solution)/shard_map/ppermute | solution.py:370
  67.3 7.2 %collective-permute-start.8 = (f32[8,128]{1,0:T(8,128)S(1)}, f32[8,128]{1,0:T(8,128)S(1)}, u32[]{:S(2)}, u32[]{:S(2)}) collective-permute-start(f32[8,128]{1,0:T(8,128)S(1)} %buckets.1.b0_ref), channel_id=1, source_target_pairs={{0,96},{32,64},{64,32},{96,0},{1,97},{33,65},{65,33},{97,1},{2,98}... | collective-permute-start | bytes 12296 | tf_op jit(solution)/shard_map/ppermute | solution.py:370
  68.8 5.8 %collective-permute-start.7 = (f32[8,128]{1,0:T(8,128)S(1)}, f32[8,128]{1,0:T(8,128)S(1)}, u32[]{:S(2)}, u32[]{:S(2)}) collective-permute-start(f32[8,128]{1,0:T(8,128)S(1)} %buckets.1.b0_ref), channel_id=1, source_target_pairs={{0,32},{32,0},{64,96},{96,64},{1,33},{33,1},{65,97},{97,65},{2,34}... | collective-permute-start | bytes 12296 | tf_op jit(solution)/shard_map/ppermute | solution.py:370
  75.3 17.0 %all-to-all-start.1 = ((bf16[16,208,128]{2,1,0:T(8,128)(2,1)}), bf16[16,208,128]{2,1,0:T(8,128)(2,1)S(1)}, u32[]{:S(2)}, u32[]{:S(2)}) async-start(bf16[16,208,128]{2,1,0:T(8,128)(2,1)} %bias.1), calls=%async_computation.1 | async-start | bytes 1703936 | tf_op jit(solution)/shard_map/all_to_all | solution.py:475
  92.2 3.8 %collective-permute-start.10 = (f32[4,20]{1,0:T(4,128)S(1)}, f32[4,20]{1,0:T(4,128)S(1)}, u32[]{:S(2)}, u32[]{:S(2)}) collective-permute-start(f32[4,20]{1,0:T(4,128)S(1)} %bitcast.11), channel_id=1, source_target_pairs={{0,1},{1,0},{2,3},{3,2},{4,5},{5,4},{6,7},{7,6},{8,9},{9,8},{10,11... | collective-permute-start | bytes 968 | tf_op jit(solution)/shard_map/ppermute | solution.py:370

commit v8 on v7

--- a/solution.py
+++ b/solution.py
@@ -326,12 +326,13 @@
         give_ref[n, ROWS:] = line[block(n, k_both), :]
 
 
-def combine_kernel(mine_ref, got_qo_ref, dkv_ref, got_dkv_ref, out_ref):
+def combine_kernel(mine_ref, got_qo_ref, keep_ref, got_ref, got_dkv_ref, out_ref):
     @pl.loop(0, GROUPS, unroll=4)
     def _(n):
         qo = mine_ref[n] + got_qo_ref[n].astype(jnp.float32)
         out_ref[n, :ROWS] = qo.astype(jnp.bfloat16)
-        dkv = dkv_ref[n, :ROWS] + got_dkv_ref[n].astype(jnp.float32)
+        dkv = keep_ref[n, :ROWS].astype(jnp.float32) + got_ref[n, :ROWS].astype(jnp.float32)
+        dkv = dkv + got_dkv_ref[n].astype(jnp.float32)
         out_ref[n, ROWS : 2 * ROWS] = dkv.astype(jnp.bfloat16)
 
 
@@ -438,8 +439,7 @@
         name="attend",
     )(where, plan, table, starts, scales, own, kv_x, kv_core, kv_both, qg_x)
     got = swap(give, "core", (1, 0))
-    dkv = keep.astype(f32) + got.astype(f32)
-    dkv_x = dkv[:, ROWS:].astype(bf16)
+    dkv_x = (keep[:, ROWS:].astype(f32) + got[:, ROWS:].astype(f32)).astype(bf16)
     got_qo = swap(theirs, "x", (3, 2, 1, 0))
     got_dkv = swap(dkv_x, "x", (1, 0, 3, 2))
     bias = pl.pallas_call(
@@ -456,12 +456,12 @@
     results = pl.pallas_call(
         combine_kernel,
         out_shape=jax.ShapeDtypeStruct((H, 2 * ROWS + 16, 128), bf16),
-        in_specs=[whole] * 4,
+        in_specs=[whole] * 5,
         out_specs=whole,
         compiler_params=small,
         cost_estimate=pl.CostEstimate(flops=0, bytes_accessed=10**7, transcendentals=0),
         name="combine",
-    )(mine, got_qo, dkv, got_dkv)
+    )(mine, got_qo, keep, got, got_dkv)
     results = pl.pallas_call(
         bias_kernel,
         out_shape=jax.ShapeDtypeStruct((H, 2 * ROWS + 16, 128), bf16),

time: 96.9 us -> 96.3 us (level)
  starting transfers between devices: 22.5 us -> 21.3 us
    ppermute x11, starting transfers between devices: 18.9 us -> 17.6 us  [swap(): return lax.ppermute(v, axis, [(i, p) for i, p in enumerate(partner)])]
  transfers between devices with their start and end apart: 12 -> 12, of which waited for: 7 -> 7; matrix products, arithmetic and copies ran while one was open for 0% -> 0% of each run, Pallas kernels for 8% -> 9%
where the time goes in v8:
time: 96.3 us; the launch traced here: 95.4 us
  Pallas kernels  29 us (30%)
  blocking collectives  22 us (23%)
  waiting for transfers between devices  21.6 us (22%)
  starting transfers between devices  21.3 us (22%)
    all_to_all x1, blocking collectives, per_device(): own = lax.all_to_all(packed, ('y', 'z'), 0, 0, tiled=True)  22 us
    pallas_call x1, Pallas kernels, per_device(): pl.pallas_call(main_kernel, out_shape=[double, double, jax.ShapeDtypeStru...  17.7 us
    ppermute x11, starting transfers between devices, swap(): return lax.ppermute(v, axis, [(i, p) for i, p in enumerate(partner)])  17.6 us
    all_to_all x1, waiting for transfers between devices, per_device(): results = lax.all_to_all(results, ('y', 'z'), 0, 0, tiled=True)  13.3 us
    ppermute x11, waiting for transfers between devices, swap(): return lax.ppermute(v, axis, [(i, p) for i, p in enumerate(partner)])  8.25 us
    pallas_call x1, Pallas kernels, per_device(): pl.pallas_call(table_kernel, out_shape=(slabs, jax.ShapeDtypeStruct((GROU...  4.34 us
    all_to_all x1, starting transfers between devices, per_device(): results = lax.all_to_all(results, ('y', 'z'), 0, 0, tiled=True)  3.64 us
    pallas_call x1, Pallas kernels, per_device(): pl.pallas_call(pack_kernel, out_shape=(double, jax.ShapeDtypeStruct((DOCS...  2.37 us
  transfers between devices with their start and end apart: 12, of which 7 were waited for; matrix products, arithmetic and copies ran while one was open for 0% of the time, Pallas kernels for 9%

profile of v8, /device:TPU:1, one launch (start us, length us, event | category | flops | bytes accessed | tf_op | source)
XLA Modules:
  0.0 95.4 jit_solution(3222272355263848316)
XLA Ops:
  0.6 0.0 copy-start
  0.7 2.4 %pack.1 = (bf16[16,192,128]{2,1,0:T(8,128)(2,1)}, s32[8]{0:T(128)}) custom-call(s32[1]{0:T(128)} %bitcast.2.where_ref, s32[96,128]{1,0:T(8,128)} %bitcast.10, bf16[3,96,1024]{2,1,0:T(8,128)(2,1)} %bitcast.9, bf16[96,1024]{1,0:T(8,128)(2,1)} %g_in.1), custom_call_target="tpu_custom_call" | custom-call | tf_op jit(solution)/shard_map/pack/pallas_call | solution.py:386
  3.0 0.0 copy-start.1
  3.0 22.0 %all_to_all.10.own_ref = bf16[16,192,128]{2,1,0:T(8,128)(2,1)S(1)} all-to-all(bf16[16,192,128]{2,1,0:T(8,128)(2,1)} %get-tuple-element.22), channel_id=1, replica_groups=mesh['x'=4,'y'=4,'z'=4,'core'=2] {'y','z'}, dimensions={0} | all-to-all | bytes 1572864 | tf_op jit(solution)/shard_map/all_to_all | solution.py:400
  25.0 0.1 fusion
  25.1 2.6 %collective-permute-start.1 = (bf16[16,96,128]{2,1,0:T(8,128)(2,1)S(1)}, bf16[16,96,128]{2,1,0:T(8,128)(2,1)S(1)}, u32[]{:S(2)}, u32[]{:S(2)}) collective-permute-start(bf16[16,96,128]{2,1,0:T(8,128)(2,1)S(1)} %get-tuple-element.41), channel_id=1, source_target_pairs={{0,96},{32,64},{64,32},{96,0},{1,97},{33,65},{65,33},{97,1},{2,98}... | collective-permute-start | bytes 1179656 | tf_op jit(solution)/shard_map/ppermute | solution.py:371
  27.6 0.0 collective-permute-start
  27.6 0.1 pad_add_fusion.where_ref
  27.7 0.0 copy-done
  27.7 0.0 copy-done.1
  27.7 4.3 %table.1 = (f32[28,192,128]{2,1,0:T(8,128)S(1)}, s32[16,192,128]{2,1,0:T(8,128)S(1)}, f32[16,192,128]{2,1,0:T(8,128)S(1)}, s32[1281]{0:T(1024)S(1)}) custom-call(s32[2]{0:T(128)S(1)} %pad_add_fusion.where_ref, f32[20]{0:T(128)S(1)} %dynamic-slice_bitcast_fusion.rab_ref, s32[8]{0:T(128)S(1)} %copy-done.1), custom_call_target="tpu_custom_call" | custom-call | tf_op jit(solution)/shard_map/table/pallas_call | solution.py:406
  32.1 2.7 %collective-permute-start.2 = (bf16[16,96,128]{2,1,0:T(8,128)(2,1)S(1)}, bf16[16,96,128]{2,1,0:T(8,128)(2,1)S(1)}, u32[]{:S(2)}, u32[]{:S(2)}) collective-permute-start(bf16[16,96,128]{2,1,0:T(8,128)(2,1)S(1)} %get-tuple-element.42), channel_id=1, source_target_pairs={{0,1},{1,0},{2,3},{3,2},{4,5},{5,4},{6,7},{7,6},{8,9},{9,8},{10,11... | collective-permute-start | bytes 1179656 | tf_op jit(solution)/shard_map/ppermute | solution.py:371
  34.7 0.5 collective-permute-done.1.qgx_ref
  35.2 1.0 %collective-permute-done.kvx_ref = bf16[16,96,128]{2,1,0:T(8,128)(2,1)S(1)} collective-permute-done((bf16[16,96,128]{2,1,0:T(8,128)(2,1)S(1)}, bf16[16,96,128]{2,1,0:T(8,128)(2,1)S(1)}, u32[]{:S(2)}, u32[]{:S(2)}) %collective-permute-start) | collective-permute-done | bytes 393248 | tf_op jit(solution)/shard_map/ppermute | solution.py:371
  36.2 2.9 %collective-permute-start.3 = (bf16[16,96,128]{2,1,0:T(8,128)(2,1)S(1)}, bf16[16,96,128]{2,1,0:T(8,128)(2,1)S(1)}, u32[]{:S(2)}, u32[]{:S(2)}) collective-permute-start(bf16[16,96,128]{2,1,0:T(8,128)(2,1)S(1)} %collective-permute-done.kvx_ref), channel_id=1, source_target_pairs={{0,1},{1,0},{2,3},{3,2},{4,5},{5,4},{6,7},{7,6},{8,9},{9,8},{10,11... | collective-permute-start | bytes 1179656 | tf_op jit(solution)/shard_map/ppermute | solution.py:371
  39.2 0.0 collective-permute-done.2.kvc_ref
  39.2 1.3 %collective-permute-done.3.kvxc_ref = bf16[16,96,128]{2,1,0:T(8,128)(2,1)S(1)} collective-permute-done((bf16[16,96,128]{2,1,0:T(8,128)(2,1)S(1)}, bf16[16,96,128]{2,1,0:T(8,128)(2,1)S(1)}, u32[]{:S(2)}, u32[]{:S(2)}) %collective-permute-start.3) | collective-permute-done | bytes 393248 | tf_op jit(solution)/shard_map/ppermute | solution.py:371
  40.5 17.7 %attend.1 = (bf16[16,192,128]{2,1,0:T(8,128)(2,1)S(1)}, bf16[16,192,128]{2,1,0:T(8,128)(2,1)S(1)}, f32[16,96,128]{2,1,0:T(8,128)S(1)}, bf16[16,96,128]{2,1,0:T(8,128)(2,1)S(1)}, f32[28,192,128]{2,1,0:T(8,128)S(1)}) custom-call(s32[2]{0:T(128)S(1)} %pad_add_fusion.where_ref, s32[1281]{0:T(1024)S(1)} %get-tuple-element.28.plan_ref, ...), custom_call_target="tpu_custom_call" | custom-call | tf_op jit(solution)/shard_map/attend/pallas_call | solution.py:424
  58.2 1.6 %collective-permute-start.5 = (bf16[16,192,128]{2,1,0:T(8,128)(2,1)S(1)}, bf16[16,192,128]{2,1,0:T(8,128)(2,1)S(1)}, u32[]{:S(2)}, u32[]{:S(2)}) collective-permute-start(bf16[16,192,128]{2,1,0:T(8,128)(2,1)S(1)} %get-tuple-element.37), channel_id=1, source_target_pairs={{0,1},{1,0},{2,3},{3,2},{4,5},{5,4},{6,7},{7,6},{8,9},{9,8},{10,11... | collective-permute-start | bytes 2359304 | tf_op jit(solution)/shard_map/ppermute | solution.py:371
  59.8 1.2 %collective-permute-start.4 = (bf16[16,96,128]{2,1,0:T(8,128)(2,1)S(1)}, bf16[16,96,128]{2,1,0:T(8,128)(2,1)S(1)}, u32[]{:S(2)}, u32[]{:S(2)}) collective-permute-start(bf16[16,96,128]{2,1,0:T(8,128)(2,1)S(1)} %get-tuple-element.35), channel_id=1, source_target_pairs={{0,96},{32,64},{64,32},{96,0},{1,97},{33,65},{65,33},{97,1},{2,98}... | collective-permute-start | bytes 1179656 | tf_op jit(solution)/shard_map/ppermute | solution.py:371
  61.0 0.7 collective-permute-done.5.got_ref
  61.7 0.1 add_convert_fusion
  61.8 0.1 collective-permute-start.6
  61.9 1.7 %buckets.1.b0_ref = f32[8,128]{1,0:T(8,128)S(1)} custom-call(s32[2]{0:T(128)S(1)} %pad_add_fusion.where_ref, f32[28,192,128]{2,1,0:T(8,128)S(1)} %get-tuple-element.38.sums_ref), custom_call_target="tpu_custom_call" | custom-call | tf_op jit(solution)/shard_map/buckets/pallas_call | solution.py:445
  63.6 2.5 %collective-permute-start.9 = (f32[8,128]{1,0:T(8,128)S(1)}, f32[8,128]{1,0:T(8,128)S(1)}, u32[]{:S(2)}, u32[]{:S(2)}) collective-permute-start(f32[8,128]{1,0:T(8,128)S(1)} %buckets.1.b0_ref), channel_id=1, source_target_pairs={{0,64},{32,96},{64,0},{96,32},{1,65},{33,97},{65,1},{97,33},{2,66}... | collective-permute-start | bytes 12296 | tf_op jit(solution)/shard_map/ppermute | solution.py:371
  66.1 1.5 %collective-permute-start.8 = (f32[8,128]{1,0:T(8,128)S(1)}, f32[8,128]{1,0:T(8,128)S(1)}, u32[]{:S(2)}, u32[]{:S(2)}) collective-permute-start(f32[8,128]{1,0:T(8,128)S(1)} %buckets.1.b0_ref), channel_id=1, source_target_pairs={{0,96},{32,64},{64,32},{96,0},{1,97},{33,65},{65,33},{97,1},{2,98}... | collective-permute-start | bytes 12296 | tf_op jit(solution)/shard_map/ppermute | solution.py:371
  67.5 0.0 collective-permute-start.7
  67.5 4.2 %collective-permute-done.4.got_qo_ref = bf16[16,96,128]{2,1,0:T(8,128)(2,1)S(1)} collective-permute-done((bf16[16,96,128]{2,1,0:T(8,128)(2,1)S(1)}, bf16[16,96,128]{2,1,0:T(8,128)(2,1)S(1)}, u32[]{:S(2)}, u32[]{:S(2)}) %collective-permute-start.4) | collective-permute-done | bytes 393248 | tf_op jit(solution)/shard_map/ppermute | solution.py:371
  71.7 0.5 collective-permute-done.6.got_dkv_ref
  72.2 1.1 %combine.1.in_ref = bf16[16,208,128]{2,1,0:T(8,128)(2,1)} custom-call(f32[16,96,128]{2,1,0:T(8,128)S(1)} %get-tuple-element.34.mine_ref, bf16[16,96,128]{2,1,0:T(8,128)(2,1)S(1)} %collective-permute-done.4.got_qo_ref, bf16[16,192,128]{2,1,0:T(8,128)(2,1)S(1)} %get-tuple-element.36.keep_ref, bf16[16,192,128]{2,1,0:T(8,128)(2,1)S(1)} %collective-permute-done.5.got_ref, ...), custom_call_target="tpu_custom_call" | custom-call | bytes 10000000 | tf_op jit(solution)/shard_map/combine/pallas_call | solution.py:456
  73.4 0.0 collective-permute-done.9.b3_ref
  73.4 0.0 collective-permute-done.8.b2_ref
  73.4 0.0 collective-permute-done.7.b1_ref
  73.4 0.7 bias.1
  74.0 3.6 %all-to-all-start.1 = ((bf16[16,208,128]{2,1,0:T(8,128)(2,1)}), bf16[16,208,128]{2,1,0:T(8,128)(2,1)S(1)}, u32[]{:S(2)}, u32[]{:S(2)}) async-start(bf16[16,208,128]{2,1,0:T(8,128)(2,1)} %bias.1), calls=%async_computation.1 | async-start | bytes 1703936 | tf_op jit(solution)/shard_map/all_to_all | solution.py:475
  77.7 13.3 %all-to-all-done.1.in_ref = bf16[16,208,128]{2,1,0:T(8,128)(2,1)S(1)} async-done(((bf16[16,208,128]{2,1,0:T(8,128)(2,1)}), bf16[16,208,128]{2,1,0:T(8,128)(2,1)S(1)}, u32[]{:S(2)}, u32[]{:S(2)}) %all-to-all-start.1) | async-done | bytes 852000 | tf_op jit(solution)/shard_map/all_to_all | solution.py:475
  91.0 2.7 %collective-permute-start.10 = (f32[4,20]{1,0:T(4,128)S(1)}, f32[4,20]{1,0:T(4,128)S(1)}, u32[]{:S(2)}, u32[]{:S(2)}) collective-permute-start(f32[4,20]{1,0:T(4,128)S(1)} %bitcast.11), channel_id=1, source_target_pairs={{0,1},{1,0},{2,3},{3,2},{4,5},{5,4},{6,7},{7,6},{8,9},{9,8},{10,11... | collective-permute-start | bytes 968 | tf_op jit(solution)/shard_map/ppermute | solution.py:371
  93.7 1.2 %unpack.1 = (bf16[96,1024]{1,0:T(8,128)(2,1)}, bf16[3,96,1024]{2,1,0:T(8,128)(2,1)}) custom-call(bf16[16,208,128]{2,1,0:T(8,128)(2,1)S(1)} %all-to-all-done.1.in_ref), custom_call_target="tpu_custom_call" | custom-call | tf_op jit(solution)/shard_map/unpack/pallas_call | solution.py:479
  94.9 0.0 collective-permute-done.10
  94.9 0.6 add.41
  (3 shorter events, 0.0 us)
Async XLA Ops:
  0.6 27.1 %copy-start = (f32[16,20]{1,0:T(8,128)S(1)}, f32[16,20]{1,0:T(8,128)}, u32[]{:S(2)}) copy-start(f32[16,20]{1,0:T(8,128)} %param.6) | copy-start | bytes 3844
  3.0 24.7 %copy-start.1 = (s32[8]{0:T(128)S(1)}, s32[8]{0:T(128)}, u32[]{:S(2)}) copy-start(s32[8]{0:T(128)} %get-tuple-element.23.bounds_ref) | copy-start | bytes 100
  25.1 10.2 %collective-permute-start.1 = (bf16[16,96,128]{2,1,0:T(8,128)(2,1)S(1)}, bf16[16,96,128]{2,1,0:T(8,128)(2,1)S(1)}, u32[]{:S(2)}, u32[]{:S(2)}) collective-permute-start(bf16[16,96,128]{2,1,0:T(8,128)(2,1)S(1)} %get-tuple-element.41), channel_id=1, source_target_pairs={{0,96},{32,64},{64,32},{96,0},{1,97},{33,65},{65,33},{97,1},{2,98}... | collective-permute-start | bytes 1179656 | tf_op jit(solution)/shard_map/ppermute | solution.py:371
  27.6 8.6 %collective-permute-start = (bf16[16,96,128]{2,1,0:T(8,128)(2,1)S(1)}, bf16[16,96,128]{2,1,0:T(8,128)(2,1)S(1)}, u32[]{:S(2)}, u32[]{:S(2)}) collective-permute-start(bf16[16,96,128]{2,1,0:T(8,128)(2,1)S(1)} %get-tuple-element.42), channel_id=1, source_target_pairs={{0,32},{32,0},{64,96},{96,64},{1,33},{33,1},{65,97},{97,65},{2,34}... | collective-permute-start | bytes 1179656 | tf_op jit(solution)/shard_map/ppermute | solution.py:371
  32.1 7.1 %collective-permute-start.2 = (bf16[16,96,128]{2,1,0:T(8,128)(2,1)S(1)}, bf16[16,96,128]{2,1,0:T(8,128)(2,1)S(1)}, u32[]{:S(2)}, u32[]{:S(2)}) collective-permute-start(bf16[16,96,128]{2,1,0:T(8,128)(2,1)S(1)} %get-tuple-element.42), channel_id=1, source_target_pairs={{0,1},{1,0},{2,3},{3,2},{4,5},{5,4},{6,7},{7,6},{8,9},{9,8},{10,11... | collective-permute-start | bytes 1179656 | tf_op jit(solution)/shard_map/ppermute | solution.py:371
  36.2 4.3 %collective-permute-start.3 = (bf16[16,96,128]{2,1,0:T(8,128)(2,1)S(1)}, bf16[16,96,128]{2,1,0:T(8,128)(2,1)S(1)}, u32[]{:S(2)}, u32[]{:S(2)}) collective-permute-start(bf16[16,96,128]{2,1,0:T(8,128)(2,1)S(1)} %collective-permute-done.kvx_ref), channel_id=1, source_target_pairs={{0,1},{1,0},{2,3},{3,2},{4,5},{5,4},{6,7},{7,6},{8,9},{9,8},{10,11... | collective-permute-start | bytes 1179656 | tf_op jit(solution)/shard_map/ppermute | solution.py:371
  58.2 3.5 %collective-permute-start.5 = (bf16[16,192,128]{2,1,0:T(8,128)(2,1)S(1)}, bf16[16,192,128]{2,1,0:T(8,128)(2,1)S(1)}, u32[]{:S(2)}, u32[]{:S(2)}) collective-permute-start(bf16[16,192,128]{2,1,0:T(8,128)(2,1)S(1)} %get-tuple-element.37), channel_id=1, source_target_pairs={{0,1},{1,0},{2,3},{3,2},{4,5},{5,4},{6,7},{7,6},{8,9},{9,8},{10,11... | collective-permute-start | bytes 2359304 | tf_op jit(solution)/shard_map/ppermute | solution.py:371
  59.8 11.9 %collective-permute-start.4 = (bf16[16,96,128]{2,1,0:T(8,128)(2,1)S(1)}, bf16[16,96,128]{2,1,0:T(8,128)(2,1)S(1)}, u32[]{:S(2)}, u32[]{:S(2)}) collective-permute-start(bf16[16,96,128]{2,1,0:T(8,128)(2,1)S(1)} %get-tuple-element.35), channel_id=1, source_target_pairs={{0,96},{32,64},{64,32},{96,0},{1,97},{33,65},{65,33},{97,1},{2,98}... | collective-permute-start | bytes 1179656 | tf_op jit(solution)/shard_map/ppermute | solution.py:371
  61.8 10.4 %collective-permute-start.6 = (bf16[16,96,128]{2,1,0:T(8,128)(2,1)S(1)}, bf16[16,96,128]{2,1,0:T(8,128)(2,1)S(1)}, u32[]{:S(2)}, u32[]{:S(2)}) collective-permute-start(bf16[16,96,128]{2,1,0:T(8,128)(2,1)S(1)} %add_convert_fusion), channel_id=1, source_target_pairs={{0,32},{32,0},{64,96},{96,64},{1,33},{33,1},{65,97},{97,65},{2,34}... | collective-permute-start | bytes 1179656 | tf_op jit(solution)/shard_map/ppermute | solution.py:371
  63.6 9.8 %collective-permute-start.9 = (f32[8,128]{1,0:T(8,128)S(1)}, f32[8,128]{1,0:T(8,128)S(1)}, u32[]{:S(2)}, u32[]{:S(2)}) collective-permute-start(f32[8,128]{1,0:T(8,128)S(1)} %buckets.1.b0_ref), channel_id=1, source_target_pairs={{0,64},{32,96},{64,0},{96,32},{1,65},{33,97},{65,1},{97,33},{2,66}... | collective-permute-start | bytes 12296 | tf_op jit(solution)/shard_map/ppermute | solution.py:371
  66.1 7.3 %collective-permute-start.8 = (f32[8,128]{1,0:T(8,128)S(1)}, f32[8,128]{1,0:T(8,128)S(1)}, u32[]{:S(2)}, u32[]{:S(2)}) collective-permute-start(f32[8,128]{1,0:T(8,128)S(1)} %buckets.1.b0_ref), channel_id=1, source_target_pairs={{0,96},{32,64},{64,32},{96,0},{1,97},{33,65},{65,33},{97,1},{2,98}... | collective-permute-start | bytes 12296 | tf_op jit(solution)/shard_map/ppermute | solution.py:371
  67.5 5.8 %collective-permute-start.7 = (f32[8,128]{1,0:T(8,128)S(1)}, f32[8,128]{1,0:T(8,128)S(1)}, u32[]{:S(2)}, u32[]{:S(2)}) collective-permute-start(f32[8,128]{1,0:T(8,128)S(1)} %buckets.1.b0_ref), channel_id=1, source_target_pairs={{0,32},{32,0},{64,96},{96,64},{1,33},{33,1},{65,97},{97,65},{2,34}... | collective-permute-start | bytes 12296 | tf_op jit(solution)/shard_map/ppermute | solution.py:371
  74.0 17.0 %all-to-all-start.1 = ((bf16[16,208,128]{2,1,0:T(8,128)(2,1)}), bf16[16,208,128]{2,1,0:T(8,128)(2,1)S(1)}, u32[]{:S(2)}, u32[]{:S(2)}) async-start(bf16[16,208,128]{2,1,0:T(8,128)(2,1)} %bias.1), calls=%async_computation.1 | async-start | bytes 1703936 | tf_op jit(solution)/shard_map/all_to_all | solution.py:475
  91.0 3.8 %collective-permute-start.10 = (f32[4,20]{1,0:T(4,128)S(1)}, f32[4,20]{1,0:T(4,128)S(1)}, u32[]{:S(2)}, u32[]{:S(2)}) collective-permute-start(f32[4,20]{1,0:T(4,128)S(1)} %bitcast.11), channel_id=1, source_target_pairs={{0,1},{1,0},{2,3},{3,2},{4,5},{5,4},{6,7},{7,6},{8,9},{9,8},{10,11... | collective-permute-start | bytes 968 | tf_op jit(solution)/shard_map/ppermute | solution.py:371
